TPU v7x, 32 devices: a whole 2x2x4 slice. The times are simulated.
32 devices in a mesh: feat: 8 (over z, x), pair: 4 (over y, core).
Axes of the slice: x: 2, y: 2, z: 4, core: 2. Of those that a mesh axis runs over, the one named last changes fastest.
Arguments:
- resid: bfloat16 [4, 1024, 2048], P('pair'), may hold values from -6 to 6
- enc_weight: bfloat16 [4, 2048, 16384], P('pair', None, 'feat'), may hold values from -0.125 to 0.125
- enc_bias: float32 [4, 16384], P('pair', 'feat'), may hold values from -3 to 3
- active: int32 [4, 1024, 64], P('pair'), may hold values from 0 to 16383, all different within a row
- dec_weight: bfloat16 [4, 4, 16384, 2048], P('pair', None, 'feat'), may hold values from -0.75 to 0.75
- dec_bias: float32 [4, 2048], P('pair'), may hold values from -3 to 3
- target: bfloat16 [4, 1024, 2048], P('pair', 'feat'), may hold values from -6 to 6
Outputs:
- error: float32 [4, 1024, 2048], P('pair', 'feat')
- dec_grad: bfloat16 [4, 4, 16384, 2048], P('pair', None, 'feat')
Inputs may be any that keep to these rules, and one draw needn't show every extreme that they name: `active`: within one layer, the 64 indices of a token are distinct; every feature number occurs somewhere in the array.
All inputs are finite; a program needn't handle non-finite values.
Results may differ from a plain program's by a relative error of at most 0.0058.
Values may be sent and summed in bfloat16 or wider, within the bound.
No kernel may reach another device: no remote copies, remote signals or barrier semaphores. Data moves between devices by JAX's collectives and lax.ppermute only.
A program may use at most 192 MiB of HBM per device.

v0:
```python
import jax
import jax.numpy as jnp
from jax import lax
from jax.sharding import PartitionSpec as P


def local(resid, enc_weight, enc_bias, active, dec_weight, dec_bias, target):
    slice_width = enc_weight.shape[2]
    model_width = resid.shape[2]
    layers = dec_weight.shape[1]
    shard_rows = target.shape[1]
    feat_index = lax.axis_index("feat")
    pair_index = lax.axis_index("pair")
    columns = feat_index * slice_width + jnp.arange(slice_width, dtype=jnp.int32)
    chosen = jnp.any(active[0][:, :, None] == columns[None, None, :], axis=1)
    pre_act = (
        jnp.dot(resid[0], enc_weight[0], preferred_element_type=jnp.float32) + enc_bias[0][None, :]
    )
    values = jnp.where(chosen, jnp.maximum(pre_act, 0.0), 0.0).astype(jnp.bfloat16)
    gathered = lax.all_gather(values[None], "pair", axis=0, tiled=True)
    decoders = dec_weight[0]

    def add_source(source, partial_value):
        left_rows = lax.dynamic_index_in_dim(gathered, source, 0, keepdims=False)
        weight_rows = lax.dynamic_index_in_dim(decoders, source, 0, keepdims=False)
        return partial_value + jnp.dot(left_rows, weight_rows, preferred_element_type=jnp.float32)

    rebuilt = lax.psum_scatter(
        lax.fori_loop(
            0,
            pair_index + 1,
            add_source,
            jnp.zeros((shard_rows * lax.axis_size("feat"), model_width), jnp.float32),
        ),
        "feat",
        scatter_dimension=0,
        tiled=True,
    )
    error_shard = rebuilt + dec_bias[0][None, :] - target[0].astype(jnp.float32)
    error_half = lax.all_gather(error_shard.astype(jnp.bfloat16), "feat", axis=0, tiled=True)

    def source_grad(source, error_rows):
        left_rows = lax.dynamic_index_in_dim(gathered, source, 0, keepdims=False)
        product = lax.dot_general(
            left_rows, error_rows, (((0,), (0,)), ((), ())), preferred_element_type=jnp.float32
        )
        return product.astype(jnp.bfloat16)

    def add_grad(source, gradients):
        return lax.dynamic_update_index_in_dim(
            gradients, source_grad(source, error_half), source, 0
        )

    empty = jnp.zeros((layers, slice_width, model_width), jnp.bfloat16)
    gradients = lax.fori_loop(0, pair_index + 1, add_grad, empty)
    return (error_shard[None], gradients[None])


def solution(mesh):
    in_specs = (
        P("pair", None, None),
        P("pair", None, "feat"),
        P("pair", "feat"),
        P("pair", None, None),
        P("pair", None, "feat", None),
        P("pair", None),
        P("pair", "feat", None),
    )
    out_specs = (P("pair", "feat", None), P("pair", None, "feat", None))
    return jax.shard_map(local, mesh=mesh, in_specs=in_specs, out_specs=out_specs, check_vma=False)
```

profile of v0, /device:TPU:7, one launch (start us, length us, event | category | flops | bytes accessed | tf_op | source)
XLA Modules:
  0.0 579.9 jit_solution(7541132158021069268)
XLA Ops:
  7.2 0.0 all-gather.6.cloned.1.call-start
  7.2 1.1 copy.10
  8.4 86.8 %compare_reduce_fusion = pred[1024,2048]{1,0:T(8,128)(4,1)S(1)} fusion(s32[2048]{0:T(1024)S(1)} %iota_add_fusion, s32[1024,64]{1,0:T(8,128)S(1)} %copy.10), kind=kLoop, calls=%fused_computation.11 | loop fusion | flops 266338304 | bytes 2367488 | tf_op jit(solution)/shard_map/reduce_or | solution.py:15
  95.2 14.2 %select_convert_fusion = bf16[1024,2048]{1,0:T(8,128)(2,1)} fusion(pred[1024,2048]{1,0:T(8,128)(4,1)S(1)} %compare_reduce_fusion, bf16[1,2048,2048]{2,1,0:T(8,128)(2,1)} %param.12, bf16[1,1024,2048]{2,1,0:T(8,128)(2,1)} %param.11, f32[2048]{0:T(1024)} %bitcast.51), kind=kOutput, calls=%fused_computation.14 | convolution fusion | flops 8598323200 | bytes 18882560 | tf_op jit(solution)/shard_map/dot_general | solution.py:17
  109.4 0.0 all-gather.6.cloned.1.call-update
  109.4 0.0 reduce-scatter.2.cloned.1.call-start
  109.5 106.7 %all-gather.6.cloned.1.call-done = bf16[4096,2048]{1,0:T(8,128)(2,1)} async-done(((bf16[1024,2048]{1,0:T(8,128)(2,1)}), bf16[4096,2048]{1,0:T(8,128)(2,1)}) %all-gather.6.cloned.1.call-update) | async-done | bytes 16777232 | tf_op jit(solution)/shard_map/all_gather | solution.py:20
  216.2 4.5 broadcast.7
  220.7 62.7 %while.20 = (s32[]{:T(128)}, f32[1024,2048]{1,0:T(8,128)}, s32[]{:T(128)}, bf16[4,1024,2048]{2,1,0:T(8,128)(2,1)}, bf16[4,2048,2048]{2,1,0:T(8,128)(2,1)}, /*index=5*/s32[]{:T(128)}, s32[]{:T(128)}, s32[]{:T(128)}) while((s32[]{:T(128)}, f32[1024,2048]{1,0:T(8,128)}, s32[]{:T(128)}, bf16[4,1024,2048]{2,1,0:T(8,128)(2,1)}, ...), condition=%wide.region_2.3_spmd, body=%wide.region_1.2_spmd.sunk | while | flops 8592031744 | bytes 29361280 | solution.py:29
  220.7 15.7 %fusion.29 = f32[1024,2048]{1,0:T(8,128)} fusion(f32[1024,2048]{1,0:T(8,128)} %get-tuple-element.155, bf16[4,2048,2048]{2,1,0:T(8,128)(2,1)} %get-tuple-element.166, s32[]{:T(128)S(6)} %select_n.19, bf16[4,1024,2048]{2,1,0:T(8,128)(2,1)} %get-tuple-element.165), kind=kOutput, calls=%fused_computation.5.clone.1 | convolution fusion | flops 8592031744 | bytes 29361152 | tf_op jit(solution)/shard_map/while/body/dot_general | solution.py:26
  236.3 15.7 %fusion.29 = f32[1024,2048]{1,0:T(8,128)} fusion(f32[1024,2048]{1,0:T(8,128)} %get-tuple-element.155, bf16[4,2048,2048]{2,1,0:T(8,128)(2,1)} %get-tuple-element.166, s32[]{:T(128)S(6)} %select_n.19, bf16[4,1024,2048]{2,1,0:T(8,128)(2,1)} %get-tuple-element.165), kind=kOutput, calls=%fused_computation.5.clone.1 | convolution fusion | flops 8592031744 | bytes 29361152 | tf_op jit(solution)/shard_map/while/body/dot_general | solution.py:26
  252.0 15.7 %fusion.29 = f32[1024,2048]{1,0:T(8,128)} fusion(f32[1024,2048]{1,0:T(8,128)} %get-tuple-element.155, bf16[4,2048,2048]{2,1,0:T(8,128)(2,1)} %get-tuple-element.166, s32[]{:T(128)S(6)} %select_n.19, bf16[4,1024,2048]{2,1,0:T(8,128)(2,1)} %get-tuple-element.165), kind=kOutput, calls=%fused_computation.5.clone.1 | convolution fusion | flops 8592031744 | bytes 29361152 | tf_op jit(solution)/shard_map/while/body/dot_general | solution.py:26
  267.7 15.7 %fusion.29 = f32[1024,2048]{1,0:T(8,128)} fusion(f32[1024,2048]{1,0:T(8,128)} %get-tuple-element.155, bf16[4,2048,2048]{2,1,0:T(8,128)(2,1)} %get-tuple-element.166, s32[]{:T(128)S(6)} %select_n.19, bf16[4,1024,2048]{2,1,0:T(8,128)(2,1)} %get-tuple-element.165), kind=kOutput, calls=%fused_computation.5.clone.1 | convolution fusion | flops 8592031744 | bytes 29361152 | tf_op jit(solution)/shard_map/while/body/dot_general | solution.py:26
  283.4 0.0 copy-start
  283.4 0.0 copy-start.1
  283.4 0.0 reduce-scatter.2.cloned.1.call-update
  283.4 0.2 all-gather.4.cloned.1.call-start
  283.6 149.3 %reduce-scatter.2.cloned.1.call-done = f32[128,2048]{1,0:T(8,128)} async-done(((f32[1024,2048]{1,0:T(8,128)}), f32[128,2048]{1,0:T(8,128)}) %reduce-scatter.2.cloned.1.call-update) | async-done | bytes 1048592 | tf_op jit(solution)/shard_map/reduce_scatter | solution.py:28
  433.0 0.0 copy-done
  433.0 0.0 copy-done.1
  433.0 2.5 fusion.19
  435.5 0.0 all-gather.4.cloned.1.call-update
  435.5 70.6 %all-gather.4.cloned.1.call-done = bf16[1024,2048]{1,0:T(8,128)(2,1)} async-done(((bf16[128,2048]{1,0:T(8,128)(2,1)}), bf16[1024,2048]{1,0:T(8,128)(2,1)}) %all-gather.4.cloned.1.call-update) | async-done | bytes 4194320 | tf_op jit(solution)/shard_map/all_gather | solution.py:40
  506.2 11.2 %broadcast_in_dim.21 = bf16[4,2048,2048]{2,1,0:T(8,128)(2,1)} broadcast(bf16[]{:T(256)} %constant.43.clone.1), dimensions={} | broadcast | bytes 33554432 | tf_op jit(solution)/shard_map/broadcast_in_dim | solution.py:54
  517.3 56.0 %while.21 = (s32[]{:T(128)}, bf16[4,2048,2048]{2,1,0:T(8,128)(2,1)}, s32[]{:T(128)}, bf16[4,1024,2048]{2,1,0:T(8,128)(2,1)}, bf16[1024,2048]{1,0:T(8,128)(2,1)}, /*index=5*/s32[]{:T(128)}, s32[]{:T(128)}, s32[]{:T(128)}) while((s32[]{:T(128)}, bf16[4,2048,2048]{2,1,0:T(8,128)(2,1)}, s32[]{:T(128)}, bf16[4,1024,2048]{2,1,0:T(8,128)(2,1)}, ...), condition=%wide.region_5.6_spmd, body=%wide.region_4.5_spmd.sunk | while | flops 8594128896 | bytes 16778368 | solution.py:55
  517.3 14.0 %bitcast_dynamic-update-slice_fusion.2 = bf16[4,2048,2048]{2,1,0:T(8,128)(2,1)} fusion(bf16[4,2048,2048]{2,1,0:T(8,128)(2,1)} %get-tuple-element.179, s32[]{:T(128)S(6)} %select_n.20, bf16[1024,2048]{1,0:T(8,128)(2,1)} %get-tuple-element.190, bf16[4,1024,2048]{2,1,0:T(8,128)(2,1)} %get-tuple-element.189), kind=kOutput, calls=%fused_computation.7.clone.1 | convolution fusion | flops 8594128896 | bytes 16778240 | tf_op jit(solution)/shard_map/while/body/dot_general | solution.py:44
  531.3 14.0 %bitcast_dynamic-update-slice_fusion.2 = bf16[4,2048,2048]{2,1,0:T(8,128)(2,1)} fusion(bf16[4,2048,2048]{2,1,0:T(8,128)(2,1)} %get-tuple-element.179, s32[]{:T(128)S(6)} %select_n.20, bf16[1024,2048]{1,0:T(8,128)(2,1)} %get-tuple-element.190, bf16[4,1024,2048]{2,1,0:T(8,128)(2,1)} %get-tuple-element.189), kind=kOutput, calls=%fused_computation.7.clone.1 | convolution fusion | flops 8594128896 | bytes 16778240 | tf_op jit(solution)/shard_map/while/body/dot_general | solution.py:44
  545.3 14.0 %bitcast_dynamic-update-slice_fusion.2 = bf16[4,2048,2048]{2,1,0:T(8,128)(2,1)} fusion(bf16[4,2048,2048]{2,1,0:T(8,128)(2,1)} %get-tuple-element.179, s32[]{:T(128)S(6)} %select_n.20, bf16[1024,2048]{1,0:T(8,128)(2,1)} %get-tuple-element.190, bf16[4,1024,2048]{2,1,0:T(8,128)(2,1)} %get-tuple-element.189), kind=kOutput, calls=%fused_computation.7.clone.1 | convolution fusion | flops 8594128896 | bytes 16778240 | tf_op jit(solution)/shard_map/while/body/dot_general | solution.py:44
  559.3 14.0 %bitcast_dynamic-update-slice_fusion.2 = bf16[4,2048,2048]{2,1,0:T(8,128)(2,1)} fusion(bf16[4,2048,2048]{2,1,0:T(8,128)(2,1)} %get-tuple-element.179, s32[]{:T(128)S(6)} %select_n.20, bf16[1024,2048]{1,0:T(8,128)(2,1)} %get-tuple-element.190, bf16[4,1024,2048]{2,1,0:T(8,128)(2,1)} %get-tuple-element.189), kind=kOutput, calls=%fused_computation.7.clone.1 | convolution fusion | flops 8594128896 | bytes 16778240 | tf_op jit(solution)/shard_map/while/body/dot_general | solution.py:44
  (1 shorter events, 0.0 us)
Async XLA Ops:
  7.2 209.0 %all-gather.6.cloned.1.call-start = ((), (), s32[]{:S(2)}) async-start(), calls=%async_computation.3 | async-start | bytes 20971520 | tf_op jit(solution)/shard_map/all_gather | solution.py:20
  109.4 323.5 %reduce-scatter.2.cloned.1.call-start = ((), (), s32[]{:S(2)}) async-start(), calls=%async_computation.1 | async-start | bytes 9437184 | tf_op jit(solution)/shard_map/reduce_scatter | solution.py:28
  283.4 149.6 %copy-start = (bf16[1,128,2048]{2,1,0:T(8,128)(2,1)S(1)}, bf16[1,128,2048]{2,1,0:T(8,128)(2,1)}, u32[]{:S(2)}) copy-start(bf16[1,128,2048]{2,1,0:T(8,128)(2,1)} %param.17) | copy-start | bytes 1572868
  283.4 149.6 %copy-start.1 = (f32[1,2048]{1,0:T(1,128)S(1)}, f32[1,2048]{1,0:T(1,128)}, u32[]{:S(2)}) copy-start(f32[1,2048]{1,0:T(1,128)} %param.16) | copy-start | bytes 24580
  283.4 222.8 %all-gather.4.cloned.1.call-start = ((), (), s32[]{:S(2)}) async-start(), calls=%async_computation.2 | async-start | bytes 4718592 | tf_op jit(solution)/shard_map/all_gather | solution.py:40
Sparse Core Ops, SparseCore 0:
  109.6 106.6 all-gather.5
  283.5 149.4 reduce-scatter.1
  435.9 70.2 all-gather.3
where the time goes:
time: 581 us; the launch traced here: 580 us
  waiting for transfers between devices  327 us (56%)
  matrix products  133 us (23%)
  other arithmetic  89.3 us (15%)
  local copies, waits for them, and re-layouts  16.8 us (3%)
  between operations  13.8 us (2%)
    reduce_scatter x1, waiting for transfers between devices, local(): lax.psum_scatter(lax.fori_loop(0, pair_index + 1, add_source, jnp.zeros((...  149 us
    all_gather x1, waiting for transfers between devices, local(): gathered = lax.all_gather(values[None], 'pair', axis=0, tiled=True)  107 us
    reduce_or x1, other arithmetic, local(): chosen = jnp.any(active[0][:, :, None] == columns[None, None, :], axis=1)  86.8 us
    all_gather x1, waiting for transfers between devices, local(): lax.all_gather(error_shard.astype(jnp.bfloat16), 'feat', axis=0, tiled=True)  70.6 us
    dot_general x4, matrix products, add_source(): jnp.dot(left_rows, weight_rows, preferred_element_type=jnp.float32)  62.7 us
    dot_general x4, matrix products, source_grad(): lax.dot_general(left_rows, error_rows, (((0,), (0,)), ((), ())), preferre...  56 us
    dot_general x1, matrix products, local(): jnp.dot(resid[0], enc_weight[0], preferred_element_type=jnp.float32)  14.2 us
  transfers between devices with their start and end apart: 3, of which 3 were waited for; matrix products, arithmetic and copies ran while one was open for 0% of the time, Pallas kernels for 0%

commit v1 on v0

v1 whole, which is shorter than its diff:
```python
import functools

import jax
import jax.numpy as jnp
from jax import lax
from jax.experimental import pallas as pl
from jax.experimental.pallas import tpu as pltpu
from jax.sharding import PartitionSpec as P

LANES = 128
ROWS = 8
SLOTS = 32
FAR = 32767
VMEM_BYTES = 40 * 1024 * 1024
SMALL_BYTES = 8 * 1024 * 1024
PIECE = 512
CHUNK = 1024


def params(limit=VMEM_BYTES):
    return pltpu.CompilerParams(vmem_limit_bytes=limit)


def encode_kernel(resid_ref, weight_ref, bias_ref, slot_ref, out_ref, pre_ref, picked_ref, index_ref):
    step = pl.program_id(0)
    tokens = resid_ref.shape[0]
    width = weight_ref.shape[1]
    slots = slot_ref.shape[1]
    groups = width // LANES

    @pl.when(step == 0)
    def _():
        picked_ref[...] = jnp.zeros_like(picked_ref)
        pre_ref[1] = jnp.zeros_like(pre_ref[1])
        index_ref[...] = jnp.full_like(index_ref, FAR)
        index_ref[:, :slots] = slot_ref[...]

    now = lax.rem(step, 2)
    before = 1 - now
    pre_ref[now] = (
        jnp.dot(resid_ref[...], weight_ref[...], preferred_element_type=jnp.float32)
        + bias_ref[...]
    )
    first = (step - 1) * groups
    for row in range(0, tokens, ROWS):
        rows = pl.ds(row, ROWS)
        index = index_ref[rows, :]
        group = (index >> 7) - first
        lane = index & (LANES - 1)
        picked = picked_ref[rows, :]
        for part in range(groups):
            source = pre_ref[before, rows, part * LANES : (part + 1) * LANES]
            found = jnp.take_along_axis(source, lane, axis=1)
            picked = jnp.where(group == part, found, picked)
        picked_ref[rows, :] = picked

    @pl.when(step == pl.num_programs(0) - 1)
    def _():
        out_ref[...] = jnp.maximum(picked_ref[:, :slots], 0.0).astype(out_ref.dtype)


def encode(resid, weight, bias, slot_index):
    tokens, depth = resid.shape
    features = weight.shape[1]
    slots = slot_index.shape[1]
    width = min(256, features)
    steps = features // width
    return pl.pallas_call(
        encode_kernel,
        grid=(steps + 1,),
        in_specs=[
            pl.BlockSpec((tokens, depth), lambda i: (0, 0)),
            pl.BlockSpec((depth, width), lambda i: (0, jnp.minimum(i, steps - 1))),
            pl.BlockSpec((1, width), lambda i: (0, jnp.minimum(i, steps - 1))),
            pl.BlockSpec((tokens, slots), lambda i: (0, 0)),
        ],
        out_specs=pl.BlockSpec((tokens, slots), lambda i: (0, 0)),
        out_shape=jax.ShapeDtypeStruct((tokens, slots), jnp.bfloat16),
        scratch_shapes=[
            pltpu.VMEM((2, tokens, width), jnp.float32),
            pltpu.VMEM((tokens, LANES), jnp.float32),
            pltpu.VMEM((tokens, LANES), jnp.int32),
        ],
        compiler_params=params(),
        cost_estimate=pl.CostEstimate(
            flops=2 * tokens * depth * features,
            bytes_accessed=2 * depth * (features + tokens),
            transcendentals=0,
        ),
    )(resid, weight, bias, slot_index)


def spread_kernel(top_ref, deep_ref, place_ref, index_ref, value_ref, *refs):
    out_ref = refs[-1]
    place = place_ref[pl.program_id(0)]
    blocks = index_ref.shape[1]
    features = out_ref.shape[2]
    groups = features // LANES
    top = top_ref[0]
    source = jnp.bitwise_xor(top, place)
    span = ROWS * SLOTS

    def rows_of(block, rounds):
        high = lax.broadcasted_iota(jnp.int32, (groups * ROWS, span), 0)
        low = lax.broadcasted_iota(jnp.int32, (LANES, span), 0)
        token = lax.broadcasted_iota(jnp.int32, (1, span), 1) // SLOTS
        total = None
        for turn in range(rounds):
            at = pl.ds(turn * span, span)
            index = index_ref[0, pl.ds(block, 1), at]
            value = value_ref[0, pl.ds(block, 1), at]
            key = (index >> 7) * ROWS + token
            lane = index & (LANES - 1)
            left = jnp.where(
                jnp.broadcast_to(key, high.shape) == high, jnp.broadcast_to(value, high.shape), 0.0
            ).astype(jnp.bfloat16)
            right = jnp.where(jnp.broadcast_to(lane, low.shape) == low, 1.0, 0.0).astype(
                jnp.bfloat16
            )
            part = lax.dot_general(
                left, right, (((1,), (1,)), ((), ())), preferred_element_type=jnp.float32
            )
            total = part if total is None else total + part
        return total

    def run(rounds, unroll):
        def pair(i, carry):
            one, two = rows_of(2 * i, rounds), rows_of(2 * i + 1, rounds)
            rows = pl.ds(pl.multiple_of(i * 2 * ROWS, 2 * ROWS), 2 * ROWS)
            for group in range(groups):
                part = slice(group * ROWS, (group + 1) * ROWS)
                out_ref[0, rows, group * LANES : (group + 1) * LANES] = jnp.concatenate(
                    [one[part], two[part]], axis=0
                ).astype(out_ref.dtype)
            return carry

        lax.fori_loop(0, blocks // 2, pair, 0, unroll=unroll)

    deep = deep_ref[pl.program_id(0)]

    @pl.when((source <= top) & (deep == 0))
    def _():
        run(1, 8)

    @pl.when((source <= top) & (deep != 0))
    def _():
        run(index_ref.shape[2] // span, 1)


def spread(top, places, index, value, features, layers, held=None):
    count, blocks, wide = index.shape
    block = min(32, blocks)
    deep = jnp.any(index[:, :, ROWS * SLOTS :] != FAR, axis=(1, 2)).astype(jnp.int32)
    operands = [top, deep, jnp.array(places, jnp.int32), index, value]
    in_specs = [pl.BlockSpec((1, block, wide), lambda p, b, top, deep, place: (p, b, 0))] * 2
    aliases = {}
    if held is not None:
        operands.append(held)
        in_specs = in_specs + [pl.BlockSpec(memory_space=pl.ANY)]
        aliases = {5: 0}
    tokens = blocks * ROWS
    return pl.pallas_call(
        spread_kernel,
        grid_spec=pltpu.PrefetchScalarGridSpec(
            num_scalar_prefetch=3,
            grid=(count, blocks // block),
            in_specs=in_specs,
            out_specs=pl.BlockSpec(
                (1, block * ROWS, features),
                lambda p, b, top, deep, place: (jnp.bitwise_xor(top[0], place[p]), b, 0),
            ),
        ),
        out_shape=jax.ShapeDtypeStruct((layers, tokens, features), jnp.bfloat16),
        input_output_aliases=aliases,
        compiler_params=params(),
        cost_estimate=pl.CostEstimate(
            flops=count * 2 * tokens * features * 1000,
            bytes_accessed=count * tokens * features * 2,
            transcendentals=0,
        ),
    )(*operands)


def relative_block(me, place, bits):
    pattern = sum(((place >> j) & 1) << (bits - 1 - j) for j in range(bits))
    return jnp.bitwise_xor(me, pattern)


def rebuild_kernel(bits, top_ref, me_ref, value_ref, weight_ref, after_ref, *refs):
    keep_refs, send_refs, total_ref = refs[: len(refs) // 2], refs[len(refs) // 2 : -1], refs[-1]
    source = pl.program_id(0)

    @pl.when(source == 0)
    def _():
        total_ref[...] = jnp.dot(value_ref[0], weight_ref[0], preferred_element_type=jnp.float32)

    @pl.when((source > 0) & (source <= top_ref[0]))
    def _():
        total_ref[...] += jnp.dot(value_ref[0], weight_ref[0], preferred_element_type=jnp.float32)

    @pl.when(source == pl.num_programs(0) - 1)
    def _():
        count = 1 << bits
        rows = total_ref.shape[0] // count
        half = count // 2
        width = keep_refs[0].shape[1]
        for place in range(count):
            start = pl.multiple_of(relative_block(me_ref[0], place, bits) * rows, rows)
            for piece in range(len(keep_refs)):
                block = total_ref[pl.ds(start, rows), piece * width : (piece + 1) * width]
                if place < half:
                    keep_refs[piece][place * rows : (place + 1) * rows, :] = block
                else:
                    at = (place - half) * rows
                    send_refs[piece][at : at + rows, :] = block.astype(jnp.bfloat16)


def rebuild(top, me, values, weight, start, width, piece, bits, after):
    layers, tokens, features = values.shape
    first = start // width
    pieces = width // piece
    shape = (tokens // 2, piece)
    outs = pl.pallas_call(
        functools.partial(rebuild_kernel, bits),
        grid_spec=pltpu.PrefetchScalarGridSpec(
            num_scalar_prefetch=2,
            grid=(layers,),
            in_specs=[
                pl.BlockSpec(
                    (1, tokens, features), lambda s, top, me: (jnp.minimum(s, top[0]), 0, 0)
                ),
                pl.BlockSpec(
                    (1, features, width), lambda s, top, me: (jnp.minimum(s, top[0]), 0, first)
                ),
                pl.BlockSpec(memory_space=pl.ANY),
            ],
            out_specs=[pl.BlockSpec(shape, lambda s, top, me: (0, 0))] * (2 * pieces),
            scratch_shapes=[pltpu.VMEM((tokens, width), jnp.float32)],
        ),
        out_shape=[jax.ShapeDtypeStruct(shape, jnp.float32)] * pieces
        + [jax.ShapeDtypeStruct(shape, jnp.bfloat16)] * pieces,
        compiler_params=params(),
        cost_estimate=pl.CostEstimate(
            flops=2 * layers * tokens * features * width,
            bytes_accessed=2 * layers * features * (tokens + width),
            transcendentals=0,
        ),
    )(top, me, values, weight, after)
    return list(zip(outs[:pieces], outs[pieces:]))


def grad_kernel(bits, pieces, top_ref, me_ref, value_ref, *refs):
    near_refs, far_refs = refs[:pieces], refs[pieces : 2 * pieces]
    out_ref, error_ref = refs[-2:]
    source = pl.program_id(0)

    @pl.when(source == 0)
    def _():
        count = 1 << bits
        rows = error_ref.shape[0] // count
        half = count // 2
        width = near_refs[0].shape[1]
        for place in range(count):
            start = pl.multiple_of(relative_block(me_ref[0], place, bits) * rows, rows)
            for piece in range(pieces):
                from_ref = near_refs[piece] if place < half else far_refs[piece]
                at = (place % half) * rows
                error_ref[pl.ds(start, rows), piece * width : (piece + 1) * width] = from_ref[
                    at : at + rows, :
                ]

    @pl.when(source <= top_ref[0])
    def _():
        out_ref[0] = lax.dot_general(
            value_ref[0],
            error_ref[...],
            (((0,), (0,)), ((), ())),
            preferred_element_type=jnp.float32,
        ).astype(out_ref.dtype)

    @pl.when(source > top_ref[0])
    def _():
        out_ref[...] = jnp.zeros_like(out_ref)


def gradients(top, me, values, halves, start, width, depth, bits, held, after):
    layers, tokens, features = values.shape
    pieces = len(halves)
    piece = width // pieces
    first = start // width
    operands = [top, me, values] + [near for near, _ in halves] + [far for _, far in halves]
    in_specs = [
        pl.BlockSpec((1, tokens, features), lambda s, top, me: (jnp.minimum(s, top[0]), 0, 0))
    ] + [pl.BlockSpec((tokens // 2, piece), lambda s, top, me: (0, 0))] * (2 * pieces)
    operands.append(after)
    in_specs.append(pl.BlockSpec(memory_space=pl.ANY))
    aliases = {}
    if held is not None:
        aliases = {len(operands): 0}
        operands.append(held)
        in_specs.append(pl.BlockSpec(memory_space=pl.ANY))
    return pl.pallas_call(
        functools.partial(grad_kernel, bits, pieces),
        grid_spec=pltpu.PrefetchScalarGridSpec(
            num_scalar_prefetch=2,
            grid=(layers,),
            in_specs=in_specs,
            out_specs=pl.BlockSpec((1, features, width), lambda s, top, me: (s, 0, first)),
            scratch_shapes=[pltpu.VMEM((tokens, width), jnp.bfloat16)],
        ),
        out_shape=jax.ShapeDtypeStruct((layers, features, depth), jnp.bfloat16),
        input_output_aliases=aliases,
        compiler_params=params(),
        cost_estimate=pl.CostEstimate(
            flops=2 * layers * tokens * features * width,
            bytes_accessed=2 * layers * features * (tokens + width),
            transcendentals=0,
        ),
    )(*operands)


def ordered(kernel, operands, specs, out_shape, after):
    def run(*refs):
        kernel(*refs[: len(operands)], *refs[len(operands) + 1 :])

    return pl.pallas_call(
        run,
        grid=(1,),
        in_specs=specs + [pl.BlockSpec(memory_space=pl.ANY)],
        out_specs=[pl.BlockSpec(x.shape, lambda i: (0, 0)) for x in out_shape],
        out_shape=out_shape,
        compiler_params=params(SMALL_BYTES),
        cost_estimate=pl.CostEstimate(flops=1000, bytes_accessed=1 << 20, transcendentals=0),
    )(*operands, after)


def columns_of(x, width, at):
    return pl.BlockSpec((x.shape[0], width), lambda i: (0, at))


def split(keep, arrived, width, at, after):
    rows = keep.shape[0] // 2

    def kernel(keep_ref, arrived_ref, out_ref, send_ref):
        out_ref[...] = keep_ref[:rows, :] + arrived_ref[:rows, :].astype(jnp.float32)
        send_ref[...] = (keep_ref[rows:, :] + arrived_ref[rows:, :].astype(jnp.float32)).astype(
            send_ref.dtype
        )

    return ordered(
        kernel,
        [keep, arrived],
        [columns_of(keep, width, at), columns_of(arrived, width, at)],
        [
            jax.ShapeDtypeStruct((rows, width), jnp.float32),
            jax.ShapeDtypeStruct((rows, width), jnp.bfloat16),
        ],
        after,
    )


def error_of(keep, arrived, bias, target, width, at, after):
    rows = keep.shape[0]

    def kernel(keep_ref, arrived_ref, bias_ref, target_ref, error_ref, half_ref):
        total = keep_ref[...] + arrived_ref[...].astype(jnp.float32)
        error = total + bias_ref[...] - target_ref[...].astype(jnp.float32)
        error_ref[...] = error
        half_ref[...] = error.astype(half_ref.dtype)

    return ordered(
        kernel,
        [keep, arrived, bias, target],
        [
            columns_of(keep, width, 0),
            columns_of(arrived, width, 0),
            columns_of(bias, width, at),
            columns_of(target, width, at),
        ],
        [
            jax.ShapeDtypeStruct((rows, width), jnp.float32),
            jax.ShapeDtypeStruct((rows, width), jnp.bfloat16),
        ],
        after,
    )


def joined(pieces, after):
    rows, width = pieces[0][0].shape

    def kernel(*refs):
        out_ref = refs[-1]
        for i in range(len(pieces)):
            columns = slice(i * width, (i + 1) * width)
            out_ref[:rows, columns] = refs[2 * i][...]
            out_ref[rows:, columns] = refs[2 * i + 1][...]

    operands = [x for piece in pieces for x in piece]
    return ordered(
        kernel,
        operands,
        [columns_of(x, width, 0) for x in operands],
        [jax.ShapeDtypeStruct((2 * rows, width * len(pieces)), jnp.bfloat16)],
        after,
    )[0]


def local(resid, enc_weight, enc_bias, active, dec_weight, dec_bias, target):
    features = enc_weight.shape[2]
    layers = dec_weight.shape[1]
    tokens, depth = resid.shape[1:]
    slots = active.shape[2]
    shards = lax.axis_size("feat")
    bits = shards.bit_length() - 1
    rows = tokens // shards
    feat_index = lax.axis_index("feat")
    pair_index = lax.axis_index("pair")
    top = pair_index.astype(jnp.int32).reshape(1)
    me = feat_index.astype(jnp.int32).reshape(1)

    offset = active[0] - feat_index * features
    inside = (offset >= 0) & (offset < features)
    slot_index = jnp.sort(jnp.where(inside, offset, FAR), axis=1)

    def folded(x):
        x = x.reshape(tokens // ROWS, ROWS, slots // SLOTS, SLOTS)
        return x.transpose(0, 2, 1, 3).reshape(tokens // ROWS, ROWS * slots)

    def across(x, step):
        return lax.ppermute(x, "pair", [(i, i ^ step) for i in range(layers)])

    far_step, near_step = layers // 2, 1
    own_index = folded(slot_index)
    own_short = own_index.astype(jnp.int16)
    far_short = across(own_short, far_step)
    own_value = folded(encode(resid[0], enc_weight[0], enc_bias, slot_index))
    far_value = across(own_value, far_step)

    def pack(*xs):
        return jnp.stack(xs)

    def wide(x):
        return x.astype(jnp.float32 if x.dtype == jnp.bfloat16 else jnp.int32)

    values = spread(top, (0,), own_index[None], wide(own_value)[None], features, layers)
    near_short = across(pack(own_short, far_short), near_step)
    near_value = across(pack(own_value, far_value), near_step)
    values = spread(
        top, (far_step,), wide(far_short)[None], wide(far_value)[None], features, layers, values
    )
    values = spread(
        top,
        (near_step, near_step + far_step),
        wide(near_short),
        wide(near_value),
        features,
        layers,
        values,
    )

    def swap(x, bit):
        return lax.ppermute(x, "feat", [(i, i ^ (1 << bit)) for i in range(shards)])

    piece = min(PIECE, depth)
    chunk = min(CHUNK, depth)
    per = chunk // piece
    last = values

    class Chunk:
        pass

    chunks = []
    for start in range(0, depth, chunk):
        c = Chunk()
        c.start = start
        ((keep, send),) = rebuild(top, me, values, dec_weight[0], start, chunk, chunk, bits, last)
        last = send
        c.state = [(keep, swap(send, 0), i) for i in range(per)]
        chunks.append(c)

    def reduce_step(c, bit):
        nonlocal last
        for i, (keep, arrived, at) in enumerate(c.state):
            keep, send = split(keep, arrived, piece, at, last)
            last = send
            c.state[i] = (keep, swap(send, bit), 0)

    def error_step(c):
        nonlocal last
        c.errors = []
        for i, (keep, arrived, _) in enumerate(c.state):
            error, near = error_of(
                keep, arrived, dec_bias, target[0], piece, c.start // piece + i, last
            )
            last = near
            c.errors.append(error)
            c.state[i] = (near, swap(near, bits - 1))

    def gather_step(c, bit):
        nonlocal last
        if bit > 0:
            for i, pair in enumerate(c.state):
                near = joined([pair], last)
                last = near
                c.state[i] = (near, swap(near, bit))
        else:
            near = joined(c.state, last)
            last = near
            c.halves = [(near, swap(near, 0))]

    def first_steps(c):
        return [lambda: reduce_step(c, 1)]

    def later_steps(c):
        steps = [lambda bit=bit: reduce_step(c, bit) for bit in range(2, bits)]
        steps.append(lambda: error_step(c))
        steps += [lambda bit=bit: gather_step(c, bit) for bit in reversed(range(bits - 1))]
        return steps

    plan = first_steps(chunks[0]) + later_steps(chunks[0])
    for c in chunks[1:]:
        plan = plan[:-1] + first_steps(c) + plan[-1:] + later_steps(c)
    for step in plan:
        step()
    grads = None
    for c in chunks:
        grads = gradients(
            top, me, values, c.halves, c.start, chunk, depth, bits, grads, last
        )
    error = jnp.concatenate([error for c in chunks for error in c.errors], axis=1)
    return (error[None], grads[None])


def solution(mesh):
    in_specs = (
        P("pair", None, None),
        P("pair", None, "feat"),
        P("pair", "feat"),
        P("pair", None, None),
        P("pair", None, "feat", None),
        P("pair", None),
        P("pair", "feat", None),
    )
    out_specs = (P("pair", "feat", None), P("pair", None, "feat", None))
    return jax.shard_map(local, mesh=mesh, in_specs=in_specs, out_specs=out_specs, check_vma=False)
```

time: 581 us -> 234 us (0.40)
  waiting for transfers between devices: 327 us -> 61.3 us
  matrix products: 133 us -> 0 us
  Pallas kernels: 0 us -> 127 us
  other arithmetic: 89.3 us -> 7.46 us
  starting transfers between devices: 0.3 us -> 22.9 us
  between operations: 13.8 us -> 2.29 us
  local copies, waits for them, and re-layouts: 16.8 us -> 8.75 us
    all_gather x2 -> x0, waiting for transfers between devices: 177 us -> none  [the longest x1 107 us: local(): gathered = lax.all_gather(values[None], 'pair', axis=0, tiled=True)]
    reduce_scatter x1 -> x0, waiting for transfers between devices: 149 us -> none  [local(): lax.psum_scatter(lax.fori_loop(0, pair_index + 1, add_source, jnp.zeros((...]
    dot_general x9 -> x0, matrix products: 133 us -> none  [the longest x4 62.7 us: add_source(): jnp.dot(left_rows, weight_rows, preferred_element_type=jnp.float32)]
    pallas_call x0 -> x26, Pallas kernels: none -> 127 us  [the longest x2 45.4 us: gradients(): pl.pallas_call(functools.partial(grad_kernel, bits, pieces), grid_spec=pl...]
    reduce_or x1 -> x3, other arithmetic: 86.8 us -> 1.46 us  [spread(): jnp.any(index[:, :, ROWS * SLOTS:] != FAR, axis=(1, 2)).astype(jnp.int32)]
    ppermute x0 -> x24, waiting for transfers between devices: none -> 61.3 us  [the longest x20 61.3 us: swap(): return lax.ppermute(x, 'feat', [(i, i ^ 1 << bit) for i in range(shards)])]
    ppermute x0 -> x24, starting transfers between devices: none -> 22.9 us  [the longest x20 19.9 us: swap(): return lax.ppermute(x, 'feat', [(i, i ^ 1 << bit) for i in range(shards)])]
    broadcast_in_dim x1 -> x0, local copies, waits for them, and re-layouts: 11.2 us -> none  [local(): empty = jnp.zeros((layers, slice_width, model_width), jnp.bfloat16)]
  transfers between devices with their start and end apart: 3 -> 24, of which waited for: 3 -> 17; matrix products, arithmetic and copies ran while one was open for 0% -> 2% of each run, Pallas kernels for 0% -> 24%
where the time goes in v1:
time: 234 us; the launch traced here: 230 us
  Pallas kernels  127 us (54%)
  waiting for transfers between devices  61.3 us (26%)
  starting transfers between devices  22.9 us (10%)
  local copies, waits for them, and re-layouts  8.75 us (4%)
  other arithmetic  7.46 us (3%)
    ppermute x20, waiting for transfers between devices, swap(): return lax.ppermute(x, 'feat', [(i, i ^ 1 << bit) for i in range(shards)])  61.3 us
    pallas_call x2, Pallas kernels, gradients(): pl.pallas_call(functools.partial(grad_kernel, bits, pieces), grid_spec=pl...  45.4 us
    pallas_call x2, Pallas kernels, rebuild(): pl.pallas_call(functools.partial(rebuild_kernel, bits), grid_spec=pltpu.P...  43.6 us
    ppermute x20, starting transfers between devices, swap(): return lax.ppermute(x, 'feat', [(i, i ^ 1 << bit) for i in range(shards)])  19.9 us
    pallas_call x3, Pallas kernels, spread(): pl.pallas_call(spread_kernel, grid_spec=pltpu.PrefetchScalarGridSpec(num_...  19.3 us
    pallas_call x1, Pallas kernels, encode(): pl.pallas_call(encode_kernel, grid=(steps + 1,), in_specs=[pl.BlockSpec((...  17.9 us
    unnamed x12, local copies, waits for them, and re-layouts  6.28 us
  transfers between devices with their start and end apart: 24, of which 17 were waited for; matrix products, arithmetic and copies ran while one was open for 2% of the time, Pallas kernels for 24%

profile of v1, /device:TPU:7, one launch (start us, length us, event | category | flops | bytes accessed | tf_op | source)
XLA Modules:
  0.0 230.1 jit_solution(15382213234716948189)
XLA Ops:
  1.7 3.7 %sort.14 = (s32[1024,64]{0,1:T(8,128)S(1)}, s32[1024,64]{0,1:T(8,128)}) sort(s32[1024,64]{0,1:T(8,128)S(1)} %bitcast_select_fusion, s32[1024,64]{0,1:T(8,128)S(1)} %iota.3), dimensions={1}, to_apply=%region_0.1 | sort | flops 1048576 | bytes 1048576 | tf_op jit(solution)/shard_map/jit(sort)/sort | solution.py:423
  5.6 3.4 %copy-done.3 = bf16[1,2048,2048]{2,1,0:T(8,128)(2,1)S(1)} copy-done((bf16[1,2048,2048]{2,1,0:T(8,128)(2,1)S(1)}, bf16[1,2048,2048]{2,1,0:T(8,128)(2,1)}, u32[]{:S(2)}) %copy-start.3) | copy-done | bytes 8388632
  8.9 2.2 copy-done.4
  11.8 17.9 %shard_map.113 = bf16[1024,64]{1,0:T(8,128)(2,1)S(1)} custom-call(bf16[1024,2048]{1,0:T(8,128)(2,1)S(1)} %bitcast.38, bf16[2048,2048]{1,0:T(8,128)(2,1)S(1)} %bitcast.37, f32[1,2048]{1,0:T(1,128)S(1)} %copy-done.5, s32[1024,64]{1,0:T(8,128)S(1)} %copy.30.slot_ref), custom_call_target="tpu_custom_call" | custom-call | flops 8589934592 | bytes 12582912 | tf_op jit(solution)/shard_map/pallas_call | solution.py:68
  35.0 4.9 %shard_map.114.refs_0_ = bf16[4,1024,2048]{2,1,0:T(8,128)(2,1)} custom-call(s32[1]{0:T(128)} %bitcast.top_ref, s32[1]{0:T(128)} %bitcast.14.deep_ref, s32[1]{0:T(128)} %constant.26.clone.place_ref, s32[1,128,512]{2,1,0:T(8,128)S(1)} %copy.32.index_ref, f32[1,128,512]{2,1,0:T(8,128)S(1)} %convert_element_type.56.value_ref), custom_call_target="tpu_custom_call" | custom-call | flops 4194304000 | bytes 4194304 | tf_op jit(solution)/shard_map/pallas_call | solution.py:162
  40.0 1.4 collective-permute-start.3
  42.9 5.0 %shard_map.115.refs_0_ = bf16[4,1024,2048]{2,1,0:T(8,128)(2,1)} custom-call(s32[1]{0:T(128)} %bitcast.top_ref, s32[1]{0:T(128)} %bitcast.13.deep_ref, s32[1]{0:T(128)} %constant.27.clone.place_ref, s32[1,128,512]{2,1,0:T(8,128)S(1)} %bitcast_convert_fusion.2.index_ref, ...), custom_call_target="tpu_custom_call", output_to_operand_aliasing={{}: (5, {})} | custom-call | flops 4194304000 | bytes 4194304 | tf_op jit(solution)/shard_map/pallas_call | solution.py:162
  48.2 9.4 %shard_map.116.value_ref.after_ref = bf16[4,1024,2048]{2,1,0:T(8,128)(2,1)} custom-call(s32[1]{0:T(128)} %bitcast.top_ref, s32[2]{0:T(128)S(1)} %convert_element_type.50.deep_ref, s32[2]{0:T(128)S(1)} %copy-done.2, s32[2,128,512]{2,1,0:T(8,128)S(1)} %convert_element_type.49.index_ref, ...), custom_call_target="tpu_custom_call", output_to_operand_aliasing={{}: (5, {})} | custom-call | flops 8388608000 | bytes 8388608 | tf_op jit(solution)/shard_map/pallas_call | solution.py:162
  57.6 21.8 %shard_map.117 = (f32[512,1024]{1,0:T(8,128)S(1)}, bf16[512,1024]{1,0:T(8,128)(2,1)S(1)}) custom-call(s32[1]{0:T(128)} %bitcast.top_ref, s32[1]{0:T(128)} %bitcast.1.me_ref, bf16[4,1024,2048]{2,1,0:T(8,128)(2,1)} %shard_map.116.value_ref.after_ref, bf16[4,2048,2048]{2,1,0:T(8,128)(2,1)} %bitcast.39, bf16[4,1024,2048]{2,1,0:T(8,128)(2,1)} %shard_map.116.value_ref.after_ref), custom_call_target="tpu_custom_call" | custom-call | flops 17179869184 | bytes 33554432 | tf_op jit(solution)/shard_map/pallas_call | solution.py:223
  79.8 21.8 %shard_map.118 = (f32[512,1024]{1,0:T(8,128)S(1)}, bf16[512,1024]{1,0:T(8,128)(2,1)S(1)}) custom-call(s32[1]{0:T(128)} %bitcast.top_ref, s32[1]{0:T(128)} %bitcast.1.me_ref, bf16[4,1024,2048]{2,1,0:T(8,128)(2,1)} %shard_map.116.value_ref.after_ref, bf16[4,2048,2048]{2,1,0:T(8,128)(2,1)} %bitcast.40, bf16[512,1024]{1,0:T(8,128)(2,1)S(1)} %get-tuple-element.34.after_ref), custom_call_target="tpu_custom_call" | custom-call | flops 17179869184 | bytes 33554432 | tf_op jit(solution)/shard_map/pallas_call | solution.py:223
  105.5 5.6 %collective-permute-done.5.refs_1_ = bf16[256,512]{1,0:T(8,128)(2,1)S(1)} collective-permute-done((bf16[256,512]{1,0:T(8,128)(2,1)S(1)}, bf16[256,512]{1,0:T(8,128)(2,1)S(1)}, u32[]{:S(2)}, u32[]{:S(2)}) %collective-permute-start.5) | collective-permute-done | bytes 262176 | tf_op jit(solution)/shard_map/ppermute | solution.py:462
  111.2 2.1 collective-permute-start.6
  113.3 3.0 %collective-permute-done.7.refs_1_ = bf16[256,512]{1,0:T(8,128)(2,1)S(1)} collective-permute-done((bf16[256,512]{1,0:T(8,128)(2,1)S(1)}, bf16[256,512]{1,0:T(8,128)(2,1)S(1)}, u32[]{:S(2)}, u32[]{:S(2)}) %collective-permute-start.7) | collective-permute-done | bytes 262176 | tf_op jit(solution)/shard_map/ppermute | solution.py:462
  116.3 2.0 collective-permute-start.8
  118.4 3.6 %collective-permute-done.6.refs_1_ = bf16[128,512]{1,0:T(8,128)(2,1)S(1)} collective-permute-done((bf16[128,512]{1,0:T(8,128)(2,1)S(1)}, bf16[128,512]{1,0:T(8,128)(2,1)S(1)}, u32[]{:S(2)}, u32[]{:S(2)}) %collective-permute-start.6) | collective-permute-done | bytes 131104 | tf_op jit(solution)/shard_map/ppermute | solution.py:462
  124.6 3.3 %collective-permute-done.11.refs_1_ = bf16[128,512]{1,0:T(8,128)(2,1)S(1)} collective-permute-done((bf16[128,512]{1,0:T(8,128)(2,1)S(1)}, bf16[128,512]{1,0:T(8,128)(2,1)S(1)}, u32[]{:S(2)}, u32[]{:S(2)}) %collective-permute-start.11) | collective-permute-done | bytes 131104 | tf_op jit(solution)/shard_map/ppermute | solution.py:462
  128.0 2.6 %collective-permute-done.10.refs_1_ = bf16[128,512]{1,0:T(8,128)(2,1)S(1)} collective-permute-done((bf16[128,512]{1,0:T(8,128)(2,1)S(1)}, bf16[128,512]{1,0:T(8,128)(2,1)S(1)}, u32[]{:S(2)}, u32[]{:S(2)}) %collective-permute-start.10) | collective-permute-done | bytes 131104 | tf_op jit(solution)/shard_map/ppermute | solution.py:462
  132.3 3.6 %collective-permute-done.14.refs_3_ = bf16[256,512]{1,0:T(8,128)(2,1)S(1)} collective-permute-done((bf16[256,512]{1,0:T(8,128)(2,1)S(1)}, bf16[256,512]{1,0:T(8,128)(2,1)S(1)}, u32[]{:S(2)}, u32[]{:S(2)}) %collective-permute-start.14) | collective-permute-done | bytes 262176 | tf_op jit(solution)/shard_map/ppermute | solution.py:462
  135.9 3.6 %collective-permute-done.13.refs_1_ = bf16[256,512]{1,0:T(8,128)(2,1)S(1)} collective-permute-done((bf16[256,512]{1,0:T(8,128)(2,1)S(1)}, bf16[256,512]{1,0:T(8,128)(2,1)S(1)}, u32[]{:S(2)}, u32[]{:S(2)}) %collective-permute-start.13) | collective-permute-done | bytes 262176 | tf_op jit(solution)/shard_map/ppermute | solution.py:462
  139.6 1.8 collective-permute-start.23
  142.9 6.0 %collective-permute-done.12.refs_1_ = bf16[256,512]{1,0:T(8,128)(2,1)S(1)} collective-permute-done((bf16[256,512]{1,0:T(8,128)(2,1)S(1)}, bf16[256,512]{1,0:T(8,128)(2,1)S(1)}, u32[]{:S(2)}, u32[]{:S(2)}) %collective-permute-start.12) | collective-permute-done | bytes 262176 | tf_op jit(solution)/shard_map/ppermute | solution.py:462
  148.9 1.5 collective-permute-start.15
  150.4 3.4 %collective-permute-done.16.refs_1_ = bf16[256,512]{1,0:T(8,128)(2,1)S(1)} collective-permute-done((bf16[256,512]{1,0:T(8,128)(2,1)S(1)}, bf16[256,512]{1,0:T(8,128)(2,1)S(1)}, u32[]{:S(2)}, u32[]{:S(2)}) %collective-permute-start.16) | collective-permute-done | bytes 262176 | tf_op jit(solution)/shard_map/ppermute | solution.py:462
  154.1 6.5 %collective-permute-done.15.refs_1_ = bf16[128,512]{1,0:T(8,128)(2,1)S(1)} collective-permute-done((bf16[128,512]{1,0:T(8,128)(2,1)S(1)}, bf16[128,512]{1,0:T(8,128)(2,1)S(1)}, u32[]{:S(2)}, u32[]{:S(2)}) %collective-permute-start.15) | collective-permute-done | bytes 131104 | tf_op jit(solution)/shard_map/ppermute | solution.py:462
  160.7 2.7 %collective-permute-done.17.refs_1_ = bf16[128,512]{1,0:T(8,128)(2,1)S(1)} collective-permute-done((bf16[128,512]{1,0:T(8,128)(2,1)S(1)}, bf16[128,512]{1,0:T(8,128)(2,1)S(1)}, u32[]{:S(2)}, u32[]{:S(2)}) %collective-permute-start.17) | collective-permute-done | bytes 131104 | tf_op jit(solution)/shard_map/ppermute | solution.py:462
  163.5 1.9 collective-permute-done.18.refs_1_
  165.4 4.5 %collective-permute-done.20.refs_1_ = bf16[128,512]{1,0:T(8,128)(2,1)S(1)} collective-permute-done((bf16[128,512]{1,0:T(8,128)(2,1)S(1)}, bf16[128,512]{1,0:T(8,128)(2,1)S(1)}, u32[]{:S(2)}, u32[]{:S(2)}) %collective-permute-start.20) | collective-permute-done | bytes 131104 | tf_op jit(solution)/shard_map/ppermute | solution.py:462
  170.0 3.2 %collective-permute-start.21 = (bf16[256,512]{1,0:T(8,128)(2,1)S(1)}, bf16[256,512]{1,0:T(8,128)(2,1)S(1)}, u32[]{:S(2)}, u32[]{:S(2)}) collective-permute-start(bf16[256,512]{1,0:T(8,128)(2,1)S(1)} %shard_map.135.refs_2_.refs_4_), channel_id=1, source_target_pairs={{0,8},{4,12},{8,0},{12,4},{16,24},{20,28},{24,16},{28,20},{1,9},{5... | collective-permute-start | bytes 786440 | tf_op jit(solution)/shard_map/ppermute | solution.py:462
  174.3 5.8 %collective-permute-done.21.refs_3_ = bf16[256,512]{1,0:T(8,128)(2,1)S(1)} collective-permute-done((bf16[256,512]{1,0:T(8,128)(2,1)S(1)}, bf16[256,512]{1,0:T(8,128)(2,1)S(1)}, u32[]{:S(2)}, u32[]{:S(2)}) %collective-permute-start.21) | collective-permute-done | bytes 262176 | tf_op jit(solution)/shard_map/ppermute | solution.py:462
  180.1 3.1 %collective-permute-done.19.refs_1_ = bf16[256,512]{1,0:T(8,128)(2,1)S(1)} collective-permute-done((bf16[256,512]{1,0:T(8,128)(2,1)S(1)}, bf16[256,512]{1,0:T(8,128)(2,1)S(1)}, u32[]{:S(2)}, u32[]{:S(2)}) %collective-permute-start.19) | collective-permute-done | bytes 262176 | tf_op jit(solution)/shard_map/ppermute | solution.py:462
  184.6 22.7 %shard_map.137.refs_3_ = bf16[4,2048,2048]{2,1,0:T(8,128)(2,1)} custom-call(s32[1]{0:T(128)} %bitcast.top_ref, s32[1]{0:T(128)} %bitcast.1.me_ref, bf16[4,1024,2048]{2,1,0:T(8,128)(2,1)} %shard_map.116.value_ref.after_ref, bf16[512,1024]{1,0:T(8,128)(2,1)S(1)} %shard_map.129.refs_2_.refs_0_, bf16[512,1024]{1,0:T(8,128)(2,1)S(1)} %collective-permute-done.23.refs_1_, ...), custom_call_target="tpu_custom_call" | custom-call | flops 17179869184 | bytes 33554432 | tf_op jit(solution)/shard_map/pallas_call | solution.py:302
  207.3 22.7 %shard_map.138 = bf16[4,2048,2048]{2,1,0:T(8,128)(2,1)} custom-call(s32[1]{0:T(128)} %bitcast.top_ref, s32[1]{0:T(128)} %bitcast.1.me_ref, bf16[4,1024,2048]{2,1,0:T(8,128)(2,1)} %shard_map.116.value_ref.after_ref, bf16[512,1024]{1,0:T(8,128)(2,1)S(1)} %shard_map.136.refs_2_.refs_0_, ...), custom_call_target="tpu_custom_call", output_to_operand_aliasing={{}: (6, {})} | custom-call | flops 17179869184 | bytes 33554432 | tf_op jit(solution)/shard_map/pallas_call | solution.py:302
  (80 shorter events, 21.1 us)
Async XLA Ops:
  5.5 3.4 %copy-start.3 = (bf16[1,2048,2048]{2,1,0:T(8,128)(2,1)S(1)}, bf16[1,2048,2048]{2,1,0:T(8,128)(2,1)}, u32[]{:S(2)}) copy-start(bf16[1,2048,2048]{2,1,0:T(8,128)(2,1)} %param.11) | copy-start | bytes 25165828
  8.9 2.2 copy-start.4
  11.1 0.7 copy-start.5
  30.6 9.4 %collective-permute-start.2 = (bf16[128,512]{1,0:T(8,128)(2,1)S(1)}, bf16[128,512]{1,0:T(8,128)(2,1)S(1)}, u32[]{:S(2)}, u32[]{:S(2)}) collective-permute-start(bf16[128,512]{1,0:T(8,128)(2,1)S(1)} %copy.37), channel_id=1, source_target_pairs={{0,2},{1,3},{2,0},{3,1},{4,6},{5,7},{6,4},{7,5},{8,10},{9,11},{10,... | collective-permute-start | bytes 393224 | tf_op jit(solution)/shard_map/ppermute | solution.py:430
  32.1 9.2 %collective-permute-start = (s16[128,512]{1,0:T(8,128)(2,1)S(1)}, s16[128,512]{1,0:T(8,128)(2,1)S(1)}, u32[]{:S(2)}, u32[]{:S(2)}) collective-permute-start(s16[128,512]{1,0:T(8,128)(2,1)S(1)} %copy.33), channel_id=1, source_target_pairs={{0,2},{1,3},{2,0},{3,1},{4,6},{5,7},{6,4},{7,5},{8,10},{9,11},{10,... | collective-permute-start | bytes 393224 | tf_op jit(solution)/shard_map/ppermute | solution.py:430
  40.0 8.1 %collective-permute-start.3 = (bf16[2,128,512]{2,1,0:T(8,128)(2,1)S(1)}, bf16[2,128,512]{2,1,0:T(8,128)(2,1)S(1)}, u32[]{:S(2)}, u32[]{:S(2)}) collective-permute-start(bf16[2,128,512]{2,1,0:T(8,128)(2,1)S(1)} %pad_maximum_fusion), channel_id=1, source_target_pairs={{0,1},{1,0},{2,3},{3,2},{4,5},{5,4},{6,7},{7,6},{8,9},{9,8},{10,11... | collective-permute-start | bytes 786440 | tf_op jit(solution)/shard_map/ppermute | solution.py:430
  42.8 5.1 %collective-permute-start.1 = (s16[2,128,512]{2,1,0:T(8,128)(2,1)S(1)}, s16[2,128,512]{2,1,0:T(8,128)(2,1)S(1)}, u32[]{:S(2)}, u32[]{:S(2)}) collective-permute-start(s16[2,128,512]{2,1,0:T(8,128)(2,1)S(1)} %pad_add_fusion), channel_id=1, source_target_pairs={{0,1},{1,0},{2,3},{3,2},{4,5},{5,4},{6,7},{7,6},{8,9},{9,8},{10,11... | collective-permute-start | bytes 786440 | tf_op jit(solution)/shard_map/ppermute | solution.py:430
  42.9 5.3 %copy-start.2 = (s32[2]{0:T(128)S(1)}, s32[2]{0:T(128)}, u32[]{:S(2)}) copy-start(s32[2]{0:T(128)} %constant.28.clone.place_ref) | copy-start | bytes 28
  79.4 42.6 %copy-start = (bf16[1,128,2048]{2,1,0:T(8,128)(2,1)S(1)}, bf16[1,128,2048]{2,1,0:T(8,128)(2,1)}, u32[]{:S(2)}) copy-start(bf16[1,128,2048]{2,1,0:T(8,128)(2,1)} %param.16) | copy-start | bytes 1572868
  79.4 42.6 %copy-start.1 = (f32[1,2048]{1,0:T(1,128)S(1)}, f32[1,2048]{1,0:T(1,128)}, u32[]{:S(2)}) copy-start(f32[1,2048]{1,0:T(1,128)} %refs_2_.7) | copy-start | bytes 24580
  79.5 24.3 %collective-permute-start.4 = (bf16[512,1024]{1,0:T(8,128)(2,1)S(1)}, bf16[512,1024]{1,0:T(8,128)(2,1)S(1)}, u32[]{:S(2)}, u32[]{:S(2)}) collective-permute-start(bf16[512,1024]{1,0:T(8,128)(2,1)S(1)} %get-tuple-element.34.after_ref), channel_id=1, source_target_pairs={{0,4},{4,0},{8,12},{12,8},{16,20},{20,16},{24,28},{28,24},{1,5},{5... | collective-permute-start | bytes 3145736 | tf_op jit(solution)/shard_map/ppermute | solution.py:462
  101.6 30.6 %collective-permute-start.9 = (bf16[512,1024]{1,0:T(8,128)(2,1)S(1)}, bf16[512,1024]{1,0:T(8,128)(2,1)S(1)}, u32[]{:S(2)}, u32[]{:S(2)}) collective-permute-start(bf16[512,1024]{1,0:T(8,128)(2,1)S(1)} %get-tuple-element.35.refs_2_), channel_id=1, source_target_pairs={{0,4},{4,0},{8,12},{12,8},{16,20},{20,16},{24,28},{28,24},{1,5},{5... | collective-permute-start | bytes 3145736 | tf_op jit(solution)/shard_map/ppermute | solution.py:462
  103.8 7.3 %collective-permute-start.5 = (bf16[256,512]{1,0:T(8,128)(2,1)S(1)}, bf16[256,512]{1,0:T(8,128)(2,1)S(1)}, u32[]{:S(2)}, u32[]{:S(2)}) collective-permute-start(bf16[256,512]{1,0:T(8,128)(2,1)S(1)} %get-tuple-element.37.refs_2_), channel_id=1, source_target_pairs={{0,8},{4,12},{8,0},{12,4},{16,24},{20,28},{24,16},{28,20},{1,9},{5... | collective-permute-start | bytes 786440 | tf_op jit(solution)/shard_map/ppermute | solution.py:462
  105.3 11.0 %collective-permute-start.7 = (bf16[256,512]{1,0:T(8,128)(2,1)S(1)}, bf16[256,512]{1,0:T(8,128)(2,1)S(1)}, u32[]{:S(2)}, u32[]{:S(2)}) collective-permute-start(bf16[256,512]{1,0:T(8,128)(2,1)S(1)} %get-tuple-element.38.refs_2_), channel_id=1, source_target_pairs={{0,8},{4,12},{8,0},{12,4},{16,24},{20,28},{24,16},{28,20},{1,9},{5... | collective-permute-start | bytes 786440 | tf_op jit(solution)/shard_map/ppermute | solution.py:462
  111.2 10.8 %collective-permute-start.6 = (bf16[128,512]{1,0:T(8,128)(2,1)S(1)}, bf16[128,512]{1,0:T(8,128)(2,1)S(1)}, u32[]{:S(2)}, u32[]{:S(2)}) collective-permute-start(bf16[128,512]{1,0:T(8,128)(2,1)S(1)} %get-tuple-element.40.refs_2_), channel_id=1, source_target_pairs={{0,16},{4,20},{8,24},{12,28},{16,0},{20,4},{24,8},{28,12},{1,17},{... | collective-permute-start | bytes 393224 | tf_op jit(solution)/shard_map/ppermute | solution.py:462
  116.3 7.1 %collective-permute-start.8 = (bf16[128,512]{1,0:T(8,128)(2,1)S(1)}, bf16[128,512]{1,0:T(8,128)(2,1)S(1)}, u32[]{:S(2)}, u32[]{:S(2)}) collective-permute-start(bf16[128,512]{1,0:T(8,128)(2,1)S(1)} %get-tuple-element.42.refs_4_), channel_id=1, source_target_pairs={{0,16},{4,20},{8,24},{12,28},{16,0},{20,4},{24,8},{28,12},{1,17},{... | collective-permute-start | bytes 393224 | tf_op jit(solution)/shard_map/ppermute | solution.py:462
  122.1 5.9 %collective-permute-start.11 = (bf16[128,512]{1,0:T(8,128)(2,1)S(1)}, bf16[128,512]{1,0:T(8,128)(2,1)S(1)}, u32[]{:S(2)}, u32[]{:S(2)}) collective-permute-start(bf16[128,512]{1,0:T(8,128)(2,1)S(1)} %get-tuple-element.45.refs_4_.refs_0_), channel_id=1, source_target_pairs={{0,16},{4,20},{8,24},{12,28},{16,0},{20,4},{24,8},{28,12},{1,17},{... | collective-permute-start | bytes 393224 | tf_op jit(solution)/shard_map/ppermute | solution.py:462
  123.5 7.1 %collective-permute-start.10 = (bf16[128,512]{1,0:T(8,128)(2,1)S(1)}, bf16[128,512]{1,0:T(8,128)(2,1)S(1)}, u32[]{:S(2)}, u32[]{:S(2)}) collective-permute-start(bf16[128,512]{1,0:T(8,128)(2,1)S(1)} %get-tuple-element.48.refs_2_.refs_0_), channel_id=1, source_target_pairs={{0,16},{4,20},{8,24},{12,28},{16,0},{20,4},{24,8},{28,12},{1,17},{... | collective-permute-start | bytes 393224 | tf_op jit(solution)/shard_map/ppermute | solution.py:462
  130.6 5.3 %collective-permute-start.14 = (bf16[256,512]{1,0:T(8,128)(2,1)S(1)}, bf16[256,512]{1,0:T(8,128)(2,1)S(1)}, u32[]{:S(2)}, u32[]{:S(2)}) collective-permute-start(bf16[256,512]{1,0:T(8,128)(2,1)S(1)} %shard_map.126.refs_2_), channel_id=1, source_target_pairs={{0,8},{4,12},{8,0},{12,4},{16,24},{20,28},{24,16},{28,20},{1,9},{5... | collective-permute-start | bytes 786440 | tf_op jit(solution)/shard_map/ppermute | solution.py:462
  131.9 7.6 %collective-permute-start.13 = (bf16[256,512]{1,0:T(8,128)(2,1)S(1)}, bf16[256,512]{1,0:T(8,128)(2,1)S(1)}, u32[]{:S(2)}, u32[]{:S(2)}) collective-permute-start(bf16[256,512]{1,0:T(8,128)(2,1)S(1)} %shard_map.125.refs_2_.refs_0_), channel_id=1, source_target_pairs={{0,8},{4,12},{8,0},{12,4},{16,24},{20,28},{24,16},{28,20},{1,9},{5... | collective-permute-start | bytes 786440 | tf_op jit(solution)/shard_map/ppermute | solution.py:462
  139.6 45.0 %collective-permute-start.23 = (bf16[512,1024]{1,0:T(8,128)(2,1)S(1)}, bf16[512,1024]{1,0:T(8,128)(2,1)S(1)}, u32[]{:S(2)}, u32[]{:S(2)}) collective-permute-start(bf16[512,1024]{1,0:T(8,128)(2,1)S(1)} %shard_map.129.refs_2_.refs_0_), channel_id=1, source_target_pairs={{0,4},{4,0},{8,12},{12,8},{16,20},{20,16},{24,28},{28,24},{1,5},{5... | collective-permute-start | bytes 3145736 | tf_op jit(solution)/shard_map/ppermute | solution.py:462
  141.4 7.4 %collective-permute-start.12 = (bf16[256,512]{1,0:T(8,128)(2,1)S(1)}, bf16[256,512]{1,0:T(8,128)(2,1)S(1)}, u32[]{:S(2)}, u32[]{:S(2)}) collective-permute-start(bf16[256,512]{1,0:T(8,128)(2,1)S(1)} %get-tuple-element.50.refs_2_), channel_id=1, source_target_pairs={{0,8},{4,12},{8,0},{12,4},{16,24},{20,28},{24,16},{28,20},{1,9},{5... | collective-permute-start | bytes 786440 | tf_op jit(solution)/shard_map/ppermute | solution.py:462
  142.1 11.7 %collective-permute-start.16 = (bf16[256,512]{1,0:T(8,128)(2,1)S(1)}, bf16[256,512]{1,0:T(8,128)(2,1)S(1)}, u32[]{:S(2)}, u32[]{:S(2)}) collective-permute-start(bf16[256,512]{1,0:T(8,128)(2,1)S(1)} %get-tuple-element.51.refs_4_), channel_id=1, source_target_pairs={{0,8},{4,12},{8,0},{12,4},{16,24},{20,28},{24,16},{28,20},{1,9},{5... | collective-permute-start | bytes 786440 | tf_op jit(solution)/shard_map/ppermute | solution.py:462
  148.9 11.7 %collective-permute-start.15 = (bf16[128,512]{1,0:T(8,128)(2,1)S(1)}, bf16[128,512]{1,0:T(8,128)(2,1)S(1)}, u32[]{:S(2)}, u32[]{:S(2)}) collective-permute-start(bf16[128,512]{1,0:T(8,128)(2,1)S(1)} %get-tuple-element.53.refs_2_), channel_id=1, source_target_pairs={{0,16},{4,20},{8,24},{12,28},{16,0},{20,4},{24,8},{28,12},{1,17},{... | collective-permute-start | bytes 393224 | tf_op jit(solution)/shard_map/ppermute | solution.py:462
  153.8 9.6 %collective-permute-start.17 = (bf16[128,512]{1,0:T(8,128)(2,1)S(1)}, bf16[128,512]{1,0:T(8,128)(2,1)S(1)}, u32[]{:S(2)}, u32[]{:S(2)}) collective-permute-start(bf16[128,512]{1,0:T(8,128)(2,1)S(1)} %get-tuple-element.55.refs_4_), channel_id=1, source_target_pairs={{0,16},{4,20},{8,24},{12,28},{16,0},{20,4},{24,8},{28,12},{1,17},{... | collective-permute-start | bytes 393224 | tf_op jit(solution)/shard_map/ppermute | solution.py:462
  160.6 4.8 %collective-permute-start.18 = (bf16[128,512]{1,0:T(8,128)(2,1)S(1)}, bf16[128,512]{1,0:T(8,128)(2,1)S(1)}, u32[]{:S(2)}, u32[]{:S(2)}) collective-permute-start(bf16[128,512]{1,0:T(8,128)(2,1)S(1)} %get-tuple-element.58.refs_4_.refs_0_), channel_id=1, source_target_pairs={{0,16},{4,20},{8,24},{12,28},{16,0},{20,4},{24,8},{28,12},{1,17},{... | collective-permute-start | bytes 393224 | tf_op jit(solution)/shard_map/ppermute | solution.py:462
  163.4 6.5 %collective-permute-start.20 = (bf16[128,512]{1,0:T(8,128)(2,1)S(1)}, bf16[128,512]{1,0:T(8,128)(2,1)S(1)}, u32[]{:S(2)}, u32[]{:S(2)}) collective-permute-start(bf16[128,512]{1,0:T(8,128)(2,1)S(1)} %get-tuple-element.60.refs_2_.refs_0_), channel_id=1, source_target_pairs={{0,16},{4,20},{8,24},{12,28},{16,0},{20,4},{24,8},{28,12},{1,17},{... | collective-permute-start | bytes 393224 | tf_op jit(solution)/shard_map/ppermute | solution.py:462
  170.0 10.1 %collective-permute-start.21 = (bf16[256,512]{1,0:T(8,128)(2,1)S(1)}, bf16[256,512]{1,0:T(8,128)(2,1)S(1)}, u32[]{:S(2)}, u32[]{:S(2)}) collective-permute-start(bf16[256,512]{1,0:T(8,128)(2,1)S(1)} %shard_map.135.refs_2_.refs_4_), channel_id=1, source_target_pairs={{0,8},{4,12},{8,0},{12,4},{16,24},{20,28},{24,16},{28,20},{1,9},{5... | collective-permute-start | bytes 786440 | tf_op jit(solution)/shard_map/ppermute | solution.py:462
  173.1 10.1 %collective-permute-start.19 = (bf16[256,512]{1,0:T(8,128)(2,1)S(1)}, bf16[256,512]{1,0:T(8,128)(2,1)S(1)}, u32[]{:S(2)}, u32[]{:S(2)}) collective-permute-start(bf16[256,512]{1,0:T(8,128)(2,1)S(1)} %shard_map.134.refs_2_.refs_0_), channel_id=1, source_target_pairs={{0,8},{4,12},{8,0},{12,4},{16,24},{20,28},{24,16},{28,20},{1,9},{5... | collective-permute-start | bytes 786440 | tf_op jit(solution)/shard_map/ppermute | solution.py:462
  183.3 24.1 %collective-permute-start.22 = (bf16[512,1024]{1,0:T(8,128)(2,1)S(1)}, bf16[512,1024]{1,0:T(8,128)(2,1)S(1)}, u32[]{:S(2)}, u32[]{:S(2)}) collective-permute-start(bf16[512,1024]{1,0:T(8,128)(2,1)S(1)} %shard_map.136.refs_2_.refs_0_), channel_id=1, source_target_pairs={{0,4},{4,0},{8,12},{12,8},{16,20},{20,16},{24,28},{28,24},{1,5},{5... | collective-permute-start | bytes 3145736 | tf_op jit(solution)/shard_map/ppermute | solution.py:462

commit v2 on v1

v2 whole, which is shorter than its diff:
```python
import functools

import jax
import jax.numpy as jnp
from jax import lax
from jax.experimental import pallas as pl
from jax.experimental.pallas import tpu as pltpu
from jax.sharding import PartitionSpec as P

LANES = 128
ROWS = 8
SLOTS = 32
FAR = 32767
ENCODE_BYTES = 56 * 1024 * 1024
VMEM_BYTES = 24 * 1024 * 1024
SMALL_BYTES = 8 * 1024 * 1024
PIECE = 512
GROUPS = (
    (((1,), (2,)), ((2,), (1,))),
    (((1,), (2,)), ((2,), (1,))),
    (((1,), (2,)), ((2,), (1,))),
    (((1,), (2,)), ((2,), (1,))),
)
REBUILD, GRADIENT = -1, -2
PLAN = (
    (0, REBUILD), (1, REBUILD), (0, 0), (2, REBUILD), (0, 1), (1, 0), (3, REBUILD), (0, 2), (1, 1),
    (2, 0), (0, 3), (1, 2), (2, 1), (0, 4), (3, 0), (1, 3), (2, 2), (3, 1), (1, 4), (2, 3), (3, 2),
    (0, GRADIENT), (2, 4), (3, 3), (1, GRADIENT), (3, 4), (2, GRADIENT), (3, GRADIENT),
)


WHOLE = pl.BlockSpec(memory_space=pltpu.VMEM)


def in_vmem(x):
    return pltpu.with_memory_space_constraint(x, pltpu.VMEM)


def params(limit=VMEM_BYTES):
    return pltpu.CompilerParams(vmem_limit_bytes=limit)


def encode_kernel(resid_ref, weight_ref, bias_ref, slot_ref, out_ref, pre_ref, picked_ref, index_ref):
    step = pl.program_id(0)
    tokens = resid_ref.shape[0]
    width = weight_ref.shape[1]
    slots = slot_ref.shape[1]
    groups = width // LANES

    @pl.when(step == 0)
    def _():
        picked_ref[...] = jnp.zeros_like(picked_ref)
        pre_ref[1] = jnp.zeros_like(pre_ref[1])
        index_ref[...] = jnp.full_like(index_ref, FAR)
        index_ref[:, :slots] = slot_ref[...]

    now = lax.rem(step, 2)
    before = 1 - now
    first = (step - 1) * groups

    def pick():
        for row in range(0, tokens, ROWS):
            rows = pl.ds(row, ROWS)
            index = index_ref[rows, :]
            group = (index >> 7) - first
            lane = index & (LANES - 1)
            picked = picked_ref[rows, :]
            for part in range(groups):
                source = pre_ref[before, rows, part * LANES : (part + 1) * LANES]
                found = jnp.take_along_axis(source, lane, axis=1)
                picked = jnp.where(group == part, found, picked)
            picked_ref[rows, :] = picked

    @pl.when(step < pl.num_programs(0) - 1)
    def _():
        pre_ref[now] = (
            jnp.dot(resid_ref[...], weight_ref[...], preferred_element_type=jnp.float32)
            + bias_ref[...]
        )
        pick()

    @pl.when(step == pl.num_programs(0) - 1)
    def _():
        pick()
        out_ref[...] = jnp.maximum(picked_ref[:, :slots], 0.0).astype(out_ref.dtype)


def encode(resid, weight, bias, slot_index):
    tokens, depth = resid.shape
    features = weight.shape[1]
    slots = slot_index.shape[1]
    width = min(256, features)
    steps = features // width
    return pl.pallas_call(
        encode_kernel,
        grid=(steps + 1,),
        in_specs=[
            WHOLE,
            pl.BlockSpec((depth, width), lambda i: (0, jnp.minimum(i, steps - 1))),
            pl.BlockSpec((1, width), lambda i: (0, jnp.minimum(i, steps - 1))),
            pl.BlockSpec((tokens, slots), lambda i: (0, 0)),
        ],
        out_specs=pl.BlockSpec((tokens, slots), lambda i: (0, 0)),
        out_shape=jax.ShapeDtypeStruct((tokens, slots), jnp.bfloat16),
        scratch_shapes=[
            pltpu.VMEM((2, tokens, width), jnp.float32),
            pltpu.VMEM((tokens, LANES), jnp.float32),
            pltpu.VMEM((tokens, LANES), jnp.int32),
        ],
        compiler_params=params(ENCODE_BYTES),
        cost_estimate=pl.CostEstimate(
            flops=2 * tokens * depth * features,
            bytes_accessed=2 * depth * (features + tokens),
            transcendentals=0,
        ),
    )(in_vmem(resid), weight, bias, slot_index)


def spread_kernel(places, top_ref, deep_ref, index_ref, value_ref, out_ref):
    at = pl.program_id(0)
    place = places[0] + at * (places[-1] - places[0])
    blocks = index_ref.shape[1]
    features = out_ref.shape[2]
    groups = features // LANES
    top = top_ref[0]
    source = jnp.bitwise_xor(top, place)
    span = ROWS * SLOTS

    def rows_of(block, rounds):
        high = lax.broadcasted_iota(jnp.int32, (groups * ROWS, span), 0)
        low = lax.broadcasted_iota(jnp.int32, (LANES, span), 0)
        token = lax.broadcasted_iota(jnp.int32, (1, span), 1) // SLOTS
        total = None
        for turn in range(rounds):
            part = pl.ds(turn * span, span)
            index = index_ref[0, pl.ds(block, 1), part]
            value = value_ref[0, pl.ds(block, 1), part]
            key = (index >> 7) * ROWS + token
            lane = index & (LANES - 1)
            left = jnp.where(
                jnp.broadcast_to(key, high.shape) == high, jnp.broadcast_to(value, high.shape), 0.0
            ).astype(jnp.bfloat16)
            right = jnp.where(jnp.broadcast_to(lane, low.shape) == low, 1.0, 0.0).astype(
                jnp.bfloat16
            )
            part = lax.dot_general(
                left, right, (((1,), (1,)), ((), ())), preferred_element_type=jnp.float32
            )
            total = part if total is None else total + part
        return total

    def run(rounds, unroll):
        def pair(i, carry):
            one, two = rows_of(2 * i, rounds), rows_of(2 * i + 1, rounds)
            first = (pl.program_id(1) * blocks + 2 * i) * ROWS
            rows = pl.ds(pl.multiple_of(first, 2 * ROWS), 2 * ROWS)
            for group in range(groups):
                part = slice(group * ROWS, (group + 1) * ROWS)
                out_ref[at, rows, group * LANES : (group + 1) * LANES] = jnp.concatenate(
                    [one[part], two[part]], axis=0
                ).astype(out_ref.dtype)
            return carry

        lax.fori_loop(0, blocks // 2, pair, 0, unroll=unroll)

    deep = deep_ref[at]

    @pl.when((source <= top) & (deep == 0))
    def _():
        run(1, 8)

    @pl.when((source <= top) & (deep != 0))
    def _():
        run(index_ref.shape[2] // span, 1)


def spread(top, places, index, value, features):
    count, blocks, wide = index.shape
    block = min(32, blocks)
    deep = jnp.any(index[:, :, ROWS * SLOTS :] != FAR, axis=(1, 2)).astype(jnp.int32)
    tokens = blocks * ROWS
    return pl.pallas_call(
        functools.partial(spread_kernel, places),
        grid_spec=pltpu.PrefetchScalarGridSpec(
            num_scalar_prefetch=2,
            grid=(count, blocks // block),
            in_specs=[pl.BlockSpec((1, block, wide), lambda p, b, top, deep: (p, b, 0))] * 2,
            out_specs=WHOLE,
        ),
        out_shape=pltpu.VMEM((count, tokens, features), jnp.bfloat16),
        compiler_params=params(),
        cost_estimate=pl.CostEstimate(
            flops=count * 2 * tokens * features * 1000,
            bytes_accessed=count * tokens * features * 2,
            transcendentals=0,
        ),
    )(top, deep, index, value)


PLACES = (0, 2, 1, 3)


def layer_at(top, step):
    place = jnp.where(step == 0, 0, jnp.where(step == 1, PLACES[1], 2 * step - 3))
    return jnp.bitwise_xor(top, place)


def each_layer(top, value_refs, body, otherwise):
    own_ref, far_ref, near_ref = value_refs
    step = pl.program_id(0)
    used = layer_at(top, step) <= top

    @pl.when(step == 0)
    def _():
        body(own_ref.at[0], True)

    @pl.when((step == 1) & used)
    def _():
        body(far_ref.at[0], False)

    @pl.when((step > 1) & used)
    def _():
        body(near_ref.at[step - 2], False)

    if otherwise is not None:
        pl.when(jnp.logical_not(used))(otherwise)


def relative_block(me, place, bits):
    pattern = sum(((place >> j) & 1) << (bits - 1 - j) for j in range(bits))
    return jnp.bitwise_xor(me, pattern)


def rebuild_kernel(bits, top_ref, me_ref, own_ref, far_ref, near_ref, weight_ref, after_ref, *refs):
    keep_refs, send_refs, total_ref = refs[: len(refs) // 2], refs[len(refs) // 2 : -1], refs[-1]
    step = pl.program_id(0)

    def add(value_ref, first):
        product = jnp.dot(value_ref[...], weight_ref[0], preferred_element_type=jnp.float32)
        total_ref[...] = product if first else total_ref[...] + product

    each_layer(top_ref[0], (own_ref, far_ref, near_ref), add, None)

    @pl.when(step == pl.num_programs(0) - 1)
    def _():
        count = 1 << bits
        rows = total_ref.shape[0] // count
        half = count // 2
        width = keep_refs[0].shape[1]
        for place in range(count):
            start = pl.multiple_of(relative_block(me_ref[0], place, bits) * rows, rows)
            for piece in range(len(keep_refs)):
                block = total_ref[pl.ds(start, rows), piece * width : (piece + 1) * width]
                if place < half:
                    keep_refs[piece][place * rows : (place + 1) * rows, :] = block
                else:
                    at = (place - half) * rows
                    send_refs[piece][at : at + rows, :] = block.astype(jnp.bfloat16)


def rebuild(top, me, values, weight, start, width, piece, bits, after):
    layers = weight.shape[0]
    tokens, features = values[0].shape[1:]
    first = start // width
    pieces = width // piece
    shape = (tokens // 2, piece)
    outs = pl.pallas_call(
        functools.partial(rebuild_kernel, bits),
        grid_spec=pltpu.PrefetchScalarGridSpec(
            num_scalar_prefetch=2,
            grid=(layers,),
            in_specs=[
                WHOLE,
                WHOLE,
                WHOLE,
                pl.BlockSpec(
                    (1, features, width),
                    lambda s, top, me: (jnp.minimum(layer_at(top[0], s), top[0]), 0, first),
                ),
                pl.BlockSpec(memory_space=pl.ANY),
            ],
            out_specs=[pl.BlockSpec(shape, lambda s, top, me: (0, 0))] * (2 * pieces),
            scratch_shapes=[pltpu.VMEM((tokens, width), jnp.float32)],
        ),
        out_shape=[jax.ShapeDtypeStruct(shape, jnp.float32)] * pieces
        + [jax.ShapeDtypeStruct(shape, jnp.bfloat16)] * pieces,
        compiler_params=params(),
        cost_estimate=pl.CostEstimate(
            flops=2 * layers * tokens * features * width,
            bytes_accessed=2 * layers * features * (tokens + width),
            transcendentals=0,
        ),
    )(top, me, *map(in_vmem, values), weight, after)
    return list(zip(outs[:pieces], outs[pieces:]))


def grad_kernel(bits, pieces, top_ref, me_ref, own_ref, far_ref, near_ref, *refs):
    near_refs, far_refs = refs[:pieces], refs[pieces : 2 * pieces]
    out_ref, done_ref, error_ref = refs[-3:]
    source = pl.program_id(0)

    @pl.when(source == 0)
    def _():
        done_ref[...] = jnp.zeros_like(done_ref)
        count = 1 << bits
        rows = error_ref.shape[0] // count
        half = count // 2
        width = near_refs[0].shape[1]
        for place in range(count):
            start = pl.multiple_of(relative_block(me_ref[0], place, bits) * rows, rows)
            for piece in range(pieces):
                from_ref = near_refs[piece] if place < half else far_refs[piece]
                at = (place % half) * rows
                error_ref[pl.ds(start, rows), piece * width : (piece + 1) * width] = from_ref[
                    at : at + rows, :
                ]

    def multiply(value_ref, first):
        out_ref[0] = lax.dot_general(
            value_ref[...],
            error_ref[...],
            (((0,), (0,)), ((), ())),
            preferred_element_type=jnp.float32,
        ).astype(out_ref.dtype)

    def clear():
        out_ref[...] = jnp.zeros_like(out_ref)

    each_layer(top_ref[0], (own_ref, far_ref, near_ref), multiply, clear)


def gradients(top, me, values, halves, start, width, depth, bits, held, after):
    layers = sum(x.shape[0] for x in values)
    tokens, features = values[0].shape[1:]
    pieces = len(halves)
    piece = width // pieces
    first = start // width
    operands = [top, me, *map(in_vmem, values)] + [near for near, _ in halves] + [far for _, far in halves]
    in_specs = [WHOLE] * 3 + [pl.BlockSpec((tokens // 2, piece), lambda s, top, me: (0, 0))] * (2 * pieces)
    operands.append(after)
    in_specs.append(pl.BlockSpec(memory_space=pl.ANY))
    aliases = {}
    if held is not None:
        aliases = {len(operands): 0}
        operands.append(held)
        in_specs.append(pl.BlockSpec(memory_space=pl.ANY))
    return pl.pallas_call(
        functools.partial(grad_kernel, bits, pieces),
        grid_spec=pltpu.PrefetchScalarGridSpec(
            num_scalar_prefetch=2,
            grid=(layers,),
            in_specs=in_specs,
            out_specs=[
                pl.BlockSpec(
                    (1, features, width), lambda s, top, me: (layer_at(top[0], s), 0, first)
                ),
                pl.BlockSpec((ROWS, LANES), lambda s, top, me: (0, 0)),
            ],
            scratch_shapes=[pltpu.VMEM((tokens, width), jnp.bfloat16)],
        ),
        out_shape=[
            jax.ShapeDtypeStruct((layers, features, depth), jnp.bfloat16),
            jax.ShapeDtypeStruct((ROWS, LANES), jnp.float32),
        ],
        input_output_aliases=aliases,
        compiler_params=params(),
        cost_estimate=pl.CostEstimate(
            flops=2 * layers * tokens * features * width,
            bytes_accessed=2 * layers * features * (tokens + width),
            transcendentals=0,
        ),
    )(*operands)


def ordered(kernel, operands, specs, out_shape, after):
    def run(*refs):
        kernel(*refs[: len(operands)], *refs[len(operands) + 1 :])

    return pl.pallas_call(
        run,
        grid=(1,),
        in_specs=specs + [pl.BlockSpec(memory_space=pl.ANY)],
        out_specs=[pl.BlockSpec(x.shape, lambda i: (0, 0)) for x in out_shape],
        out_shape=out_shape,
        compiler_params=params(SMALL_BYTES),
        cost_estimate=pl.CostEstimate(flops=1000, bytes_accessed=1 << 20, transcendentals=0),
    )(*operands, after)


def columns_of(x, width, at):
    return pl.BlockSpec((x.shape[0], width), lambda i: (0, at))


def split(keep, arrived, parts, after):
    rows, width = keep.shape[0] // parts, keep.shape[1]

    def kernel(*refs):
        keep_ref, arrived_refs = refs[0], refs[1 : 1 + len(arrived)]
        for part, out_ref in enumerate(refs[1 + len(arrived) :]):
            at = slice(part * rows, (part + 1) * rows)
            total = keep_ref[at, :]
            for arrived_ref in arrived_refs:
                total = total + arrived_ref[at, :].astype(jnp.float32)
            out_ref[...] = total.astype(out_ref.dtype)

    operands = [keep, *arrived]
    outs = ordered(
        kernel,
        operands,
        [columns_of(x, width, 0) for x in operands],
        [jax.ShapeDtypeStruct((rows, width), jnp.float32)]
        + [jax.ShapeDtypeStruct((rows, width), jnp.bfloat16)] * (parts - 1),
        after,
    )
    return outs[0], outs[1:]


def error_of(keep, arrived, bias, target, at, after):
    rows, width = keep.shape

    def kernel(bias_ref, target_ref, keep_ref, *refs):
        total = keep_ref[...]
        for arrived_ref in refs[:-2]:
            total = total + arrived_ref[...].astype(jnp.float32)
        error = total + bias_ref[...] - target_ref[...].astype(jnp.float32)
        refs[-2][...] = error
        refs[-1][...] = error.astype(jnp.bfloat16)

    return ordered(
        kernel,
        [bias, target, keep, *arrived],
        [columns_of(bias, width, at), columns_of(target, width, at)]
        + [columns_of(x, width, 0) for x in [keep, *arrived]],
        [
            jax.ShapeDtypeStruct((rows, width), jnp.float32),
            jax.ShapeDtypeStruct((rows, width), jnp.bfloat16),
        ],
        after,
    )


def joined(arrays, after):
    rows, width = arrays[0].shape

    def kernel(*refs):
        for i, ref in enumerate(refs[:-1]):
            refs[-1][i * rows : (i + 1) * rows, :] = ref[...]

    return ordered(
        kernel,
        arrays,
        [columns_of(x, width, 0) for x in arrays],
        [jax.ShapeDtypeStruct((rows * len(arrays), width), jnp.bfloat16)],
        after,
    )[0]


def local(resid, enc_weight, enc_bias, active, dec_weight, dec_bias, target):
    features = enc_weight.shape[2]
    layers = dec_weight.shape[1]
    tokens, depth = resid.shape[1:]
    slots = active.shape[2]
    shards = lax.axis_size("feat")
    bits = shards.bit_length() - 1
    rows = tokens // shards
    feat_index = lax.axis_index("feat")
    pair_index = lax.axis_index("pair")
    top = pair_index.astype(jnp.int32).reshape(1)
    me = feat_index.astype(jnp.int32).reshape(1)

    offset = active[0] - feat_index * features
    inside = (offset >= 0) & (offset < features)
    slot_index = jnp.sort(jnp.where(inside, offset, FAR), axis=1)

    def folded(x):
        x = x.reshape(tokens // ROWS, ROWS, slots // SLOTS, SLOTS)
        return x.transpose(0, 2, 1, 3).reshape(tokens // ROWS, ROWS * slots)

    def across(x, step):
        return lax.ppermute(x, "pair", [(i, i ^ step) for i in range(layers)])

    far_step, near_step = layers // 2, 1
    own_index = folded(slot_index)
    own_short = own_index.astype(jnp.int16)
    far_short = across(own_short, far_step)
    own_value = folded(encode(resid[0], enc_weight[0], enc_bias, slot_index))
    far_value = across(own_value, far_step)

    def pack(*xs):
        return jnp.stack(xs)

    def wide(x):
        return x.astype(jnp.float32 if x.dtype == jnp.bfloat16 else jnp.int32)

    own = spread(top, (0,), own_index[None], wide(own_value)[None], features)
    near_short = across(pack(own_short, far_short), near_step)
    near_value = across(pack(own_value, far_value), near_step)
    far = spread(top, (far_step,), wide(far_short)[None], wide(far_value)[None], features)
    near = spread(
        top, (near_step, near_step + far_step), wide(near_short), wide(near_value), features
    )
    values = (own, far, near)

    def swap(parts, group):
        masks = [
            sum(((part >> j) & 1) << group[-1 - j] for j in range(len(group)))
            for part in range(1, 1 << len(group))
        ]
        return [
            lax.ppermute(x, "feat", [(i, i ^ mask) for i in range(shards)])
            for x, mask in zip(parts, masks)
        ]

    piece = min(PIECE, depth)
    count = depth // piece
    last = top
    grads = None
    state = [None] * count
    halves = [None] * count
    errors = [None] * count

    def rebuild_step(p):
        nonlocal last
        ((keep, last),) = rebuild(
            top, me, values, dec_weight[0], p * piece, piece, piece, bits, last
        )
        state[p] = (keep, swap([last], (0,)))

    def reduce_step(p, group):
        nonlocal last
        keep, sends = split(*state[p], 1 << len(group), last)
        last = sends[-1]
        state[p] = (keep, swap(sends, group))

    def error_step(p, group):
        nonlocal last
        errors[p], last = error_of(*state[p], dec_bias, target[0], p, last)
        state[p] = (last, swap([last] * ((1 << len(group)) - 1), group))

    def gather_step(p, group):
        nonlocal last
        last = joined([state[p][0], *state[p][1]], last)
        state[p] = (last, swap([last] * ((1 << len(group)) - 1), group))

    def grad_step(p):
        nonlocal grads, last
        near, (far,) = state[p]
        grads, last = gradients(
            top, me, values, [(near, far)], p * piece, piece, depth, bits, grads, last
        )

    def steps_of(p, down, up):
        steps = [functools.partial(reduce_step, p, group) for group in down]
        steps.append(functools.partial(error_step, p, up[0]))
        steps += [functools.partial(gather_step, p, group) for group in [*up[1:], (0,)]]
        return steps

    if count == len(GROUPS) and bits == 3:
        groups = GROUPS
        plan = PLAN
    else:
        ones = [(bit,) for bit in range(1, bits)]
        groups = [(ones, ones[::-1])] * count
        plan = [(p, REBUILD) for p in range(count)]
        plan += [(p, i) for i in range(2 * bits - 1) for p in range(count)]
        plan += [(p, GRADIENT) for p in range(count)]
    steps = [steps_of(p, *groups[p]) for p in range(count)]
    for p, i in plan:
        if i == REBUILD:
            rebuild_step(p)
        elif i == GRADIENT:
            grad_step(p)
        else:
            steps[p][i]()
    error = jnp.concatenate(errors, axis=1)
    return (error[None], grads[None])


def solution(mesh):
    in_specs = (
        P("pair", None, None),
        P("pair", None, "feat"),
        P("pair", "feat"),
        P("pair", None, None),
        P("pair", None, "feat", None),
        P("pair", None),
        P("pair", "feat", None),
    )
    out_specs = (P("pair", "feat", None), P("pair", None, "feat", None))
    return jax.shard_map(local, mesh=mesh, in_specs=in_specs, out_specs=out_specs, check_vma=False)
```

time: 234 us -> 204 us (0.87)
  waiting for transfers between devices: 61.3 us -> 28.3 us
  starting transfers between devices: 22.9 us -> 28 us
    ppermute x20 -> x24, waiting for transfers between devices: 61.3 us -> 28.3 us  [swap(): lax.ppermute(x, 'feat', [(i, i ^ mask) for i in range(shards)])]
    ppermute x20 -> x24, starting transfers between devices: 19.9 us -> 25 us  [swap(): lax.ppermute(x, 'feat', [(i, i ^ mask) for i in range(shards)])]
    pallas_call x4, Pallas kernels: 37.3 us -> 34 us  [the longest x1 18 us: encode(): pl.pallas_call(encode_kernel, grid=(steps + 1,), in_specs=[WHOLE, pl.Bloc...]
    pallas_call x2 -> x4, Pallas kernels: 43.6 us -> 45.4 us  [rebuild(): pl.pallas_call(functools.partial(rebuild_kernel, bits), grid_spec=pltpu.P...]
    pallas_call x2 -> x4, Pallas kernels: 45.4 us -> 45.5 us  [gradients(): pl.pallas_call(functools.partial(grad_kernel, bits, pieces), grid_spec=pl...]
  transfers between devices with their start and end apart: 24 -> 28, of which waited for: 17 -> 7; matrix products, arithmetic and copies ran while one was open for 2% -> 2% of each run, Pallas kernels for 24% -> 47%
where the time goes in v2:
time: 204 us; the launch traced here: 200 us
  Pallas kernels  126 us (62%)
  waiting for transfers between devices  28.3 us (14%)
  starting transfers between devices  28 us (14%)
  local copies, waits for them, and re-layouts  7.93 us (4%)
  other arithmetic  7.46 us (4%)
  between operations  2.68 us (1%)
    pallas_call x4, Pallas kernels, gradients(): pl.pallas_call(functools.partial(grad_kernel, bits, pieces), grid_spec=pl...  45.5 us
    pallas_call x4, Pallas kernels, rebuild(): pl.pallas_call(functools.partial(rebuild_kernel, bits), grid_spec=pltpu.P...  45.4 us
    ppermute x24, waiting for transfers between devices, swap(): lax.ppermute(x, 'feat', [(i, i ^ mask) for i in range(shards)])  28.3 us
    ppermute x24, starting transfers between devices, swap(): lax.ppermute(x, 'feat', [(i, i ^ mask) for i in range(shards)])  25 us
    pallas_call x1, Pallas kernels, encode(): pl.pallas_call(encode_kernel, grid=(steps + 1,), in_specs=[WHOLE, pl.Bloc...  18 us
    pallas_call x3, Pallas kernels, spread(): pl.pallas_call(functools.partial(spread_kernel, places), grid_spec=pltpu....  16 us
    unnamed x12, local copies, waits for them, and re-layouts  4.22 us
  transfers between devices with their start and end apart: 28, of which 7 were waited for; matrix products, arithmetic and copies ran while one was open for 2% of the time, Pallas kernels for 47%

profile of v2, /device:TPU:7, one launch (start us, length us, event | category | flops | bytes accessed | tf_op | source)
XLA Modules:
  0.0 200.2 jit_solution(12354642987334601546)
XLA Ops:
  1.7 3.7 %sort.14 = (s32[1024,64]{0,1:T(8,128)S(1)}, s32[1024,64]{0,1:T(8,128)}) sort(s32[1024,64]{0,1:T(8,128)S(1)} %bitcast_select_fusion, s32[1024,64]{0,1:T(8,128)S(1)} %iota.3), dimensions={1}, to_apply=%region_0.1 | sort | flops 1048576 | bytes 1048576 | tf_op jit(solution)/shard_map/jit(sort)/sort | solution.py:473
  7.4 2.2 %copy-done.4 = bf16[1,1024,2048]{2,1,0:T(8,128)(2,1)S(1)} copy-done((bf16[1,1024,2048]{2,1,0:T(8,128)(2,1)S(1)}, bf16[1,1024,2048]{2,1,0:T(8,128)(2,1)}, u32[]{:S(2)}) %copy-start.4) | copy-done | bytes 4194328
  9.6 18.0 %shard_map.86 = bf16[1024,64]{1,0:T(8,128)(2,1)} custom-call(bf16[1024,2048]{1,0:T(8,128)(2,1)S(1)} %bitcast.37, bf16[2048,2048]{1,0:T(8,128)(2,1)} %bitcast.50, f32[1,2048]{1,0:T(1,128)} %bias_ref.1, s32[1024,64]{1,0:T(8,128)} %copy-done.5), custom_call_target="tpu_custom_call" | custom-call | flops 8589934592 | bytes 12582912 | tf_op jit(solution)/shard_map/pallas_call | solution.py:94
  29.3 1.3 collective-permute-start.1
  32.2 3.9 %shard_map.87.own_ref = bf16[1,1024,2048]{2,1,0:T(8,128)(2,1)S(1)} custom-call(s32[1]{0:T(128)} %bitcast.1.top_ref.after_ref, s32[1]{0:T(128)} %bitcast.6.deep_ref, s32[1,128,512]{2,1,0:T(8,128)S(1)} %copy.29.index_ref, f32[1,128,512]{2,1,0:T(8,128)S(1)} %convert_element_type.48.value_ref), custom_call_target="tpu_custom_call" | custom-call | flops 4194304000 | bytes 4194304 | tf_op jit(solution)/shard_map/pallas_call | solution.py:182
  36.1 2.0 %copy-done = bf16[1,1024,2048]{2,1,0:T(8,128)(2,1)} copy-done((bf16[1,1024,2048]{2,1,0:T(8,128)(2,1)}, bf16[1,1024,2048]{2,1,0:T(8,128)(2,1)S(1)}, u32[]{:S(2)}) %copy-start) | copy-done | bytes 4194328
  41.0 3.9 %shard_map.88.far_ref = bf16[1,1024,2048]{2,1,0:T(8,128)(2,1)S(1)} custom-call(s32[1]{0:T(128)} %bitcast.1.top_ref.after_ref, s32[1]{0:T(128)} %bitcast.13.deep_ref, s32[1,128,512]{2,1,0:T(8,128)S(1)} %bitcast_convert_fusion.2.index_ref, f32[1,128,512]{2,1,0:T(8,128)S(1)} %bitcast_convert_fusion.1.value_ref), custom_call_target="tpu_custom_call" | custom-call | flops 4194304000 | bytes 4194304 | tf_op jit(solution)/shard_map/pallas_call | solution.py:182
  45.2 8.3 %shard_map.89.near_ref = bf16[2,1024,2048]{2,1,0:T(8,128)(2,1)S(1)} custom-call(s32[1]{0:T(128)} %bitcast.1.top_ref.after_ref, s32[2]{0:T(128)S(1)} %convert_element_type.55.deep_ref, s32[2,128,512]{2,1,0:T(8,128)S(1)} %convert_element_type.54.index_ref, f32[2,128,512]{2,1,0:T(8,128)S(1)} %convert_element_type.56.value_ref), custom_call_target="tpu_custom_call" | custom-call | flops 8388608000 | bytes 8388608 | tf_op jit(solution)/shard_map/pallas_call | solution.py:182
  53.4 11.2 %shard_map.90 = (f32[512,512]{1,0:T(8,128)S(1)}, bf16[512,512]{1,0:T(8,128)(2,1)S(1)}) custom-call(s32[1]{0:T(128)} %bitcast.1.top_ref.after_ref, s32[1]{0:T(128)} %bitcast.2.me_ref, bf16[1,1024,2048]{2,1,0:T(8,128)(2,1)S(1)} %copy-done.1, bf16[1,1024,2048]{2,1,0:T(8,128)(2,1)S(1)} %shard_map.88.far_ref, bf16[2,1024,2048]{2,1,0:T(8,128)(2,1)S(1)} %shard_map.89.near_ref, ...), custom_call_target="tpu_custom_call" | custom-call | flops 8589934592 | bytes 25165824 | tf_op jit(solution)/shard_map/pallas_call | solution.py:267
  65.0 11.7 %shard_map.91 = (f32[512,512]{1,0:T(8,128)S(1)}, bf16[512,512]{1,0:T(8,128)(2,1)S(1)}) custom-call(s32[1]{0:T(128)} %bitcast.1.top_ref.after_ref, s32[1]{0:T(128)} %bitcast.2.me_ref, bf16[1,1024,2048]{2,1,0:T(8,128)(2,1)S(1)} %copy-done.1, bf16[1,1024,2048]{2,1,0:T(8,128)(2,1)S(1)} %shard_map.88.far_ref, bf16[2,1024,2048]{2,1,0:T(8,128)(2,1)S(1)} %shard_map.89.near_ref, ...), custom_call_target="tpu_custom_call" | custom-call | flops 8589934592 | bytes 25165824 | tf_op jit(solution)/shard_map/pallas_call | solution.py:267
  78.1 1.4 collective-permute-start.5
  79.4 11.2 %shard_map.93 = (f32[512,512]{1,0:T(8,128)S(1)}, bf16[512,512]{1,0:T(8,128)(2,1)S(1)}) custom-call(s32[1]{0:T(128)} %bitcast.1.top_ref.after_ref, s32[1]{0:T(128)} %bitcast.2.me_ref, bf16[1,1024,2048]{2,1,0:T(8,128)(2,1)S(1)} %copy-done.1, bf16[1,1024,2048]{2,1,0:T(8,128)(2,1)S(1)} %shard_map.88.far_ref, bf16[2,1024,2048]{2,1,0:T(8,128)(2,1)S(1)} %shard_map.89.near_ref, ...), custom_call_target="tpu_custom_call" | custom-call | flops 8589934592 | bytes 25165824 | tf_op jit(solution)/shard_map/pallas_call | solution.py:267
  91.0 2.4 %collective-permute-start.6 = (bf16[128,512]{1,0:T(8,128)(2,1)S(1)}, bf16[128,512]{1,0:T(8,128)(2,1)S(1)}, u32[]{:S(2)}, u32[]{:S(2)}) collective-permute-start(bf16[128,512]{1,0:T(8,128)(2,1)S(1)} %get-tuple-element.51.refs_2_), channel_id=1, source_target_pairs={{0,16},{4,20},{8,24},{12,28},{16,0},{20,4},{24,8},{28,12},{1,17},{... | collective-permute-start | bytes 393224 | tf_op jit(solution)/shard_map/ppermute | solution.py:510
  93.8 11.3 %shard_map.96 = (f32[512,512]{1,0:T(8,128)S(1)}, bf16[512,512]{1,0:T(8,128)(2,1)S(1)}) custom-call(s32[1]{0:T(128)} %bitcast.1.top_ref.after_ref, s32[1]{0:T(128)} %bitcast.2.me_ref, bf16[1,1024,2048]{2,1,0:T(8,128)(2,1)S(1)} %copy-done.1, bf16[1,1024,2048]{2,1,0:T(8,128)(2,1)S(1)} %shard_map.88.far_ref, bf16[2,1024,2048]{2,1,0:T(8,128)(2,1)S(1)} %shard_map.89.near_ref, ...), custom_call_target="tpu_custom_call" | custom-call | flops 8589934592 | bytes 25165824 | tf_op jit(solution)/shard_map/pallas_call | solution.py:267
  106.7 1.4 collective-permute-start.12
  108.1 3.8 %collective-permute-done.10.refs_1_ = bf16[128,512]{1,0:T(8,128)(2,1)S(1)} collective-permute-done((bf16[128,512]{1,0:T(8,128)(2,1)S(1)}, bf16[128,512]{1,0:T(8,128)(2,1)S(1)}, u32[]{:S(2)}, u32[]{:S(2)}) %collective-permute-start.10) | collective-permute-done | bytes 131104 | tf_op jit(solution)/shard_map/ppermute | solution.py:510
  111.9 2.0 collective-permute-start.16
  114.1 6.2 %collective-permute-done.9.refs_3_ = bf16[128,512]{1,0:T(8,128)(2,1)S(1)} collective-permute-done((bf16[128,512]{1,0:T(8,128)(2,1)S(1)}, bf16[128,512]{1,0:T(8,128)(2,1)S(1)}, u32[]{:S(2)}, u32[]{:S(2)}) %collective-permute-start.9) | collective-permute-done | bytes 131104 | tf_op jit(solution)/shard_map/ppermute | solution.py:510
  120.4 2.9 %collective-permute-start.14 = (bf16[128,512]{1,0:T(8,128)(2,1)S(1)}, bf16[128,512]{1,0:T(8,128)(2,1)S(1)}, u32[]{:S(2)}, u32[]{:S(2)}) collective-permute-start(bf16[128,512]{1,0:T(8,128)(2,1)S(1)} %get-tuple-element.64.refs_2_.refs_0_), channel_id=1, source_target_pairs={{0,16},{4,20},{8,24},{12,28},{16,0},{20,4},{24,8},{28,12},{1,17},{... | collective-permute-start | bytes 393224 | tf_op jit(solution)/shard_map/ppermute | solution.py:510
  124.8 2.4 %collective-permute-start.13 = (bf16[128,512]{1,0:T(8,128)(2,1)S(1)}, bf16[128,512]{1,0:T(8,128)(2,1)S(1)}, u32[]{:S(2)}, u32[]{:S(2)}) collective-permute-start(bf16[128,512]{1,0:T(8,128)(2,1)S(1)} %get-tuple-element.66.refs_2_), channel_id=1, source_target_pairs={{0,16},{4,20},{8,24},{12,28},{16,0},{20,4},{24,8},{28,12},{1,17},{... | collective-permute-start | bytes 393224 | tf_op jit(solution)/shard_map/ppermute | solution.py:510
  127.2 2.8 %collective-permute-done.14.refs_1_ = bf16[128,512]{1,0:T(8,128)(2,1)S(1)} collective-permute-done((bf16[128,512]{1,0:T(8,128)(2,1)S(1)}, bf16[128,512]{1,0:T(8,128)(2,1)S(1)}, u32[]{:S(2)}, u32[]{:S(2)}) %collective-permute-start.14) | collective-permute-done | bytes 131104 | tf_op jit(solution)/shard_map/ppermute | solution.py:510
  130.6 4.5 %collective-permute-done.13.refs_3_ = bf16[128,512]{1,0:T(8,128)(2,1)S(1)} collective-permute-done((bf16[128,512]{1,0:T(8,128)(2,1)S(1)}, bf16[128,512]{1,0:T(8,128)(2,1)S(1)}, u32[]{:S(2)}, u32[]{:S(2)}) %collective-permute-start.13) | collective-permute-done | bytes 131104 | tf_op jit(solution)/shard_map/ppermute | solution.py:510
  135.2 2.9 %collective-permute-start.19 = (bf16[128,512]{1,0:T(8,128)(2,1)S(1)}, bf16[128,512]{1,0:T(8,128)(2,1)S(1)}, u32[]{:S(2)}, u32[]{:S(2)}) collective-permute-start(bf16[128,512]{1,0:T(8,128)(2,1)S(1)} %get-tuple-element.71.refs_2_.refs_0_), channel_id=1, source_target_pairs={{0,16},{4,20},{8,24},{12,28},{16,0},{20,4},{24,8},{28,12},{1,17},{... | collective-permute-start | bytes 393224 | tf_op jit(solution)/shard_map/ppermute | solution.py:510
  138.2 6.5 %collective-permute-done.20.refs_1_ = bf16[256,512]{1,0:T(8,128)(2,1)S(1)} collective-permute-done((bf16[256,512]{1,0:T(8,128)(2,1)S(1)}, bf16[256,512]{1,0:T(8,128)(2,1)S(1)}, u32[]{:S(2)}, u32[]{:S(2)}) %collective-permute-start.20) | collective-permute-done | bytes 262176 | tf_op jit(solution)/shard_map/ppermute | solution.py:510
  145.0 2.6 %collective-permute-done.19.refs_1_ = bf16[128,512]{1,0:T(8,128)(2,1)S(1)} collective-permute-done((bf16[128,512]{1,0:T(8,128)(2,1)S(1)}, bf16[128,512]{1,0:T(8,128)(2,1)S(1)}, u32[]{:S(2)}, u32[]{:S(2)}) %collective-permute-start.19) | collective-permute-done | bytes 131104 | tf_op jit(solution)/shard_map/ppermute | solution.py:510
  147.7 1.7 collective-permute-done.18.refs_3_
  150.6 11.2 %shard_map.111 = (bf16[4,2048,2048]{2,1,0:T(8,128)(2,1)}, f32[8,128]{1,0:T(8,128)S(1)}) custom-call(s32[1]{0:T(128)} %bitcast.1.top_ref.after_ref, s32[1]{0:T(128)} %bitcast.2.me_ref, bf16[1,1024,2048]{2,1,0:T(8,128)(2,1)S(1)} %copy-done.1, bf16[1,1024,2048]{2,1,0:T(8,128)(2,1)S(1)} %shard_map.88.far_ref, bf16[2,1024,2048]{2,1,0:T(8,128)(2,1)S(1)} %shard_map.89.near_ref, ...), custom_call_target="tpu_custom_call" | custom-call | flops 8589934592 | bytes 25165824 | tf_op jit(solution)/shard_map/pallas_call | solution.py:347
  162.2 1.8 collective-permute-start.24
  164.0 11.4 %shard_map.114 = (bf16[4,2048,2048]{2,1,0:T(8,128)(2,1)}, f32[8,128]{1,0:T(8,128)S(1)}) custom-call(s32[1]{0:T(128)} %bitcast.1.top_ref.after_ref, s32[1]{0:T(128)} %bitcast.2.me_ref, bf16[1,1024,2048]{2,1,0:T(8,128)(2,1)S(1)} %copy-done.1, bf16[1,1024,2048]{2,1,0:T(8,128)(2,1)S(1)} %shard_map.88.far_ref, ...), custom_call_target="tpu_custom_call", output_to_operand_aliasing={{0}: (8, {})} | custom-call | flops 8589934592 | bytes 25165824 | tf_op jit(solution)/shard_map/pallas_call | solution.py:347
  175.5 1.5 collective-permute-start.26
  177.0 11.4 %shard_map.116 = (bf16[4,2048,2048]{2,1,0:T(8,128)(2,1)}, f32[8,128]{1,0:T(8,128)S(1)}) custom-call(s32[1]{0:T(128)} %bitcast.1.top_ref.after_ref, s32[1]{0:T(128)} %bitcast.2.me_ref, bf16[1,1024,2048]{2,1,0:T(8,128)(2,1)S(1)} %copy-done.1, bf16[1,1024,2048]{2,1,0:T(8,128)(2,1)S(1)} %shard_map.88.far_ref, ...), custom_call_target="tpu_custom_call", output_to_operand_aliasing={{0}: (8, {})} | custom-call | flops 8589934592 | bytes 25165824 | tf_op jit(solution)/shard_map/pallas_call | solution.py:347
  188.4 11.5 %shard_map.117 = (bf16[4,2048,2048]{2,1,0:T(8,128)(2,1)}, f32[8,128]{1,0:T(8,128)}) custom-call(s32[1]{0:T(128)} %bitcast.1.top_ref.after_ref, s32[1]{0:T(128)} %bitcast.2.me_ref, bf16[1,1024,2048]{2,1,0:T(8,128)(2,1)S(1)} %copy-done.1, bf16[1,1024,2048]{2,1,0:T(8,128)(2,1)S(1)} %shard_map.88.far_ref, ...), custom_call_target="tpu_custom_call", output_to_operand_aliasing={{0}: (8, {})} | custom-call | flops 8589934592 | bytes 25165824 | tf_op jit(solution)/shard_map/pallas_call | solution.py:347
  (94 shorter events, 16.8 us)
Async XLA Ops:
  7.1 31.0 %collective-permute-start = (s16[128,512]{1,0:T(8,128)(2,1)S(1)}, s16[128,512]{1,0:T(8,128)(2,1)S(1)}, u32[]{:S(2)}, u32[]{:S(2)}) collective-permute-start(s16[128,512]{1,0:T(8,128)(2,1)S(1)} %copy.34), channel_id=1, source_target_pairs={{0,2},{1,3},{2,0},{3,1},{4,6},{5,7},{6,4},{7,5},{8,10},{9,11},{10,... | collective-permute-start | bytes 393224 | tf_op jit(solution)/shard_map/ppermute | solution.py:480
  7.4 2.2 %copy-start.4 = (bf16[1,1024,2048]{2,1,0:T(8,128)(2,1)S(1)}, bf16[1,1024,2048]{2,1,0:T(8,128)(2,1)}, u32[]{:S(2)}) copy-start(bf16[1,1024,2048]{2,1,0:T(8,128)(2,1)} %param.7) | copy-start | bytes 12582916
  29.3 10.1 %collective-permute-start.1 = (bf16[128,512]{1,0:T(8,128)(2,1)S(1)}, bf16[128,512]{1,0:T(8,128)(2,1)S(1)}, u32[]{:S(2)}, u32[]{:S(2)}) collective-permute-start(bf16[128,512]{1,0:T(8,128)(2,1)S(1)} %copy.36), channel_id=1, source_target_pairs={{0,2},{1,3},{2,0},{3,1},{4,6},{5,7},{6,4},{7,5},{8,10},{9,11},{10,... | collective-permute-start | bytes 393224 | tf_op jit(solution)/shard_map/ppermute | solution.py:480
  38.2 6.7 %collective-permute-start.2 = (s16[2,128,512]{2,1,0:T(8,128)(2,1)S(1)}, s16[2,128,512]{2,1,0:T(8,128)(2,1)S(1)}, u32[]{:S(2)}, u32[]{:S(2)}) collective-permute-start(s16[2,128,512]{2,1,0:T(8,128)(2,1)S(1)} %pad_add_fusion), channel_id=1, source_target_pairs={{0,1},{1,0},{2,3},{3,2},{4,5},{5,4},{6,7},{7,6},{8,9},{9,8},{10,11... | collective-permute-start | bytes 786440 | tf_op jit(solution)/shard_map/ppermute | solution.py:480
  39.5 5.6 %collective-permute-start.3 = (bf16[2,128,512]{2,1,0:T(8,128)(2,1)S(1)}, bf16[2,128,512]{2,1,0:T(8,128)(2,1)S(1)}, u32[]{:S(2)}, u32[]{:S(2)}) collective-permute-start(bf16[2,128,512]{2,1,0:T(8,128)(2,1)S(1)} %pad_maximum_fusion), channel_id=1, source_target_pairs={{0,1},{1,0},{2,3},{3,2},{4,5},{5,4},{6,7},{7,6},{8,9},{9,8},{10,11... | collective-permute-start | bytes 786440 | tf_op jit(solution)/shard_map/ppermute | solution.py:480
  40.9 12.5 %copy-start.1 = (bf16[1,1024,2048]{2,1,0:T(8,128)(2,1)S(1)}, bf16[1,1024,2048]{2,1,0:T(8,128)(2,1)}, u32[]{:S(2)}) copy-start(bf16[1,1024,2048]{2,1,0:T(8,128)(2,1)} %copy-done) | copy-start | bytes 12582916
  64.7 13.3 %collective-permute-start.4 = (bf16[512,512]{1,0:T(8,128)(2,1)S(1)}, bf16[512,512]{1,0:T(8,128)(2,1)S(1)}, u32[]{:S(2)}, u32[]{:S(2)}) collective-permute-start(bf16[512,512]{1,0:T(8,128)(2,1)S(1)} %get-tuple-element.45.after_ref), channel_id=1, source_target_pairs={{0,4},{4,0},{8,12},{12,8},{16,20},{20,16},{24,28},{28,24},{1,5},{5... | collective-permute-start | bytes 1572872 | tf_op jit(solution)/shard_map/ppermute | solution.py:510
  76.7 16.7 %collective-permute-start.7 = (bf16[512,512]{1,0:T(8,128)(2,1)S(1)}, bf16[512,512]{1,0:T(8,128)(2,1)S(1)}, u32[]{:S(2)}, u32[]{:S(2)}) collective-permute-start(bf16[512,512]{1,0:T(8,128)(2,1)S(1)} %get-tuple-element.46.refs_2_), channel_id=1, source_target_pairs={{0,4},{4,0},{8,12},{12,8},{16,20},{20,16},{24,28},{28,24},{1,5},{5... | collective-permute-start | bytes 1572872 | tf_op jit(solution)/shard_map/ppermute | solution.py:510
  78.1 12.9 %collective-permute-start.5 = (bf16[256,512]{1,0:T(8,128)(2,1)S(1)}, bf16[256,512]{1,0:T(8,128)(2,1)S(1)}, u32[]{:S(2)}, u32[]{:S(2)}) collective-permute-start(bf16[256,512]{1,0:T(8,128)(2,1)S(1)} %get-tuple-element.48.after_ref), channel_id=1, source_target_pairs={{0,8},{4,12},{8,0},{12,4},{16,24},{20,28},{24,16},{28,20},{1,9},{5... | collective-permute-start | bytes 786440 | tf_op jit(solution)/shard_map/ppermute | solution.py:510
  90.6 15.8 %copy-start.2 = (bf16[1,128,2048]{2,1,0:T(8,128)(2,1)S(1)}, bf16[1,128,2048]{2,1,0:T(8,128)(2,1)}, u32[]{:S(2)}) copy-start(bf16[1,128,2048]{2,1,0:T(8,128)(2,1)} %param.13) | copy-start | bytes 1572868
  90.6 15.7 %copy-start.3 = (f32[1,2048]{1,0:T(1,128)S(1)}, f32[1,2048]{1,0:T(1,128)}, u32[]{:S(2)}) copy-start(f32[1,2048]{1,0:T(1,128)} %refs_0_.7) | copy-start | bytes 24580
  90.6 16.0 %collective-permute-start.11 = (bf16[512,512]{1,0:T(8,128)(2,1)S(1)}, bf16[512,512]{1,0:T(8,128)(2,1)S(1)}, u32[]{:S(2)}, u32[]{:S(2)}) collective-permute-start(bf16[512,512]{1,0:T(8,128)(2,1)S(1)} %get-tuple-element.49.refs_2_), channel_id=1, source_target_pairs={{0,4},{4,0},{8,12},{12,8},{16,20},{20,16},{24,28},{28,24},{1,5},{5... | collective-permute-start | bytes 1572872 | tf_op jit(solution)/shard_map/ppermute | solution.py:510
  91.0 15.4 %collective-permute-start.6 = (bf16[128,512]{1,0:T(8,128)(2,1)S(1)}, bf16[128,512]{1,0:T(8,128)(2,1)S(1)}, u32[]{:S(2)}, u32[]{:S(2)}) collective-permute-start(bf16[128,512]{1,0:T(8,128)(2,1)S(1)} %get-tuple-element.51.refs_2_), channel_id=1, source_target_pairs={{0,16},{4,20},{8,24},{12,28},{16,0},{20,4},{24,8},{28,12},{1,17},{... | collective-permute-start | bytes 393224 | tf_op jit(solution)/shard_map/ppermute | solution.py:510
  93.5 13.0 %collective-permute-start.8 = (bf16[256,512]{1,0:T(8,128)(2,1)S(1)}, bf16[256,512]{1,0:T(8,128)(2,1)S(1)}, u32[]{:S(2)}, u32[]{:S(2)}) collective-permute-start(bf16[256,512]{1,0:T(8,128)(2,1)S(1)} %get-tuple-element.53.after_ref), channel_id=1, source_target_pairs={{0,8},{4,12},{8,0},{12,4},{16,24},{20,28},{24,16},{28,20},{1,9},{5... | collective-permute-start | bytes 786440 | tf_op jit(solution)/shard_map/ppermute | solution.py:510
  105.1 18.3 %collective-permute-start.15 = (bf16[512,512]{1,0:T(8,128)(2,1)S(1)}, bf16[512,512]{1,0:T(8,128)(2,1)S(1)}, u32[]{:S(2)}, u32[]{:S(2)}) collective-permute-start(bf16[512,512]{1,0:T(8,128)(2,1)S(1)} %get-tuple-element.54.refs_4_), channel_id=1, source_target_pairs={{0,4},{4,0},{8,12},{12,8},{16,20},{20,16},{24,28},{28,24},{1,5},{5... | collective-permute-start | bytes 1572872 | tf_op jit(solution)/shard_map/ppermute | solution.py:510
  106.4 5.4 %collective-permute-start.10 = (bf16[128,512]{1,0:T(8,128)(2,1)S(1)}, bf16[128,512]{1,0:T(8,128)(2,1)S(1)}, u32[]{:S(2)}, u32[]{:S(2)}) collective-permute-start(bf16[128,512]{1,0:T(8,128)(2,1)S(1)} %get-tuple-element.57.refs_2_.refs_0_), channel_id=1, source_target_pairs={{0,16},{4,20},{8,24},{12,28},{16,0},{20,4},{24,8},{28,12},{1,17},{... | collective-permute-start | bytes 393224 | tf_op jit(solution)/shard_map/ppermute | solution.py:510
  106.7 16.6 %collective-permute-start.12 = (bf16[256,512]{1,0:T(8,128)(2,1)S(1)}, bf16[256,512]{1,0:T(8,128)(2,1)S(1)}, u32[]{:S(2)}, u32[]{:S(2)}) collective-permute-start(bf16[256,512]{1,0:T(8,128)(2,1)S(1)} %get-tuple-element.61.refs_2_), channel_id=1, source_target_pairs={{0,8},{4,12},{8,0},{12,4},{16,24},{20,28},{24,16},{28,20},{1,9},{5... | collective-permute-start | bytes 786440 | tf_op jit(solution)/shard_map/ppermute | solution.py:510
  111.9 11.5 %collective-permute-start.16 = (bf16[256,512]{1,0:T(8,128)(2,1)S(1)}, bf16[256,512]{1,0:T(8,128)(2,1)S(1)}, u32[]{:S(2)}, u32[]{:S(2)}) collective-permute-start(bf16[256,512]{1,0:T(8,128)(2,1)S(1)} %shard_map.100.refs_4_.refs_0_), channel_id=1, source_target_pairs={{0,8},{4,12},{8,0},{12,4},{16,24},{20,28},{24,16},{28,20},{1,9},{5... | collective-permute-start | bytes 786440 | tf_op jit(solution)/shard_map/ppermute | solution.py:510
  113.8 6.5 %collective-permute-start.9 = (bf16[128,512]{1,0:T(8,128)(2,1)S(1)}, bf16[128,512]{1,0:T(8,128)(2,1)S(1)}, u32[]{:S(2)}, u32[]{:S(2)}) collective-permute-start(bf16[128,512]{1,0:T(8,128)(2,1)S(1)} %get-tuple-element.59.refs_2_), channel_id=1, source_target_pairs={{0,16},{4,20},{8,24},{12,28},{16,0},{20,4},{24,8},{28,12},{1,17},{... | collective-permute-start | bytes 393224 | tf_op jit(solution)/shard_map/ppermute | solution.py:510
  120.4 9.6 %collective-permute-start.14 = (bf16[128,512]{1,0:T(8,128)(2,1)S(1)}, bf16[128,512]{1,0:T(8,128)(2,1)S(1)}, u32[]{:S(2)}, u32[]{:S(2)}) collective-permute-start(bf16[128,512]{1,0:T(8,128)(2,1)S(1)} %get-tuple-element.64.refs_2_.refs_0_), channel_id=1, source_target_pairs={{0,16},{4,20},{8,24},{12,28},{16,0},{20,4},{24,8},{28,12},{1,17},{... | collective-permute-start | bytes 393224 | tf_op jit(solution)/shard_map/ppermute | solution.py:510
  123.5 14.5 %collective-permute-start.17 = (bf16[256,512]{1,0:T(8,128)(2,1)S(1)}, bf16[256,512]{1,0:T(8,128)(2,1)S(1)}, u32[]{:S(2)}, u32[]{:S(2)}) collective-permute-start(bf16[256,512]{1,0:T(8,128)(2,1)S(1)} %get-tuple-element.68.refs_2_), channel_id=1, source_target_pairs={{0,8},{4,12},{8,0},{12,4},{16,24},{20,28},{24,16},{28,20},{1,9},{5... | collective-permute-start | bytes 786440 | tf_op jit(solution)/shard_map/ppermute | solution.py:510
  124.6 26.1 %collective-permute-start.23 = (bf16[512,512]{1,0:T(8,128)(2,1)S(1)}, bf16[512,512]{1,0:T(8,128)(2,1)S(1)}, u32[]{:S(2)}, u32[]{:S(2)}) collective-permute-start(bf16[512,512]{1,0:T(8,128)(2,1)S(1)} %shard_map.103.refs_2_.refs_0_), channel_id=1, source_target_pairs={{0,4},{4,0},{8,12},{12,8},{16,20},{20,16},{24,28},{28,24},{1,5},{5... | collective-permute-start | bytes 1572872 | tf_op jit(solution)/shard_map/ppermute | solution.py:510
  124.8 10.3 %collective-permute-start.13 = (bf16[128,512]{1,0:T(8,128)(2,1)S(1)}, bf16[128,512]{1,0:T(8,128)(2,1)S(1)}, u32[]{:S(2)}, u32[]{:S(2)}) collective-permute-start(bf16[128,512]{1,0:T(8,128)(2,1)S(1)} %get-tuple-element.66.refs_2_), channel_id=1, source_target_pairs={{0,16},{4,20},{8,24},{12,28},{16,0},{20,4},{24,8},{28,12},{1,17},{... | collective-permute-start | bytes 393224 | tf_op jit(solution)/shard_map/ppermute | solution.py:510
  130.1 14.6 %collective-permute-start.20 = (bf16[256,512]{1,0:T(8,128)(2,1)S(1)}, bf16[256,512]{1,0:T(8,128)(2,1)S(1)}, u32[]{:S(2)}, u32[]{:S(2)}) collective-permute-start(bf16[256,512]{1,0:T(8,128)(2,1)S(1)} %shard_map.105.refs_4_.refs_0_), channel_id=1, source_target_pairs={{0,8},{4,12},{8,0},{12,4},{16,24},{20,28},{24,16},{28,20},{1,9},{5... | collective-permute-start | bytes 786440 | tf_op jit(solution)/shard_map/ppermute | solution.py:510
  135.2 12.5 %collective-permute-start.19 = (bf16[128,512]{1,0:T(8,128)(2,1)S(1)}, bf16[128,512]{1,0:T(8,128)(2,1)S(1)}, u32[]{:S(2)}, u32[]{:S(2)}) collective-permute-start(bf16[128,512]{1,0:T(8,128)(2,1)S(1)} %get-tuple-element.71.refs_2_.refs_0_), channel_id=1, source_target_pairs={{0,16},{4,20},{8,24},{12,28},{16,0},{20,4},{24,8},{28,12},{1,17},{... | collective-permute-start | bytes 393224 | tf_op jit(solution)/shard_map/ppermute | solution.py:510
  138.1 11.3 %collective-permute-start.18 = (bf16[128,512]{1,0:T(8,128)(2,1)S(1)}, bf16[128,512]{1,0:T(8,128)(2,1)S(1)}, u32[]{:S(2)}, u32[]{:S(2)}) collective-permute-start(bf16[128,512]{1,0:T(8,128)(2,1)S(1)} %get-tuple-element.73.refs_2_), channel_id=1, source_target_pairs={{0,16},{4,20},{8,24},{12,28},{16,0},{20,4},{24,8},{28,12},{1,17},{... | collective-permute-start | bytes 393224 | tf_op jit(solution)/shard_map/ppermute | solution.py:510
  144.7 19.3 %collective-permute-start.25 = (bf16[512,512]{1,0:T(8,128)(2,1)S(1)}, bf16[512,512]{1,0:T(8,128)(2,1)S(1)}, u32[]{:S(2)}, u32[]{:S(2)}) collective-permute-start(bf16[512,512]{1,0:T(8,128)(2,1)S(1)} %shard_map.108.refs_2_.refs_0_), channel_id=1, source_target_pairs={{0,4},{4,0},{8,12},{12,8},{16,20},{20,16},{24,28},{28,24},{1,5},{5... | collective-permute-start | bytes 1572872 | tf_op jit(solution)/shard_map/ppermute | solution.py:510
  147.7 14.2 %collective-permute-start.22 = (bf16[256,512]{1,0:T(8,128)(2,1)S(1)}, bf16[256,512]{1,0:T(8,128)(2,1)S(1)}, u32[]{:S(2)}, u32[]{:S(2)}) collective-permute-start(bf16[256,512]{1,0:T(8,128)(2,1)S(1)} %shard_map.109.refs_4_.refs_0_), channel_id=1, source_target_pairs={{0,8},{4,12},{8,0},{12,4},{16,24},{20,28},{24,16},{28,20},{1,9},{5... | collective-permute-start | bytes 786440 | tf_op jit(solution)/shard_map/ppermute | solution.py:510
  149.5 12.7 %collective-permute-start.21 = (bf16[128,512]{1,0:T(8,128)(2,1)S(1)}, bf16[128,512]{1,0:T(8,128)(2,1)S(1)}, u32[]{:S(2)}, u32[]{:S(2)}) collective-permute-start(bf16[128,512]{1,0:T(8,128)(2,1)S(1)} %get-tuple-element.75.refs_2_.refs_0_), channel_id=1, source_target_pairs={{0,16},{4,20},{8,24},{12,28},{16,0},{20,4},{24,8},{28,12},{1,17},{... | collective-permute-start | bytes 393224 | tf_op jit(solution)/shard_map/ppermute | solution.py:510
  161.9 15.1 %collective-permute-start.27 = (bf16[512,512]{1,0:T(8,128)(2,1)S(1)}, bf16[512,512]{1,0:T(8,128)(2,1)S(1)}, u32[]{:S(2)}, u32[]{:S(2)}) collective-permute-start(bf16[512,512]{1,0:T(8,128)(2,1)S(1)} %shard_map.112.refs_2_.refs_0_), channel_id=1, source_target_pairs={{0,4},{4,0},{8,12},{12,8},{16,20},{20,16},{24,28},{28,24},{1,5},{5... | collective-permute-start | bytes 1572872 | tf_op jit(solution)/shard_map/ppermute | solution.py:510
  162.2 13.2 %collective-permute-start.24 = (bf16[256,512]{1,0:T(8,128)(2,1)S(1)}, bf16[256,512]{1,0:T(8,128)(2,1)S(1)}, u32[]{:S(2)}, u32[]{:S(2)}) collective-permute-start(bf16[256,512]{1,0:T(8,128)(2,1)S(1)} %shard_map.113.refs_2_.refs_0_), channel_id=1, source_target_pairs={{0,8},{4,12},{8,0},{12,4},{16,24},{20,28},{24,16},{28,20},{1,9},{5... | collective-permute-start | bytes 786440 | tf_op jit(solution)/shard_map/ppermute | solution.py:510
  175.5 12.9 %collective-permute-start.26 = (bf16[512,512]{1,0:T(8,128)(2,1)S(1)}, bf16[512,512]{1,0:T(8,128)(2,1)S(1)}, u32[]{:S(2)}, u32[]{:S(2)}) collective-permute-start(bf16[512,512]{1,0:T(8,128)(2,1)S(1)} %shard_map.115.refs_2_.refs_0_), channel_id=1, source_target_pairs={{0,4},{4,0},{8,12},{12,8},{16,20},{20,16},{24,28},{28,24},{1,5},{5... | collective-permute-start | bytes 1572872 | tf_op jit(solution)/shard_map/ppermute | solution.py:510
  (2 other events, 3.9 us)

commit v3 on v2

--- a/solution.py
+++ b/solution.py
@@ -16,7 +16,7 @@
 SMALL_BYTES = 8 * 1024 * 1024
 PIECE = 512
 GROUPS = (
-    (((1,), (2,)), ((2,), (1,))),
+    (((1, 2),), ((2,), (1,))),
     (((1,), (2,)), ((2,), (1,))),
     (((1,), (2,)), ((2,), (1,))),
     (((1,), (2,)), ((2,), (1,))),
@@ -24,7 +24,7 @@
 REBUILD, GRADIENT = -1, -2
 PLAN = (
     (0, REBUILD), (1, REBUILD), (0, 0), (2, REBUILD), (0, 1), (1, 0), (3, REBUILD), (0, 2), (1, 1),
-    (2, 0), (0, 3), (1, 2), (2, 1), (0, 4), (3, 0), (1, 3), (2, 2), (3, 1), (1, 4), (2, 3), (3, 2),
+    (2, 0), (0, 3), (1, 2), (2, 1), (3, 0), (1, 3), (2, 2), (3, 1), (1, 4), (2, 3), (3, 2),
     (0, GRADIENT), (2, 4), (3, 3), (1, GRADIENT), (3, 4), (2, GRADIENT), (3, GRADIENT),
 )
 

time: 204 us -> 209 us (1.025)
  waiting for transfers between devices: 28.3 us -> 31.5 us
  starting transfers between devices: 28 us -> 30.5 us
    ppermute x24 -> x25, waiting for transfers between devices: 28.3 us -> 31.5 us  [swap(): lax.ppermute(x, 'feat', [(i, i ^ mask) for i in range(shards)])]
    ppermute x24 -> x25, starting transfers between devices: 25 us -> 27.5 us  [swap(): lax.ppermute(x, 'feat', [(i, i ^ mask) for i in range(shards)])]
  transfers between devices with their start and end apart: 28 -> 29, of which waited for: 7 -> 8; matrix products, arithmetic and copies ran while one was open for 2% -> 2% of each run, Pallas kernels for 47% -> 46%
where the time goes in v3:
time: 209 us; the launch traced here: 206 us
  Pallas kernels  126 us (60%)
  waiting for transfers between devices  31.5 us (15%)
  starting transfers between devices  30.5 us (15%)
  local copies, waits for them, and re-layouts  7.93 us (4%)
  other arithmetic  7.46 us (4%)
  between operations  2.71 us (1%)
    pallas_call x4, Pallas kernels, gradients(): pl.pallas_call(functools.partial(grad_kernel, bits, pieces), grid_spec=pl...  45.5 us
    pallas_call x4, Pallas kernels, rebuild(): pl.pallas_call(functools.partial(rebuild_kernel, bits), grid_spec=pltpu.P...  45.4 us
    ppermute x25, waiting for transfers between devices, swap(): lax.ppermute(x, 'feat', [(i, i ^ mask) for i in range(shards)])  31.5 us
    ppermute x25, starting transfers between devices, swap(): lax.ppermute(x, 'feat', [(i, i ^ mask) for i in range(shards)])  27.5 us
    pallas_call x1, Pallas kernels, encode(): pl.pallas_call(encode_kernel, grid=(steps + 1,), in_specs=[WHOLE, pl.Bloc...  18 us
    pallas_call x3, Pallas kernels, spread(): pl.pallas_call(functools.partial(spread_kernel, places), grid_spec=pltpu....  16 us
    unnamed x12, local copies, waits for them, and re-layouts  4.22 us
  transfers between devices with their start and end apart: 29, of which 8 were waited for; matrix products, arithmetic and copies ran while one was open for 2% of the time, Pallas kernels for 46%

profile of v3, /device:TPU:7, one launch (start us, length us, event | category | flops | bytes accessed | tf_op | source)
XLA Modules:
  0.0 206.0 jit_solution(4549332567069557177)
XLA Ops:
  1.7 3.7 %sort.14 = (s32[1024,64]{0,1:T(8,128)S(1)}, s32[1024,64]{0,1:T(8,128)}) sort(s32[1024,64]{0,1:T(8,128)S(1)} %bitcast_select_fusion, s32[1024,64]{0,1:T(8,128)S(1)} %iota.3), dimensions={1}, to_apply=%region_0.1 | sort | flops 1048576 | bytes 1048576 | tf_op jit(solution)/shard_map/jit(sort)/sort | solution.py:473
  7.4 2.2 %copy-done.4 = bf16[1,1024,2048]{2,1,0:T(8,128)(2,1)S(1)} copy-done((bf16[1,1024,2048]{2,1,0:T(8,128)(2,1)S(1)}, bf16[1,1024,2048]{2,1,0:T(8,128)(2,1)}, u32[]{:S(2)}) %copy-start.4) | copy-done | bytes 4194328
  9.6 18.0 %shard_map.86 = bf16[1024,64]{1,0:T(8,128)(2,1)} custom-call(bf16[1024,2048]{1,0:T(8,128)(2,1)S(1)} %bitcast.37, bf16[2048,2048]{1,0:T(8,128)(2,1)} %bitcast.50, f32[1,2048]{1,0:T(1,128)} %bias_ref.1, s32[1024,64]{1,0:T(8,128)} %copy-done.5), custom_call_target="tpu_custom_call" | custom-call | flops 8589934592 | bytes 12582912 | tf_op jit(solution)/shard_map/pallas_call | solution.py:94
  29.3 1.3 collective-permute-start.1
  32.2 3.9 %shard_map.87.own_ref = bf16[1,1024,2048]{2,1,0:T(8,128)(2,1)S(1)} custom-call(s32[1]{0:T(128)} %bitcast.1.top_ref.after_ref, s32[1]{0:T(128)} %bitcast.6.deep_ref, s32[1,128,512]{2,1,0:T(8,128)S(1)} %copy.29.index_ref, f32[1,128,512]{2,1,0:T(8,128)S(1)} %convert_element_type.48.value_ref), custom_call_target="tpu_custom_call" | custom-call | flops 4194304000 | bytes 4194304 | tf_op jit(solution)/shard_map/pallas_call | solution.py:182
  36.1 2.0 copy-done
  41.0 3.9 %shard_map.88.far_ref = bf16[1,1024,2048]{2,1,0:T(8,128)(2,1)S(1)} custom-call(s32[1]{0:T(128)} %bitcast.1.top_ref.after_ref, s32[1]{0:T(128)} %bitcast.13.deep_ref, s32[1,128,512]{2,1,0:T(8,128)S(1)} %bitcast_convert_fusion.2.index_ref, f32[1,128,512]{2,1,0:T(8,128)S(1)} %bitcast_convert_fusion.1.value_ref), custom_call_target="tpu_custom_call" | custom-call | flops 4194304000 | bytes 4194304 | tf_op jit(solution)/shard_map/pallas_call | solution.py:182
  45.2 8.3 %shard_map.89.near_ref = bf16[2,1024,2048]{2,1,0:T(8,128)(2,1)S(1)} custom-call(s32[1]{0:T(128)} %bitcast.1.top_ref.after_ref, s32[2]{0:T(128)S(1)} %convert_element_type.55.deep_ref, s32[2,128,512]{2,1,0:T(8,128)S(1)} %convert_element_type.54.index_ref, f32[2,128,512]{2,1,0:T(8,128)S(1)} %convert_element_type.56.value_ref), custom_call_target="tpu_custom_call" | custom-call | flops 8388608000 | bytes 8388608 | tf_op jit(solution)/shard_map/pallas_call | solution.py:182
  53.4 11.2 %shard_map.90 = (f32[512,512]{1,0:T(8,128)S(1)}, bf16[512,512]{1,0:T(8,128)(2,1)S(1)}) custom-call(s32[1]{0:T(128)} %bitcast.1.top_ref.after_ref, s32[1]{0:T(128)} %bitcast.2.me_ref, bf16[1,1024,2048]{2,1,0:T(8,128)(2,1)S(1)} %copy-done.1, bf16[1,1024,2048]{2,1,0:T(8,128)(2,1)S(1)} %shard_map.88.far_ref, bf16[2,1024,2048]{2,1,0:T(8,128)(2,1)S(1)} %shard_map.89.near_ref, ...), custom_call_target="tpu_custom_call" | custom-call | flops 8589934592 | bytes 25165824 | tf_op jit(solution)/shard_map/pallas_call | solution.py:267
  65.0 11.7 %shard_map.91 = (f32[512,512]{1,0:T(8,128)S(1)}, bf16[512,512]{1,0:T(8,128)(2,1)S(1)}) custom-call(s32[1]{0:T(128)} %bitcast.1.top_ref.after_ref, s32[1]{0:T(128)} %bitcast.2.me_ref, bf16[1,1024,2048]{2,1,0:T(8,128)(2,1)S(1)} %copy-done.1, bf16[1,1024,2048]{2,1,0:T(8,128)(2,1)S(1)} %shard_map.88.far_ref, bf16[2,1024,2048]{2,1,0:T(8,128)(2,1)S(1)} %shard_map.89.near_ref, ...), custom_call_target="tpu_custom_call" | custom-call | flops 8589934592 | bytes 25165824 | tf_op jit(solution)/shard_map/pallas_call | solution.py:267
  78.1 2.4 %collective-permute-start.5 = (bf16[128,512]{1,0:T(8,128)(2,1)S(1)}, bf16[128,512]{1,0:T(8,128)(2,1)S(1)}, u32[]{:S(2)}, u32[]{:S(2)}) collective-permute-start(bf16[128,512]{1,0:T(8,128)(2,1)S(1)} %get-tuple-element.48), channel_id=1, source_target_pairs={{0,16},{4,20},{8,24},{12,28},{16,0},{20,4},{24,8},{28,12},{1,17},{... | collective-permute-start | bytes 393224 | tf_op jit(solution)/shard_map/ppermute | solution.py:510
  81.7 11.2 %shard_map.93 = (f32[512,512]{1,0:T(8,128)S(1)}, bf16[512,512]{1,0:T(8,128)(2,1)S(1)}) custom-call(s32[1]{0:T(128)} %bitcast.1.top_ref.after_ref, s32[1]{0:T(128)} %bitcast.2.me_ref, bf16[1,1024,2048]{2,1,0:T(8,128)(2,1)S(1)} %copy-done.1, bf16[1,1024,2048]{2,1,0:T(8,128)(2,1)S(1)} %shard_map.88.far_ref, bf16[2,1024,2048]{2,1,0:T(8,128)(2,1)S(1)} %shard_map.89.near_ref, ...), custom_call_target="tpu_custom_call" | custom-call | flops 8589934592 | bytes 25165824 | tf_op jit(solution)/shard_map/pallas_call | solution.py:267
  93.9 11.3 %shard_map.96 = (f32[512,512]{1,0:T(8,128)S(1)}, bf16[512,512]{1,0:T(8,128)(2,1)S(1)}) custom-call(s32[1]{0:T(128)} %bitcast.1.top_ref.after_ref, s32[1]{0:T(128)} %bitcast.2.me_ref, bf16[1,1024,2048]{2,1,0:T(8,128)(2,1)S(1)} %copy-done.1, bf16[1,1024,2048]{2,1,0:T(8,128)(2,1)S(1)} %shard_map.88.far_ref, bf16[2,1024,2048]{2,1,0:T(8,128)(2,1)S(1)} %shard_map.89.near_ref, ...), custom_call_target="tpu_custom_call" | custom-call | flops 8589934592 | bytes 25165824 | tf_op jit(solution)/shard_map/pallas_call | solution.py:267
  106.5 3.2 %collective-permute-start.10 = (bf16[128,512]{1,0:T(8,128)(2,1)S(1)}, bf16[128,512]{1,0:T(8,128)(2,1)S(1)}, u32[]{:S(2)}, u32[]{:S(2)}) collective-permute-start(bf16[128,512]{1,0:T(8,128)(2,1)S(1)} %get-tuple-element.54.refs_2_.refs_0_), channel_id=1, source_target_pairs={{0,16},{4,20},{8,24},{12,28},{16,0},{20,4},{24,8},{28,12},{1,17},{... | collective-permute-start | bytes 393224 | tf_op jit(solution)/shard_map/ppermute | solution.py:510
  109.7 3.8 %collective-permute-done.10.refs_1_ = bf16[128,512]{1,0:T(8,128)(2,1)S(1)} collective-permute-done((bf16[128,512]{1,0:T(8,128)(2,1)S(1)}, bf16[128,512]{1,0:T(8,128)(2,1)S(1)}, u32[]{:S(2)}, u32[]{:S(2)}) %collective-permute-start.10) | collective-permute-done | bytes 131104 | tf_op jit(solution)/shard_map/ppermute | solution.py:510
  113.8 1.5 collective-permute-start.14
  115.3 1.6 collective-permute-start.11
  116.9 7.9 %collective-permute-done.12.refs_1_ = bf16[256,512]{1,0:T(8,128)(2,1)S(1)} collective-permute-done((bf16[256,512]{1,0:T(8,128)(2,1)S(1)}, bf16[256,512]{1,0:T(8,128)(2,1)S(1)}, u32[]{:S(2)}, u32[]{:S(2)}) %collective-permute-start.12) | collective-permute-done | bytes 262176 | tf_op jit(solution)/shard_map/ppermute | solution.py:510
  125.8 2.9 %collective-permute-start.16 = (bf16[128,512]{1,0:T(8,128)(2,1)S(1)}, bf16[128,512]{1,0:T(8,128)(2,1)S(1)}, u32[]{:S(2)}, u32[]{:S(2)}) collective-permute-start(bf16[128,512]{1,0:T(8,128)(2,1)S(1)} %get-tuple-element.64.refs_2_.refs_0_), channel_id=1, source_target_pairs={{0,16},{4,20},{8,24},{12,28},{16,0},{20,4},{24,8},{28,12},{1,17},{... | collective-permute-start | bytes 393224 | tf_op jit(solution)/shard_map/ppermute | solution.py:510
  128.9 2.3 %collective-permute-start.15 = (bf16[128,512]{1,0:T(8,128)(2,1)S(1)}, bf16[128,512]{1,0:T(8,128)(2,1)S(1)}, u32[]{:S(2)}, u32[]{:S(2)}) collective-permute-start(bf16[128,512]{1,0:T(8,128)(2,1)S(1)} %get-tuple-element.66.refs_2_), channel_id=1, source_target_pairs={{0,16},{4,20},{8,24},{12,28},{16,0},{20,4},{24,8},{28,12},{1,17},{... | collective-permute-start | bytes 393224 | tf_op jit(solution)/shard_map/ppermute | solution.py:510
  131.3 4.1 %collective-permute-done.16.refs_1_ = bf16[128,512]{1,0:T(8,128)(2,1)S(1)} collective-permute-done((bf16[128,512]{1,0:T(8,128)(2,1)S(1)}, bf16[128,512]{1,0:T(8,128)(2,1)S(1)}, u32[]{:S(2)}, u32[]{:S(2)}) %collective-permute-start.16) | collective-permute-done | bytes 131104 | tf_op jit(solution)/shard_map/ppermute | solution.py:510
  135.4 5.0 %collective-permute-done.15.refs_3_ = bf16[128,512]{1,0:T(8,128)(2,1)S(1)} collective-permute-done((bf16[128,512]{1,0:T(8,128)(2,1)S(1)}, bf16[128,512]{1,0:T(8,128)(2,1)S(1)}, u32[]{:S(2)}, u32[]{:S(2)}) %collective-permute-start.15) | collective-permute-done | bytes 131104 | tf_op jit(solution)/shard_map/ppermute | solution.py:510
  140.5 2.9 %collective-permute-start.20 = (bf16[128,512]{1,0:T(8,128)(2,1)S(1)}, bf16[128,512]{1,0:T(8,128)(2,1)S(1)}, u32[]{:S(2)}, u32[]{:S(2)}) collective-permute-start(bf16[128,512]{1,0:T(8,128)(2,1)S(1)} %get-tuple-element.71.refs_2_.refs_0_), channel_id=1, source_target_pairs={{0,16},{4,20},{8,24},{12,28},{16,0},{20,4},{24,8},{28,12},{1,17},{... | collective-permute-start | bytes 393224 | tf_op jit(solution)/shard_map/ppermute | solution.py:510
  143.5 6.0 %collective-permute-done.21.refs_1_ = bf16[256,512]{1,0:T(8,128)(2,1)S(1)} collective-permute-done((bf16[256,512]{1,0:T(8,128)(2,1)S(1)}, bf16[256,512]{1,0:T(8,128)(2,1)S(1)}, u32[]{:S(2)}, u32[]{:S(2)}) %collective-permute-start.21) | collective-permute-done | bytes 262176 | tf_op jit(solution)/shard_map/ppermute | solution.py:510
  149.9 2.6 %collective-permute-done.20.refs_1_ = bf16[128,512]{1,0:T(8,128)(2,1)S(1)} collective-permute-done((bf16[128,512]{1,0:T(8,128)(2,1)S(1)}, bf16[128,512]{1,0:T(8,128)(2,1)S(1)}, u32[]{:S(2)}, u32[]{:S(2)}) %collective-permute-start.20) | collective-permute-done | bytes 131104 | tf_op jit(solution)/shard_map/ppermute | solution.py:510
  152.6 1.6 collective-permute-done.19.refs_3_
  155.0 11.2 %shard_map.110 = (bf16[4,2048,2048]{2,1,0:T(8,128)(2,1)}, f32[8,128]{1,0:T(8,128)S(1)}) custom-call(s32[1]{0:T(128)} %bitcast.1.top_ref.after_ref, s32[1]{0:T(128)} %bitcast.2.me_ref, bf16[1,1024,2048]{2,1,0:T(8,128)(2,1)S(1)} %copy-done.1, bf16[1,1024,2048]{2,1,0:T(8,128)(2,1)S(1)} %shard_map.88.far_ref, bf16[2,1024,2048]{2,1,0:T(8,128)(2,1)S(1)} %shard_map.89.near_ref, ...), custom_call_target="tpu_custom_call" | custom-call | flops 8589934592 | bytes 25165824 | tf_op jit(solution)/shard_map/pallas_call | solution.py:347
  167.5 2.3 %collective-permute-start.25 = (bf16[256,512]{1,0:T(8,128)(2,1)S(1)}, bf16[256,512]{1,0:T(8,128)(2,1)S(1)}, u32[]{:S(2)}, u32[]{:S(2)}) collective-permute-start(bf16[256,512]{1,0:T(8,128)(2,1)S(1)} %shard_map.112.refs_2_.refs_0_), channel_id=1, source_target_pairs={{0,8},{4,12},{8,0},{12,4},{16,24},{20,28},{24,16},{28,20},{1,9},{5... | collective-permute-start | bytes 786440 | tf_op jit(solution)/shard_map/ppermute | solution.py:510
  169.8 11.4 %shard_map.113 = (bf16[4,2048,2048]{2,1,0:T(8,128)(2,1)}, f32[8,128]{1,0:T(8,128)S(1)}) custom-call(s32[1]{0:T(128)} %bitcast.1.top_ref.after_ref, s32[1]{0:T(128)} %bitcast.2.me_ref, bf16[1,1024,2048]{2,1,0:T(8,128)(2,1)S(1)} %copy-done.1, bf16[1,1024,2048]{2,1,0:T(8,128)(2,1)S(1)} %shard_map.88.far_ref, ...), custom_call_target="tpu_custom_call", output_to_operand_aliasing={{0}: (8, {})} | custom-call | flops 8589934592 | bytes 25165824 | tf_op jit(solution)/shard_map/pallas_call | solution.py:347
  181.3 1.5 collective-permute-start.27
  182.8 11.4 %shard_map.115 = (bf16[4,2048,2048]{2,1,0:T(8,128)(2,1)}, f32[8,128]{1,0:T(8,128)S(1)}) custom-call(s32[1]{0:T(128)} %bitcast.1.top_ref.after_ref, s32[1]{0:T(128)} %bitcast.2.me_ref, bf16[1,1024,2048]{2,1,0:T(8,128)(2,1)S(1)} %copy-done.1, bf16[1,1024,2048]{2,1,0:T(8,128)(2,1)S(1)} %shard_map.88.far_ref, ...), custom_call_target="tpu_custom_call", output_to_operand_aliasing={{0}: (8, {})} | custom-call | flops 8589934592 | bytes 25165824 | tf_op jit(solution)/shard_map/pallas_call | solution.py:347
  194.2 11.5 %shard_map.116 = (bf16[4,2048,2048]{2,1,0:T(8,128)(2,1)}, f32[8,128]{1,0:T(8,128)}) custom-call(s32[1]{0:T(128)} %bitcast.1.top_ref.after_ref, s32[1]{0:T(128)} %bitcast.2.me_ref, bf16[1,1024,2048]{2,1,0:T(8,128)(2,1)S(1)} %copy-done.1, bf16[1,1024,2048]{2,1,0:T(8,128)(2,1)S(1)} %shard_map.88.far_ref, ...), custom_call_target="tpu_custom_call", output_to_operand_aliasing={{0}: (8, {})} | custom-call | flops 8589934592 | bytes 25165824 | tf_op jit(solution)/shard_map/pallas_call | solution.py:347
  (95 shorter events, 17.8 us)
Async XLA Ops:
  7.1 31.0 %collective-permute-start = (s16[128,512]{1,0:T(8,128)(2,1)S(1)}, s16[128,512]{1,0:T(8,128)(2,1)S(1)}, u32[]{:S(2)}, u32[]{:S(2)}) collective-permute-start(s16[128,512]{1,0:T(8,128)(2,1)S(1)} %copy.34), channel_id=1, source_target_pairs={{0,2},{1,3},{2,0},{3,1},{4,6},{5,7},{6,4},{7,5},{8,10},{9,11},{10,... | collective-permute-start | bytes 393224 | tf_op jit(solution)/shard_map/ppermute | solution.py:480
  29.3 10.1 %collective-permute-start.1 = (bf16[128,512]{1,0:T(8,128)(2,1)S(1)}, bf16[128,512]{1,0:T(8,128)(2,1)S(1)}, u32[]{:S(2)}, u32[]{:S(2)}) collective-permute-start(bf16[128,512]{1,0:T(8,128)(2,1)S(1)} %copy.36), channel_id=1, source_target_pairs={{0,2},{1,3},{2,0},{3,1},{4,6},{5,7},{6,4},{7,5},{8,10},{9,11},{10,... | collective-permute-start | bytes 393224 | tf_op jit(solution)/shard_map/ppermute | solution.py:480
  38.2 6.7 %collective-permute-start.2 = (s16[2,128,512]{2,1,0:T(8,128)(2,1)S(1)}, s16[2,128,512]{2,1,0:T(8,128)(2,1)S(1)}, u32[]{:S(2)}, u32[]{:S(2)}) collective-permute-start(s16[2,128,512]{2,1,0:T(8,128)(2,1)S(1)} %pad_add_fusion), channel_id=1, source_target_pairs={{0,1},{1,0},{2,3},{3,2},{4,5},{5,4},{6,7},{7,6},{8,9},{9,8},{10,11... | collective-permute-start | bytes 786440 | tf_op jit(solution)/shard_map/ppermute | solution.py:480
  39.5 5.6 %collective-permute-start.3 = (bf16[2,128,512]{2,1,0:T(8,128)(2,1)S(1)}, bf16[2,128,512]{2,1,0:T(8,128)(2,1)S(1)}, u32[]{:S(2)}, u32[]{:S(2)}) collective-permute-start(bf16[2,128,512]{2,1,0:T(8,128)(2,1)S(1)} %pad_maximum_fusion), channel_id=1, source_target_pairs={{0,1},{1,0},{2,3},{3,2},{4,5},{5,4},{6,7},{7,6},{8,9},{9,8},{10,11... | collective-permute-start | bytes 786440 | tf_op jit(solution)/shard_map/ppermute | solution.py:480
  40.9 12.5 %copy-start.1 = (bf16[1,1024,2048]{2,1,0:T(8,128)(2,1)S(1)}, bf16[1,1024,2048]{2,1,0:T(8,128)(2,1)}, u32[]{:S(2)}) copy-start(bf16[1,1024,2048]{2,1,0:T(8,128)(2,1)} %copy-done) | copy-start | bytes 12582916
  64.7 13.3 %collective-permute-start.4 = (bf16[512,512]{1,0:T(8,128)(2,1)S(1)}, bf16[512,512]{1,0:T(8,128)(2,1)S(1)}, u32[]{:S(2)}, u32[]{:S(2)}) collective-permute-start(bf16[512,512]{1,0:T(8,128)(2,1)S(1)} %get-tuple-element.45.after_ref), channel_id=1, source_target_pairs={{0,4},{4,0},{8,12},{12,8},{16,20},{20,16},{24,28},{28,24},{1,5},{5... | collective-permute-start | bytes 1572872 | tf_op jit(solution)/shard_map/ppermute | solution.py:510
  76.7 16.6 %copy-start.2 = (bf16[1,128,2048]{2,1,0:T(8,128)(2,1)S(1)}, bf16[1,128,2048]{2,1,0:T(8,128)(2,1)}, u32[]{:S(2)}) copy-start(bf16[1,128,2048]{2,1,0:T(8,128)(2,1)} %param.13) | copy-start | bytes 1572868
  76.7 16.6 %copy-start.3 = (f32[1,2048]{1,0:T(1,128)S(1)}, f32[1,2048]{1,0:T(1,128)}, u32[]{:S(2)}) copy-start(f32[1,2048]{1,0:T(1,128)} %refs_0_.7) | copy-start | bytes 24580
  76.7 16.7 %collective-permute-start.8 = (bf16[512,512]{1,0:T(8,128)(2,1)S(1)}, bf16[512,512]{1,0:T(8,128)(2,1)S(1)}, u32[]{:S(2)}, u32[]{:S(2)}) collective-permute-start(bf16[512,512]{1,0:T(8,128)(2,1)S(1)} %get-tuple-element.46.refs_2_), channel_id=1, source_target_pairs={{0,4},{4,0},{8,12},{12,8},{16,20},{20,16},{24,28},{28,24},{1,5},{5... | collective-permute-start | bytes 1572872 | tf_op jit(solution)/shard_map/ppermute | solution.py:510
  78.1 15.2 %collective-permute-start.5 = (bf16[128,512]{1,0:T(8,128)(2,1)S(1)}, bf16[128,512]{1,0:T(8,128)(2,1)S(1)}, u32[]{:S(2)}, u32[]{:S(2)}) collective-permute-start(bf16[128,512]{1,0:T(8,128)(2,1)S(1)} %get-tuple-element.48), channel_id=1, source_target_pairs={{0,16},{4,20},{8,24},{12,28},{16,0},{20,4},{24,8},{28,12},{1,17},{... | collective-permute-start | bytes 393224 | tf_op jit(solution)/shard_map/ppermute | solution.py:510
  80.4 12.8 %collective-permute-start.6 = (bf16[128,512]{1,0:T(8,128)(2,1)S(1)}, bf16[128,512]{1,0:T(8,128)(2,1)S(1)}, u32[]{:S(2)}, u32[]{:S(2)}) collective-permute-start(bf16[128,512]{1,0:T(8,128)(2,1)S(1)} %get-tuple-element.49), channel_id=1, source_target_pairs={{0,8},{4,12},{8,0},{12,4},{16,24},{20,28},{24,16},{28,20},{1,9},{5... | collective-permute-start | bytes 393224 | tf_op jit(solution)/shard_map/ppermute | solution.py:510
  81.7 11.5 %collective-permute-start.7 = (bf16[128,512]{1,0:T(8,128)(2,1)S(1)}, bf16[128,512]{1,0:T(8,128)(2,1)S(1)}, u32[]{:S(2)}, u32[]{:S(2)}) collective-permute-start(bf16[128,512]{1,0:T(8,128)(2,1)S(1)} %get-tuple-element.50.after_ref), channel_id=1, source_target_pairs={{0,24},{4,28},{8,16},{12,20},{16,8},{20,12},{24,0},{28,4},{1,25},{... | collective-permute-start | bytes 393224 | tf_op jit(solution)/shard_map/ppermute | solution.py:510
  92.9 20.8 %collective-permute-start.13 = (bf16[512,512]{1,0:T(8,128)(2,1)S(1)}, bf16[512,512]{1,0:T(8,128)(2,1)S(1)}, u32[]{:S(2)}, u32[]{:S(2)}) collective-permute-start(bf16[512,512]{1,0:T(8,128)(2,1)S(1)} %get-tuple-element.51.refs_6_), channel_id=1, source_target_pairs={{0,4},{4,0},{8,12},{12,8},{16,20},{20,16},{24,28},{28,24},{1,5},{5... | collective-permute-start | bytes 1572872 | tf_op jit(solution)/shard_map/ppermute | solution.py:510
  93.5 20.1 %collective-permute-start.9 = (bf16[256,512]{1,0:T(8,128)(2,1)S(1)}, bf16[256,512]{1,0:T(8,128)(2,1)S(1)}, u32[]{:S(2)}, u32[]{:S(2)}) collective-permute-start(bf16[256,512]{1,0:T(8,128)(2,1)S(1)} %get-tuple-element.56.after_ref), channel_id=1, source_target_pairs={{0,8},{4,12},{8,0},{12,4},{16,24},{20,28},{24,16},{28,20},{1,9},{5... | collective-permute-start | bytes 786440 | tf_op jit(solution)/shard_map/ppermute | solution.py:510
  105.3 23.4 %collective-permute-start.17 = (bf16[512,512]{1,0:T(8,128)(2,1)S(1)}, bf16[512,512]{1,0:T(8,128)(2,1)S(1)}, u32[]{:S(2)}, u32[]{:S(2)}) collective-permute-start(bf16[512,512]{1,0:T(8,128)(2,1)S(1)} %get-tuple-element.57.refs_2_), channel_id=1, source_target_pairs={{0,4},{4,0},{8,12},{12,8},{16,20},{20,16},{24,28},{28,24},{1,5},{5... | collective-permute-start | bytes 1572872 | tf_op jit(solution)/shard_map/ppermute | solution.py:510
  106.5 7.0 %collective-permute-start.10 = (bf16[128,512]{1,0:T(8,128)(2,1)S(1)}, bf16[128,512]{1,0:T(8,128)(2,1)S(1)}, u32[]{:S(2)}, u32[]{:S(2)}) collective-permute-start(bf16[128,512]{1,0:T(8,128)(2,1)S(1)} %get-tuple-element.54.refs_2_.refs_0_), channel_id=1, source_target_pairs={{0,16},{4,20},{8,24},{12,28},{16,0},{20,4},{24,8},{28,12},{1,17},{... | collective-permute-start | bytes 393224 | tf_op jit(solution)/shard_map/ppermute | solution.py:510
  113.5 11.3 %collective-permute-start.12 = (bf16[256,512]{1,0:T(8,128)(2,1)S(1)}, bf16[256,512]{1,0:T(8,128)(2,1)S(1)}, u32[]{:S(2)}, u32[]{:S(2)}) collective-permute-start(bf16[256,512]{1,0:T(8,128)(2,1)S(1)} %shard_map.97.refs_2_.refs_0_), channel_id=1, source_target_pairs={{0,8},{4,12},{8,0},{12,4},{16,24},{20,28},{24,16},{28,20},{1,9},{5... | collective-permute-start | bytes 786440 | tf_op jit(solution)/shard_map/ppermute | solution.py:510
  113.8 14.8 %collective-permute-start.14 = (bf16[256,512]{1,0:T(8,128)(2,1)S(1)}, bf16[256,512]{1,0:T(8,128)(2,1)S(1)}, u32[]{:S(2)}, u32[]{:S(2)}) collective-permute-start(bf16[256,512]{1,0:T(8,128)(2,1)S(1)} %get-tuple-element.61.refs_2_), channel_id=1, source_target_pairs={{0,8},{4,12},{8,0},{12,4},{16,24},{20,28},{24,16},{28,20},{1,9},{5... | collective-permute-start | bytes 786440 | tf_op jit(solution)/shard_map/ppermute | solution.py:510
  115.3 10.4 %collective-permute-start.11 = (bf16[128,512]{1,0:T(8,128)(2,1)S(1)}, bf16[128,512]{1,0:T(8,128)(2,1)S(1)}, u32[]{:S(2)}, u32[]{:S(2)}) collective-permute-start(bf16[128,512]{1,0:T(8,128)(2,1)S(1)} %get-tuple-element.59.refs_2_), channel_id=1, source_target_pairs={{0,16},{4,20},{8,24},{12,28},{16,0},{20,4},{24,8},{28,12},{1,17},{... | collective-permute-start | bytes 393224 | tf_op jit(solution)/shard_map/ppermute | solution.py:510
  124.8 30.1 %collective-permute-start.24 = (bf16[512,512]{1,0:T(8,128)(2,1)S(1)}, bf16[512,512]{1,0:T(8,128)(2,1)S(1)}, u32[]{:S(2)}, u32[]{:S(2)}) collective-permute-start(bf16[512,512]{1,0:T(8,128)(2,1)S(1)} %shard_map.100.refs_4_.refs_0_), channel_id=1, source_target_pairs={{0,4},{4,0},{8,12},{12,8},{16,20},{20,16},{24,28},{28,24},{1,5},{5... | collective-permute-start | bytes 1572872 | tf_op jit(solution)/shard_map/ppermute | solution.py:510
  125.8 9.6 %collective-permute-start.16 = (bf16[128,512]{1,0:T(8,128)(2,1)S(1)}, bf16[128,512]{1,0:T(8,128)(2,1)S(1)}, u32[]{:S(2)}, u32[]{:S(2)}) collective-permute-start(bf16[128,512]{1,0:T(8,128)(2,1)S(1)} %get-tuple-element.64.refs_2_.refs_0_), channel_id=1, source_target_pairs={{0,16},{4,20},{8,24},{12,28},{16,0},{20,4},{24,8},{28,12},{1,17},{... | collective-permute-start | bytes 393224 | tf_op jit(solution)/shard_map/ppermute | solution.py:510
  128.8 14.5 %collective-permute-start.18 = (bf16[256,512]{1,0:T(8,128)(2,1)S(1)}, bf16[256,512]{1,0:T(8,128)(2,1)S(1)}, u32[]{:S(2)}, u32[]{:S(2)}) collective-permute-start(bf16[256,512]{1,0:T(8,128)(2,1)S(1)} %get-tuple-element.68.refs_2_), channel_id=1, source_target_pairs={{0,8},{4,12},{8,0},{12,4},{16,24},{20,28},{24,16},{28,20},{1,9},{5... | collective-permute-start | bytes 786440 | tf_op jit(solution)/shard_map/ppermute | solution.py:510
  128.9 11.5 %collective-permute-start.15 = (bf16[128,512]{1,0:T(8,128)(2,1)S(1)}, bf16[128,512]{1,0:T(8,128)(2,1)S(1)}, u32[]{:S(2)}, u32[]{:S(2)}) collective-permute-start(bf16[128,512]{1,0:T(8,128)(2,1)S(1)} %get-tuple-element.66.refs_2_), channel_id=1, source_target_pairs={{0,16},{4,20},{8,24},{12,28},{16,0},{20,4},{24,8},{28,12},{1,17},{... | collective-permute-start | bytes 393224 | tf_op jit(solution)/shard_map/ppermute | solution.py:510
  135.3 14.2 %collective-permute-start.21 = (bf16[256,512]{1,0:T(8,128)(2,1)S(1)}, bf16[256,512]{1,0:T(8,128)(2,1)S(1)}, u32[]{:S(2)}, u32[]{:S(2)}) collective-permute-start(bf16[256,512]{1,0:T(8,128)(2,1)S(1)} %shard_map.104.refs_4_.refs_0_), channel_id=1, source_target_pairs={{0,8},{4,12},{8,0},{12,4},{16,24},{20,28},{24,16},{28,20},{1,9},{5... | collective-permute-start | bytes 786440 | tf_op jit(solution)/shard_map/ppermute | solution.py:510
  140.5 12.0 %collective-permute-start.20 = (bf16[128,512]{1,0:T(8,128)(2,1)S(1)}, bf16[128,512]{1,0:T(8,128)(2,1)S(1)}, u32[]{:S(2)}, u32[]{:S(2)}) collective-permute-start(bf16[128,512]{1,0:T(8,128)(2,1)S(1)} %get-tuple-element.71.refs_2_.refs_0_), channel_id=1, source_target_pairs={{0,16},{4,20},{8,24},{12,28},{16,0},{20,4},{24,8},{28,12},{1,17},{... | collective-permute-start | bytes 393224 | tf_op jit(solution)/shard_map/ppermute | solution.py:510
  143.4 10.8 %collective-permute-start.19 = (bf16[128,512]{1,0:T(8,128)(2,1)S(1)}, bf16[128,512]{1,0:T(8,128)(2,1)S(1)}, u32[]{:S(2)}, u32[]{:S(2)}) collective-permute-start(bf16[128,512]{1,0:T(8,128)(2,1)S(1)} %get-tuple-element.73.refs_2_), channel_id=1, source_target_pairs={{0,16},{4,20},{8,24},{12,28},{16,0},{20,4},{24,8},{28,12},{1,17},{... | collective-permute-start | bytes 393224 | tf_op jit(solution)/shard_map/ppermute | solution.py:510
  149.6 20.2 %collective-permute-start.26 = (bf16[512,512]{1,0:T(8,128)(2,1)S(1)}, bf16[512,512]{1,0:T(8,128)(2,1)S(1)}, u32[]{:S(2)}, u32[]{:S(2)}) collective-permute-start(bf16[512,512]{1,0:T(8,128)(2,1)S(1)} %shard_map.107.refs_2_.refs_0_), channel_id=1, source_target_pairs={{0,4},{4,0},{8,12},{12,8},{16,20},{20,16},{24,28},{28,24},{1,5},{5... | collective-permute-start | bytes 1572872 | tf_op jit(solution)/shard_map/ppermute | solution.py:510
  152.5 14.7 %collective-permute-start.23 = (bf16[256,512]{1,0:T(8,128)(2,1)S(1)}, bf16[256,512]{1,0:T(8,128)(2,1)S(1)}, u32[]{:S(2)}, u32[]{:S(2)}) collective-permute-start(bf16[256,512]{1,0:T(8,128)(2,1)S(1)} %shard_map.108.refs_4_.refs_0_), channel_id=1, source_target_pairs={{0,8},{4,12},{8,0},{12,4},{16,24},{20,28},{24,16},{28,20},{1,9},{5... | collective-permute-start | bytes 786440 | tf_op jit(solution)/shard_map/ppermute | solution.py:510
  154.3 13.3 %collective-permute-start.22 = (bf16[128,512]{1,0:T(8,128)(2,1)S(1)}, bf16[128,512]{1,0:T(8,128)(2,1)S(1)}, u32[]{:S(2)}, u32[]{:S(2)}) collective-permute-start(bf16[128,512]{1,0:T(8,128)(2,1)S(1)} %get-tuple-element.75.refs_2_.refs_0_), channel_id=1, source_target_pairs={{0,16},{4,20},{8,24},{12,28},{16,0},{20,4},{24,8},{28,12},{1,17},{... | collective-permute-start | bytes 393224 | tf_op jit(solution)/shard_map/ppermute | solution.py:510
  167.2 15.5 %collective-permute-start.28 = (bf16[512,512]{1,0:T(8,128)(2,1)S(1)}, bf16[512,512]{1,0:T(8,128)(2,1)S(1)}, u32[]{:S(2)}, u32[]{:S(2)}) collective-permute-start(bf16[512,512]{1,0:T(8,128)(2,1)S(1)} %shard_map.111.refs_2_.refs_0_), channel_id=1, source_target_pairs={{0,4},{4,0},{8,12},{12,8},{16,20},{20,16},{24,28},{28,24},{1,5},{5... | collective-permute-start | bytes 1572872 | tf_op jit(solution)/shard_map/ppermute | solution.py:510
  167.5 13.7 %collective-permute-start.25 = (bf16[256,512]{1,0:T(8,128)(2,1)S(1)}, bf16[256,512]{1,0:T(8,128)(2,1)S(1)}, u32[]{:S(2)}, u32[]{:S(2)}) collective-permute-start(bf16[256,512]{1,0:T(8,128)(2,1)S(1)} %shard_map.112.refs_2_.refs_0_), channel_id=1, source_target_pairs={{0,8},{4,12},{8,0},{12,4},{16,24},{20,28},{24,16},{28,20},{1,9},{5... | collective-permute-start | bytes 786440 | tf_op jit(solution)/shard_map/ppermute | solution.py:510
  181.3 12.9 %collective-permute-start.27 = (bf16[512,512]{1,0:T(8,128)(2,1)S(1)}, bf16[512,512]{1,0:T(8,128)(2,1)S(1)}, u32[]{:S(2)}, u32[]{:S(2)}) collective-permute-start(bf16[512,512]{1,0:T(8,128)(2,1)S(1)} %shard_map.114.refs_2_.refs_0_), channel_id=1, source_target_pairs={{0,4},{4,0},{8,12},{12,8},{16,20},{20,16},{24,28},{28,24},{1,5},{5... | collective-permute-start | bytes 1572872 | tf_op jit(solution)/shard_map/ppermute | solution.py:510
  (3 other events, 6.1 us)

commit v4 on v2

--- a/solution.py
+++ b/solution.py
@@ -190,7 +190,7 @@
         out_shape=pltpu.VMEM((count, tokens, features), jnp.bfloat16),
         compiler_params=params(),
         cost_estimate=pl.CostEstimate(
-            flops=count * 2 * tokens * features * 1000,
+            flops=count * 2 * tokens * features * 32,
             bytes_accessed=count * tokens * features * 2,
             transcendentals=0,
         ),

time: 204 us -> 206 us (level)
  local copies, waits for them, and re-layouts: 7.93 us -> 10.1 us
    unnamed x12, local copies, waits for them, and re-layouts: 4.22 us -> 6.4 us
where the time goes in v4:
time: 206 us; the launch traced here: 202 us
  Pallas kernels  126 us (61%)
  waiting for transfers between devices  28.4 us (14%)
  starting transfers between devices  27.8 us (13%)
  local copies, waits for them, and re-layouts  10.1 us (5%)
  other arithmetic  7.46 us (4%)
  between operations  2.66 us (1%)
    pallas_call x4, Pallas kernels, gradients(): pl.pallas_call(functools.partial(grad_kernel, bits, pieces), grid_spec=pl...  45.5 us
    pallas_call x4, Pallas kernels, rebuild(): pl.pallas_call(functools.partial(rebuild_kernel, bits), grid_spec=pltpu.P...  45.4 us
    ppermute x24, waiting for transfers between devices, swap(): lax.ppermute(x, 'feat', [(i, i ^ mask) for i in range(shards)])  28.4 us
    ppermute x24, starting transfers between devices, swap(): lax.ppermute(x, 'feat', [(i, i ^ mask) for i in range(shards)])  24.8 us
    pallas_call x1, Pallas kernels, encode(): pl.pallas_call(encode_kernel, grid=(steps + 1,), in_specs=[WHOLE, pl.Bloc...  18 us
    pallas_call x3, Pallas kernels, spread(): pl.pallas_call(functools.partial(spread_kernel, places), grid_spec=pltpu....  16 us
    unnamed x12, local copies, waits for them, and re-layouts  6.4 us
  transfers between devices with their start and end apart: 28, of which 7 were waited for; matrix products, arithmetic and copies ran while one was open for 2% of the time, Pallas kernels for 47%

profile of v4, /device:TPU:7, one launch (start us, length us, event | category | flops | bytes accessed | tf_op | source)
XLA Modules:
  0.0 202.3 jit_solution(10929539272902358592)
XLA Ops:
  1.7 3.7 %sort.14 = (s32[1024,64]{0,1:T(8,128)S(1)}, s32[1024,64]{0,1:T(8,128)}) sort(s32[1024,64]{0,1:T(8,128)S(1)} %bitcast_select_fusion, s32[1024,64]{0,1:T(8,128)S(1)} %iota.3), dimensions={1}, to_apply=%region_0.1 | sort | flops 1048576 | bytes 1048576 | tf_op jit(solution)/shard_map/jit(sort)/sort | solution.py:473
  7.4 2.2 %copy-done.4 = bf16[1,1024,2048]{2,1,0:T(8,128)(2,1)S(1)} copy-done((bf16[1,1024,2048]{2,1,0:T(8,128)(2,1)S(1)}, bf16[1,1024,2048]{2,1,0:T(8,128)(2,1)}, u32[]{:S(2)}) %copy-start.4) | copy-done | bytes 4194328
  9.6 18.0 %shard_map.86 = bf16[1024,64]{1,0:T(8,128)(2,1)} custom-call(bf16[1024,2048]{1,0:T(8,128)(2,1)S(1)} %bitcast.37, bf16[2048,2048]{1,0:T(8,128)(2,1)} %bitcast.50, f32[1,2048]{1,0:T(1,128)} %bias_ref.1, s32[1024,64]{1,0:T(8,128)} %copy-done.5), custom_call_target="tpu_custom_call" | custom-call | flops 8589934592 | bytes 12582912 | tf_op jit(solution)/shard_map/pallas_call | solution.py:94
  32.3 3.9 %shard_map.87.own_ref = bf16[1,1024,2048]{2,1,0:T(8,128)(2,1)S(1)} custom-call(s32[1]{0:T(128)} %bitcast.1.top_ref.after_ref, s32[1]{0:T(128)} %bitcast.6.deep_ref, s32[1,128,512]{2,1,0:T(8,128)S(1)} %copy.29.index_ref, f32[1,128,512]{2,1,0:T(8,128)S(1)} %convert_element_type.48.value_ref), custom_call_target="tpu_custom_call" | custom-call | flops 134217728 | bytes 4194304 | tf_op jit(solution)/shard_map/pallas_call | solution.py:182
  36.1 2.0 copy-done
  41.0 3.9 %shard_map.88.far_ref = bf16[1,1024,2048]{2,1,0:T(8,128)(2,1)S(1)} custom-call(s32[1]{0:T(128)} %bitcast.1.top_ref.after_ref, s32[1]{0:T(128)} %bitcast.13.deep_ref, s32[1,128,512]{2,1,0:T(8,128)S(1)} %bitcast_convert_fusion.2.index_ref, f32[1,128,512]{2,1,0:T(8,128)S(1)} %bitcast_convert_fusion.1.value_ref), custom_call_target="tpu_custom_call" | custom-call | flops 134217728 | bytes 4194304 | tf_op jit(solution)/shard_map/pallas_call | solution.py:182
  45.2 8.3 %shard_map.89.near_ref = bf16[2,1024,2048]{2,1,0:T(8,128)(2,1)S(1)} custom-call(s32[1]{0:T(128)} %bitcast.1.top_ref.after_ref, s32[2]{0:T(128)S(1)} %convert_element_type.55.deep_ref, s32[2,128,512]{2,1,0:T(8,128)S(1)} %convert_element_type.54.index_ref, f32[2,128,512]{2,1,0:T(8,128)S(1)} %convert_element_type.56.value_ref), custom_call_target="tpu_custom_call" | custom-call | flops 268435456 | bytes 8388608 | tf_op jit(solution)/shard_map/pallas_call | solution.py:182
  53.4 2.2 %copy-done.1 = bf16[1,1024,2048]{2,1,0:T(8,128)(2,1)S(1)} copy-done((bf16[1,1024,2048]{2,1,0:T(8,128)(2,1)S(1)}, bf16[1,1024,2048]{2,1,0:T(8,128)(2,1)}, u32[]{:S(2)}) %copy-start.1) | copy-done | bytes 4194328
  55.6 11.2 %shard_map.90 = (f32[512,512]{1,0:T(8,128)S(1)}, bf16[512,512]{1,0:T(8,128)(2,1)S(1)}) custom-call(s32[1]{0:T(128)} %bitcast.1.top_ref.after_ref, s32[1]{0:T(128)} %bitcast.2.me_ref, bf16[1,1024,2048]{2,1,0:T(8,128)(2,1)S(1)} %copy-done.1, bf16[1,1024,2048]{2,1,0:T(8,128)(2,1)S(1)} %shard_map.88.far_ref, bf16[2,1024,2048]{2,1,0:T(8,128)(2,1)S(1)} %shard_map.89.near_ref, ...), custom_call_target="tpu_custom_call" | custom-call | flops 8589934592 | bytes 25165824 | tf_op jit(solution)/shard_map/pallas_call | solution.py:267
  67.1 11.7 %shard_map.91 = (f32[512,512]{1,0:T(8,128)S(1)}, bf16[512,512]{1,0:T(8,128)(2,1)S(1)}) custom-call(s32[1]{0:T(128)} %bitcast.1.top_ref.after_ref, s32[1]{0:T(128)} %bitcast.2.me_ref, bf16[1,1024,2048]{2,1,0:T(8,128)(2,1)S(1)} %copy-done.1, bf16[1,1024,2048]{2,1,0:T(8,128)(2,1)S(1)} %shard_map.88.far_ref, bf16[2,1024,2048]{2,1,0:T(8,128)(2,1)S(1)} %shard_map.89.near_ref, ...), custom_call_target="tpu_custom_call" | custom-call | flops 8589934592 | bytes 25165824 | tf_op jit(solution)/shard_map/pallas_call | solution.py:267
  80.2 1.4 collective-permute-start.5
  81.6 11.2 %shard_map.93 = (f32[512,512]{1,0:T(8,128)S(1)}, bf16[512,512]{1,0:T(8,128)(2,1)S(1)}) custom-call(s32[1]{0:T(128)} %bitcast.1.top_ref.after_ref, s32[1]{0:T(128)} %bitcast.2.me_ref, bf16[1,1024,2048]{2,1,0:T(8,128)(2,1)S(1)} %copy-done.1, bf16[1,1024,2048]{2,1,0:T(8,128)(2,1)S(1)} %shard_map.88.far_ref, bf16[2,1024,2048]{2,1,0:T(8,128)(2,1)S(1)} %shard_map.89.near_ref, ...), custom_call_target="tpu_custom_call" | custom-call | flops 8589934592 | bytes 25165824 | tf_op jit(solution)/shard_map/pallas_call | solution.py:267
  93.2 2.4 %collective-permute-start.6 = (bf16[128,512]{1,0:T(8,128)(2,1)S(1)}, bf16[128,512]{1,0:T(8,128)(2,1)S(1)}, u32[]{:S(2)}, u32[]{:S(2)}) collective-permute-start(bf16[128,512]{1,0:T(8,128)(2,1)S(1)} %get-tuple-element.51.refs_2_), channel_id=1, source_target_pairs={{0,16},{4,20},{8,24},{12,28},{16,0},{20,4},{24,8},{28,12},{1,17},{... | collective-permute-start | bytes 393224 | tf_op jit(solution)/shard_map/ppermute | solution.py:510
  95.9 11.3 %shard_map.96 = (f32[512,512]{1,0:T(8,128)S(1)}, bf16[512,512]{1,0:T(8,128)(2,1)S(1)}) custom-call(s32[1]{0:T(128)} %bitcast.1.top_ref.after_ref, s32[1]{0:T(128)} %bitcast.2.me_ref, bf16[1,1024,2048]{2,1,0:T(8,128)(2,1)S(1)} %copy-done.1, bf16[1,1024,2048]{2,1,0:T(8,128)(2,1)S(1)} %shard_map.88.far_ref, bf16[2,1024,2048]{2,1,0:T(8,128)(2,1)S(1)} %shard_map.89.near_ref, ...), custom_call_target="tpu_custom_call" | custom-call | flops 8589934592 | bytes 25165824 | tf_op jit(solution)/shard_map/pallas_call | solution.py:267
  108.9 1.4 collective-permute-start.12
  110.2 3.8 %collective-permute-done.10.refs_1_ = bf16[128,512]{1,0:T(8,128)(2,1)S(1)} collective-permute-done((bf16[128,512]{1,0:T(8,128)(2,1)S(1)}, bf16[128,512]{1,0:T(8,128)(2,1)S(1)}, u32[]{:S(2)}, u32[]{:S(2)}) %collective-permute-start.10) | collective-permute-done | bytes 131104 | tf_op jit(solution)/shard_map/ppermute | solution.py:510
  114.1 1.9 collective-permute-start.16
  116.3 6.2 %collective-permute-done.9.refs_3_ = bf16[128,512]{1,0:T(8,128)(2,1)S(1)} collective-permute-done((bf16[128,512]{1,0:T(8,128)(2,1)S(1)}, bf16[128,512]{1,0:T(8,128)(2,1)S(1)}, u32[]{:S(2)}, u32[]{:S(2)}) %collective-permute-start.9) | collective-permute-done | bytes 131104 | tf_op jit(solution)/shard_map/ppermute | solution.py:510
  122.6 2.9 %collective-permute-start.14 = (bf16[128,512]{1,0:T(8,128)(2,1)S(1)}, bf16[128,512]{1,0:T(8,128)(2,1)S(1)}, u32[]{:S(2)}, u32[]{:S(2)}) collective-permute-start(bf16[128,512]{1,0:T(8,128)(2,1)S(1)} %get-tuple-element.64.refs_2_.refs_0_), channel_id=1, source_target_pairs={{0,16},{4,20},{8,24},{12,28},{16,0},{20,4},{24,8},{28,12},{1,17},{... | collective-permute-start | bytes 393224 | tf_op jit(solution)/shard_map/ppermute | solution.py:510
  127.0 2.4 %collective-permute-start.13 = (bf16[128,512]{1,0:T(8,128)(2,1)S(1)}, bf16[128,512]{1,0:T(8,128)(2,1)S(1)}, u32[]{:S(2)}, u32[]{:S(2)}) collective-permute-start(bf16[128,512]{1,0:T(8,128)(2,1)S(1)} %get-tuple-element.66.refs_2_), channel_id=1, source_target_pairs={{0,16},{4,20},{8,24},{12,28},{16,0},{20,4},{24,8},{28,12},{1,17},{... | collective-permute-start | bytes 393224 | tf_op jit(solution)/shard_map/ppermute | solution.py:510
  129.4 2.8 %collective-permute-done.14.refs_1_ = bf16[128,512]{1,0:T(8,128)(2,1)S(1)} collective-permute-done((bf16[128,512]{1,0:T(8,128)(2,1)S(1)}, bf16[128,512]{1,0:T(8,128)(2,1)S(1)}, u32[]{:S(2)}, u32[]{:S(2)}) %collective-permute-start.14) | collective-permute-done | bytes 131104 | tf_op jit(solution)/shard_map/ppermute | solution.py:510
  132.7 4.5 %collective-permute-done.13.refs_3_ = bf16[128,512]{1,0:T(8,128)(2,1)S(1)} collective-permute-done((bf16[128,512]{1,0:T(8,128)(2,1)S(1)}, bf16[128,512]{1,0:T(8,128)(2,1)S(1)}, u32[]{:S(2)}, u32[]{:S(2)}) %collective-permute-start.13) | collective-permute-done | bytes 131104 | tf_op jit(solution)/shard_map/ppermute | solution.py:510
  137.3 2.9 %collective-permute-start.19 = (bf16[128,512]{1,0:T(8,128)(2,1)S(1)}, bf16[128,512]{1,0:T(8,128)(2,1)S(1)}, u32[]{:S(2)}, u32[]{:S(2)}) collective-permute-start(bf16[128,512]{1,0:T(8,128)(2,1)S(1)} %get-tuple-element.71.refs_2_.refs_0_), channel_id=1, source_target_pairs={{0,16},{4,20},{8,24},{12,28},{16,0},{20,4},{24,8},{28,12},{1,17},{... | collective-permute-start | bytes 393224 | tf_op jit(solution)/shard_map/ppermute | solution.py:510
  140.3 6.5 %collective-permute-done.20.refs_1_ = bf16[256,512]{1,0:T(8,128)(2,1)S(1)} collective-permute-done((bf16[256,512]{1,0:T(8,128)(2,1)S(1)}, bf16[256,512]{1,0:T(8,128)(2,1)S(1)}, u32[]{:S(2)}, u32[]{:S(2)}) %collective-permute-start.20) | collective-permute-done | bytes 262176 | tf_op jit(solution)/shard_map/ppermute | solution.py:510
  147.0 2.7 %collective-permute-done.19.refs_1_ = bf16[128,512]{1,0:T(8,128)(2,1)S(1)} collective-permute-done((bf16[128,512]{1,0:T(8,128)(2,1)S(1)}, bf16[128,512]{1,0:T(8,128)(2,1)S(1)}, u32[]{:S(2)}, u32[]{:S(2)}) %collective-permute-start.19) | collective-permute-done | bytes 131104 | tf_op jit(solution)/shard_map/ppermute | solution.py:510
  149.9 1.7 collective-permute-done.18.refs_3_
  152.8 11.2 %shard_map.111 = (bf16[4,2048,2048]{2,1,0:T(8,128)(2,1)}, f32[8,128]{1,0:T(8,128)S(1)}) custom-call(s32[1]{0:T(128)} %bitcast.1.top_ref.after_ref, s32[1]{0:T(128)} %bitcast.2.me_ref, bf16[1,1024,2048]{2,1,0:T(8,128)(2,1)S(1)} %copy-done.1, bf16[1,1024,2048]{2,1,0:T(8,128)(2,1)S(1)} %shard_map.88.far_ref, bf16[2,1024,2048]{2,1,0:T(8,128)(2,1)S(1)} %shard_map.89.near_ref, ...), custom_call_target="tpu_custom_call" | custom-call | flops 8589934592 | bytes 25165824 | tf_op jit(solution)/shard_map/pallas_call | solution.py:347
  164.4 1.8 collective-permute-start.24
  166.1 11.4 %shard_map.114 = (bf16[4,2048,2048]{2,1,0:T(8,128)(2,1)}, f32[8,128]{1,0:T(8,128)S(1)}) custom-call(s32[1]{0:T(128)} %bitcast.1.top_ref.after_ref, s32[1]{0:T(128)} %bitcast.2.me_ref, bf16[1,1024,2048]{2,1,0:T(8,128)(2,1)S(1)} %copy-done.1, bf16[1,1024,2048]{2,1,0:T(8,128)(2,1)S(1)} %shard_map.88.far_ref, ...), custom_call_target="tpu_custom_call", output_to_operand_aliasing={{0}: (8, {})} | custom-call | flops 8589934592 | bytes 25165824 | tf_op jit(solution)/shard_map/pallas_call | solution.py:347
  177.6 1.5 collective-permute-start.26
  179.1 11.4 %shard_map.116 = (bf16[4,2048,2048]{2,1,0:T(8,128)(2,1)}, f32[8,128]{1,0:T(8,128)S(1)}) custom-call(s32[1]{0:T(128)} %bitcast.1.top_ref.after_ref, s32[1]{0:T(128)} %bitcast.2.me_ref, bf16[1,1024,2048]{2,1,0:T(8,128)(2,1)S(1)} %copy-done.1, bf16[1,1024,2048]{2,1,0:T(8,128)(2,1)S(1)} %shard_map.88.far_ref, ...), custom_call_target="tpu_custom_call", output_to_operand_aliasing={{0}: (8, {})} | custom-call | flops 8589934592 | bytes 25165824 | tf_op jit(solution)/shard_map/pallas_call | solution.py:347
  190.5 11.5 %shard_map.117 = (bf16[4,2048,2048]{2,1,0:T(8,128)(2,1)}, f32[8,128]{1,0:T(8,128)}) custom-call(s32[1]{0:T(128)} %bitcast.1.top_ref.after_ref, s32[1]{0:T(128)} %bitcast.2.me_ref, bf16[1,1024,2048]{2,1,0:T(8,128)(2,1)S(1)} %copy-done.1, bf16[1,1024,2048]{2,1,0:T(8,128)(2,1)S(1)} %shard_map.88.far_ref, ...), custom_call_target="tpu_custom_call", output_to_operand_aliasing={{0}: (8, {})} | custom-call | flops 8589934592 | bytes 25165824 | tf_op jit(solution)/shard_map/pallas_call | solution.py:347
  (94 shorter events, 18.0 us)
Async XLA Ops:
  7.1 31.0 %collective-permute-start = (s16[128,512]{1,0:T(8,128)(2,1)S(1)}, s16[128,512]{1,0:T(8,128)(2,1)S(1)}, u32[]{:S(2)}, u32[]{:S(2)}) collective-permute-start(s16[128,512]{1,0:T(8,128)(2,1)S(1)} %copy.34), channel_id=1, source_target_pairs={{0,2},{1,3},{2,0},{3,1},{4,6},{5,7},{6,4},{7,5},{8,10},{9,11},{10,... | collective-permute-start | bytes 393224 | tf_op jit(solution)/shard_map/ppermute | solution.py:480
  7.4 2.2 %copy-start.4 = (bf16[1,1024,2048]{2,1,0:T(8,128)(2,1)S(1)}, bf16[1,1024,2048]{2,1,0:T(8,128)(2,1)}, u32[]{:S(2)}) copy-start(bf16[1,1024,2048]{2,1,0:T(8,128)(2,1)} %param.7) | copy-start | bytes 12582916
  29.3 10.1 %collective-permute-start.1 = (bf16[128,512]{1,0:T(8,128)(2,1)S(1)}, bf16[128,512]{1,0:T(8,128)(2,1)S(1)}, u32[]{:S(2)}, u32[]{:S(2)}) collective-permute-start(bf16[128,512]{1,0:T(8,128)(2,1)S(1)} %copy.36), channel_id=1, source_target_pairs={{0,2},{1,3},{2,0},{3,1},{4,6},{5,7},{6,4},{7,5},{8,10},{9,11},{10,... | collective-permute-start | bytes 393224 | tf_op jit(solution)/shard_map/ppermute | solution.py:480
  38.2 6.7 %collective-permute-start.2 = (s16[2,128,512]{2,1,0:T(8,128)(2,1)S(1)}, s16[2,128,512]{2,1,0:T(8,128)(2,1)S(1)}, u32[]{:S(2)}, u32[]{:S(2)}) collective-permute-start(s16[2,128,512]{2,1,0:T(8,128)(2,1)S(1)} %pad_add_fusion), channel_id=1, source_target_pairs={{0,1},{1,0},{2,3},{3,2},{4,5},{5,4},{6,7},{7,6},{8,9},{9,8},{10,11... | collective-permute-start | bytes 786440 | tf_op jit(solution)/shard_map/ppermute | solution.py:480
  39.5 5.6 %collective-permute-start.3 = (bf16[2,128,512]{2,1,0:T(8,128)(2,1)S(1)}, bf16[2,128,512]{2,1,0:T(8,128)(2,1)S(1)}, u32[]{:S(2)}, u32[]{:S(2)}) collective-permute-start(bf16[2,128,512]{2,1,0:T(8,128)(2,1)S(1)} %pad_maximum_fusion), channel_id=1, source_target_pairs={{0,1},{1,0},{2,3},{3,2},{4,5},{5,4},{6,7},{7,6},{8,9},{9,8},{10,11... | collective-permute-start | bytes 786440 | tf_op jit(solution)/shard_map/ppermute | solution.py:480
  53.4 2.2 %copy-start.1 = (bf16[1,1024,2048]{2,1,0:T(8,128)(2,1)S(1)}, bf16[1,1024,2048]{2,1,0:T(8,128)(2,1)}, u32[]{:S(2)}) copy-start(bf16[1,1024,2048]{2,1,0:T(8,128)(2,1)} %copy-done) | copy-start | bytes 12582916
  66.8 13.3 %collective-permute-start.4 = (bf16[512,512]{1,0:T(8,128)(2,1)S(1)}, bf16[512,512]{1,0:T(8,128)(2,1)S(1)}, u32[]{:S(2)}, u32[]{:S(2)}) collective-permute-start(bf16[512,512]{1,0:T(8,128)(2,1)S(1)} %get-tuple-element.45.after_ref), channel_id=1, source_target_pairs={{0,4},{4,0},{8,12},{12,8},{16,20},{20,16},{24,28},{28,24},{1,5},{5... | collective-permute-start | bytes 1572872 | tf_op jit(solution)/shard_map/ppermute | solution.py:510
  78.8 16.7 %collective-permute-start.7 = (bf16[512,512]{1,0:T(8,128)(2,1)S(1)}, bf16[512,512]{1,0:T(8,128)(2,1)S(1)}, u32[]{:S(2)}, u32[]{:S(2)}) collective-permute-start(bf16[512,512]{1,0:T(8,128)(2,1)S(1)} %get-tuple-element.46.refs_2_), channel_id=1, source_target_pairs={{0,4},{4,0},{8,12},{12,8},{16,20},{20,16},{24,28},{28,24},{1,5},{5... | collective-permute-start | bytes 1572872 | tf_op jit(solution)/shard_map/ppermute | solution.py:510
  80.2 12.9 %collective-permute-start.5 = (bf16[256,512]{1,0:T(8,128)(2,1)S(1)}, bf16[256,512]{1,0:T(8,128)(2,1)S(1)}, u32[]{:S(2)}, u32[]{:S(2)}) collective-permute-start(bf16[256,512]{1,0:T(8,128)(2,1)S(1)} %get-tuple-element.48.after_ref), channel_id=1, source_target_pairs={{0,8},{4,12},{8,0},{12,4},{16,24},{20,28},{24,16},{28,20},{1,9},{5... | collective-permute-start | bytes 786440 | tf_op jit(solution)/shard_map/ppermute | solution.py:510
  92.8 15.8 %copy-start.2 = (bf16[1,128,2048]{2,1,0:T(8,128)(2,1)S(1)}, bf16[1,128,2048]{2,1,0:T(8,128)(2,1)}, u32[]{:S(2)}) copy-start(bf16[1,128,2048]{2,1,0:T(8,128)(2,1)} %param.13) | copy-start | bytes 1572868
  92.8 15.8 %copy-start.3 = (f32[1,2048]{1,0:T(1,128)S(1)}, f32[1,2048]{1,0:T(1,128)}, u32[]{:S(2)}) copy-start(f32[1,2048]{1,0:T(1,128)} %refs_0_.7) | copy-start | bytes 24580
  92.8 16.0 %collective-permute-start.11 = (bf16[512,512]{1,0:T(8,128)(2,1)S(1)}, bf16[512,512]{1,0:T(8,128)(2,1)S(1)}, u32[]{:S(2)}, u32[]{:S(2)}) collective-permute-start(bf16[512,512]{1,0:T(8,128)(2,1)S(1)} %get-tuple-element.49.refs_2_), channel_id=1, source_target_pairs={{0,4},{4,0},{8,12},{12,8},{16,20},{20,16},{24,28},{28,24},{1,5},{5... | collective-permute-start | bytes 1572872 | tf_op jit(solution)/shard_map/ppermute | solution.py:510
  93.2 15.4 %collective-permute-start.6 = (bf16[128,512]{1,0:T(8,128)(2,1)S(1)}, bf16[128,512]{1,0:T(8,128)(2,1)S(1)}, u32[]{:S(2)}, u32[]{:S(2)}) collective-permute-start(bf16[128,512]{1,0:T(8,128)(2,1)S(1)} %get-tuple-element.51.refs_2_), channel_id=1, source_target_pairs={{0,16},{4,20},{8,24},{12,28},{16,0},{20,4},{24,8},{28,12},{1,17},{... | collective-permute-start | bytes 393224 | tf_op jit(solution)/shard_map/ppermute | solution.py:510
  95.7 13.1 %collective-permute-start.8 = (bf16[256,512]{1,0:T(8,128)(2,1)S(1)}, bf16[256,512]{1,0:T(8,128)(2,1)S(1)}, u32[]{:S(2)}, u32[]{:S(2)}) collective-permute-start(bf16[256,512]{1,0:T(8,128)(2,1)S(1)} %get-tuple-element.53.after_ref), channel_id=1, source_target_pairs={{0,8},{4,12},{8,0},{12,4},{16,24},{20,28},{24,16},{28,20},{1,9},{5... | collective-permute-start | bytes 786440 | tf_op jit(solution)/shard_map/ppermute | solution.py:510
  107.2 18.3 %collective-permute-start.15 = (bf16[512,512]{1,0:T(8,128)(2,1)S(1)}, bf16[512,512]{1,0:T(8,128)(2,1)S(1)}, u32[]{:S(2)}, u32[]{:S(2)}) collective-permute-start(bf16[512,512]{1,0:T(8,128)(2,1)S(1)} %get-tuple-element.54.refs_4_), channel_id=1, source_target_pairs={{0,4},{4,0},{8,12},{12,8},{16,20},{20,16},{24,28},{28,24},{1,5},{5... | collective-permute-start | bytes 1572872 | tf_op jit(solution)/shard_map/ppermute | solution.py:510
  108.6 5.4 %collective-permute-start.10 = (bf16[128,512]{1,0:T(8,128)(2,1)S(1)}, bf16[128,512]{1,0:T(8,128)(2,1)S(1)}, u32[]{:S(2)}, u32[]{:S(2)}) collective-permute-start(bf16[128,512]{1,0:T(8,128)(2,1)S(1)} %get-tuple-element.57.refs_2_.refs_0_), channel_id=1, source_target_pairs={{0,16},{4,20},{8,24},{12,28},{16,0},{20,4},{24,8},{28,12},{1,17},{... | collective-permute-start | bytes 393224 | tf_op jit(solution)/shard_map/ppermute | solution.py:510
  108.9 16.6 %collective-permute-start.12 = (bf16[256,512]{1,0:T(8,128)(2,1)S(1)}, bf16[256,512]{1,0:T(8,128)(2,1)S(1)}, u32[]{:S(2)}, u32[]{:S(2)}) collective-permute-start(bf16[256,512]{1,0:T(8,128)(2,1)S(1)} %get-tuple-element.61.refs_2_), channel_id=1, source_target_pairs={{0,8},{4,12},{8,0},{12,4},{16,24},{20,28},{24,16},{28,20},{1,9},{5... | collective-permute-start | bytes 786440 | tf_op jit(solution)/shard_map/ppermute | solution.py:510
  114.1 11.5 %collective-permute-start.16 = (bf16[256,512]{1,0:T(8,128)(2,1)S(1)}, bf16[256,512]{1,0:T(8,128)(2,1)S(1)}, u32[]{:S(2)}, u32[]{:S(2)}) collective-permute-start(bf16[256,512]{1,0:T(8,128)(2,1)S(1)} %shard_map.100.refs_4_.refs_0_), channel_id=1, source_target_pairs={{0,8},{4,12},{8,0},{12,4},{16,24},{20,28},{24,16},{28,20},{1,9},{5... | collective-permute-start | bytes 786440 | tf_op jit(solution)/shard_map/ppermute | solution.py:510
  116.0 6.5 %collective-permute-start.9 = (bf16[128,512]{1,0:T(8,128)(2,1)S(1)}, bf16[128,512]{1,0:T(8,128)(2,1)S(1)}, u32[]{:S(2)}, u32[]{:S(2)}) collective-permute-start(bf16[128,512]{1,0:T(8,128)(2,1)S(1)} %get-tuple-element.59.refs_2_), channel_id=1, source_target_pairs={{0,16},{4,20},{8,24},{12,28},{16,0},{20,4},{24,8},{28,12},{1,17},{... | collective-permute-start | bytes 393224 | tf_op jit(solution)/shard_map/ppermute | solution.py:510
  122.6 9.6 %collective-permute-start.14 = (bf16[128,512]{1,0:T(8,128)(2,1)S(1)}, bf16[128,512]{1,0:T(8,128)(2,1)S(1)}, u32[]{:S(2)}, u32[]{:S(2)}) collective-permute-start(bf16[128,512]{1,0:T(8,128)(2,1)S(1)} %get-tuple-element.64.refs_2_.refs_0_), channel_id=1, source_target_pairs={{0,16},{4,20},{8,24},{12,28},{16,0},{20,4},{24,8},{28,12},{1,17},{... | collective-permute-start | bytes 393224 | tf_op jit(solution)/shard_map/ppermute | solution.py:510
  125.7 14.5 %collective-permute-start.17 = (bf16[256,512]{1,0:T(8,128)(2,1)S(1)}, bf16[256,512]{1,0:T(8,128)(2,1)S(1)}, u32[]{:S(2)}, u32[]{:S(2)}) collective-permute-start(bf16[256,512]{1,0:T(8,128)(2,1)S(1)} %get-tuple-element.68.refs_2_), channel_id=1, source_target_pairs={{0,8},{4,12},{8,0},{12,4},{16,24},{20,28},{24,16},{28,20},{1,9},{5... | collective-permute-start | bytes 786440 | tf_op jit(solution)/shard_map/ppermute | solution.py:510
  126.7 26.0 %collective-permute-start.23 = (bf16[512,512]{1,0:T(8,128)(2,1)S(1)}, bf16[512,512]{1,0:T(8,128)(2,1)S(1)}, u32[]{:S(2)}, u32[]{:S(2)}) collective-permute-start(bf16[512,512]{1,0:T(8,128)(2,1)S(1)} %shard_map.103.refs_2_.refs_0_), channel_id=1, source_target_pairs={{0,4},{4,0},{8,12},{12,8},{16,20},{20,16},{24,28},{28,24},{1,5},{5... | collective-permute-start | bytes 1572872 | tf_op jit(solution)/shard_map/ppermute | solution.py:510
  127.0 10.2 %collective-permute-start.13 = (bf16[128,512]{1,0:T(8,128)(2,1)S(1)}, bf16[128,512]{1,0:T(8,128)(2,1)S(1)}, u32[]{:S(2)}, u32[]{:S(2)}) collective-permute-start(bf16[128,512]{1,0:T(8,128)(2,1)S(1)} %get-tuple-element.66.refs_2_), channel_id=1, source_target_pairs={{0,16},{4,20},{8,24},{12,28},{16,0},{20,4},{24,8},{28,12},{1,17},{... | collective-permute-start | bytes 393224 | tf_op jit(solution)/shard_map/ppermute | solution.py:510
  132.3 14.6 %collective-permute-start.20 = (bf16[256,512]{1,0:T(8,128)(2,1)S(1)}, bf16[256,512]{1,0:T(8,128)(2,1)S(1)}, u32[]{:S(2)}, u32[]{:S(2)}) collective-permute-start(bf16[256,512]{1,0:T(8,128)(2,1)S(1)} %shard_map.105.refs_4_.refs_0_), channel_id=1, source_target_pairs={{0,8},{4,12},{8,0},{12,4},{16,24},{20,28},{24,16},{28,20},{1,9},{5... | collective-permute-start | bytes 786440 | tf_op jit(solution)/shard_map/ppermute | solution.py:510
  137.3 12.5 %collective-permute-start.19 = (bf16[128,512]{1,0:T(8,128)(2,1)S(1)}, bf16[128,512]{1,0:T(8,128)(2,1)S(1)}, u32[]{:S(2)}, u32[]{:S(2)}) collective-permute-start(bf16[128,512]{1,0:T(8,128)(2,1)S(1)} %get-tuple-element.71.refs_2_.refs_0_), channel_id=1, source_target_pairs={{0,16},{4,20},{8,24},{12,28},{16,0},{20,4},{24,8},{28,12},{1,17},{... | collective-permute-start | bytes 393224 | tf_op jit(solution)/shard_map/ppermute | solution.py:510
  140.2 11.3 %collective-permute-start.18 = (bf16[128,512]{1,0:T(8,128)(2,1)S(1)}, bf16[128,512]{1,0:T(8,128)(2,1)S(1)}, u32[]{:S(2)}, u32[]{:S(2)}) collective-permute-start(bf16[128,512]{1,0:T(8,128)(2,1)S(1)} %get-tuple-element.73.refs_2_), channel_id=1, source_target_pairs={{0,16},{4,20},{8,24},{12,28},{16,0},{20,4},{24,8},{28,12},{1,17},{... | collective-permute-start | bytes 393224 | tf_op jit(solution)/shard_map/ppermute | solution.py:510
  146.9 19.3 %collective-permute-start.25 = (bf16[512,512]{1,0:T(8,128)(2,1)S(1)}, bf16[512,512]{1,0:T(8,128)(2,1)S(1)}, u32[]{:S(2)}, u32[]{:S(2)}) collective-permute-start(bf16[512,512]{1,0:T(8,128)(2,1)S(1)} %shard_map.108.refs_2_.refs_0_), channel_id=1, source_target_pairs={{0,4},{4,0},{8,12},{12,8},{16,20},{20,16},{24,28},{28,24},{1,5},{5... | collective-permute-start | bytes 1572872 | tf_op jit(solution)/shard_map/ppermute | solution.py:510
  149.8 14.1 %collective-permute-start.22 = (bf16[256,512]{1,0:T(8,128)(2,1)S(1)}, bf16[256,512]{1,0:T(8,128)(2,1)S(1)}, u32[]{:S(2)}, u32[]{:S(2)}) collective-permute-start(bf16[256,512]{1,0:T(8,128)(2,1)S(1)} %shard_map.109.refs_4_.refs_0_), channel_id=1, source_target_pairs={{0,8},{4,12},{8,0},{12,4},{16,24},{20,28},{24,16},{28,20},{1,9},{5... | collective-permute-start | bytes 786440 | tf_op jit(solution)/shard_map/ppermute | solution.py:510
  151.6 12.7 %collective-permute-start.21 = (bf16[128,512]{1,0:T(8,128)(2,1)S(1)}, bf16[128,512]{1,0:T(8,128)(2,1)S(1)}, u32[]{:S(2)}, u32[]{:S(2)}) collective-permute-start(bf16[128,512]{1,0:T(8,128)(2,1)S(1)} %get-tuple-element.75.refs_2_.refs_0_), channel_id=1, source_target_pairs={{0,16},{4,20},{8,24},{12,28},{16,0},{20,4},{24,8},{28,12},{1,17},{... | collective-permute-start | bytes 393224 | tf_op jit(solution)/shard_map/ppermute | solution.py:510
  164.0 15.1 %collective-permute-start.27 = (bf16[512,512]{1,0:T(8,128)(2,1)S(1)}, bf16[512,512]{1,0:T(8,128)(2,1)S(1)}, u32[]{:S(2)}, u32[]{:S(2)}) collective-permute-start(bf16[512,512]{1,0:T(8,128)(2,1)S(1)} %shard_map.112.refs_2_.refs_0_), channel_id=1, source_target_pairs={{0,4},{4,0},{8,12},{12,8},{16,20},{20,16},{24,28},{28,24},{1,5},{5... | collective-permute-start | bytes 1572872 | tf_op jit(solution)/shard_map/ppermute | solution.py:510
  164.4 13.2 %collective-permute-start.24 = (bf16[256,512]{1,0:T(8,128)(2,1)S(1)}, bf16[256,512]{1,0:T(8,128)(2,1)S(1)}, u32[]{:S(2)}, u32[]{:S(2)}) collective-permute-start(bf16[256,512]{1,0:T(8,128)(2,1)S(1)} %shard_map.113.refs_2_.refs_0_), channel_id=1, source_target_pairs={{0,8},{4,12},{8,0},{12,4},{16,24},{20,28},{24,16},{28,20},{1,9},{5... | collective-permute-start | bytes 786440 | tf_op jit(solution)/shard_map/ppermute | solution.py:510
  177.6 12.9 %collective-permute-start.26 = (bf16[512,512]{1,0:T(8,128)(2,1)S(1)}, bf16[512,512]{1,0:T(8,128)(2,1)S(1)}, u32[]{:S(2)}, u32[]{:S(2)}) collective-permute-start(bf16[512,512]{1,0:T(8,128)(2,1)S(1)} %shard_map.115.refs_2_.refs_0_), channel_id=1, source_target_pairs={{0,4},{4,0},{8,12},{12,8},{16,20},{20,16},{24,28},{28,24},{1,5},{5... | collective-permute-start | bytes 1572872 | tf_op jit(solution)/shard_map/ppermute | solution.py:510
  (2 other events, 3.9 us)
